TPU v7x, 256 devices: a whole 4x4x8 slice. The times are simulated.
256 devices in a mesh: grp: 2 (over z_lo), dp: 32 (over z_hi, y, core), sp: 4 (over x).
Axes of the slice: x: 4, y: 4, z: 8 (z_hi: 4, z_lo: 2; z = z_hi * 2 + z_lo), core: 2. Of those that a mesh axis runs over, the one named last changes fastest.
Arguments:
- phase_mask: float32 [1024, 1024], P(None, 'sp'), may hold values from -3 to 3
- height_offsets: int32 [4, 1024, 1024], P(None, None, 'sp'), may hold values from -4 to 4
- sample_ids: int32 [32], P('dp'), may hold values from 0 to 3
- wavelength_ids: int32 [32], P('dp'), may hold values from 0 to 30
- scene: float32 [32, 1024, 1024], P('dp', 'sp'), may hold values from -6 to 6
- w_first: float32 [32, 9], replicated, may hold values from -2 to 2
- b_first: float32 [32], replicated, may hold values from -3 to 3
- w_second: float32 [9, 32], replicated, may hold values from -0.375 to 0.375
Outputs:
- mask_grad: float32 [1024, 1024], P(None, 'sp')
- w_first_grad: float32 [32, 9], replicated
- b_first_grad: float32 [32], replicated
- w_second_grad: float32 [9, 32], replicated
- loss: float32 [], replicated
All inputs are finite; a program needn't handle non-finite values.
Results may differ from a plain program's by a relative error of at most 0.00018.
Values sent between devices are 32-bit elements; how exact they have to be, the bound alone decides.
No kernel may reach another device: no remote copies, remote signals or barrier semaphores. Data moves between devices by JAX's collectives and lax.ppermute only.
A program may use at most 128 MiB of HBM per device.

v0:
```python
import functools
import itertools

import jax
import jax.numpy as jnp
import ml_dtypes
import numpy as np
from jax import lax
from jax.experimental import pallas as pl
from jax.experimental.pallas import tpu as pltpu
from jax.sharding import PartitionSpec as P

N = 1024
F32 = jnp.float32
BF16 = jnp.bfloat16
AXES = ("grp", "zh", "y", "core", "sp")
taps = ((-1, -1), (-1, 0), (-1, 1), (0, -1), (0, 0), (0, 1), (1, -1), (1, 0), (1, 1))


def halves(matrix):
    high = matrix.astype(ml_dtypes.bfloat16)
    low = (matrix - high.astype(np.float64)).astype(ml_dtypes.bfloat16)
    return high, low


def trig(rows, cols, length):
    angle = 2.0 * np.pi * (np.outer(rows, cols) % length) / length
    return np.cos(angle), np.sin(angle)


@functools.lru_cache(None)
def constants():
    half = np.arange(512)
    quarter = np.arange(256)
    fours = np.arange(4)
    cos_m, sin_m = trig(half, half, N)
    cos_f, sin_f = trig(quarter, quarter, 256)
    cos_w, sin_w = trig(half, np.arange(N), N)
    sin_w = -sin_w
    sin_w[0] = (-1.0) ** np.arange(N)
    packed = np.concatenate([cos_w, sin_w])
    weight = np.full((N,), 2.0)
    weight[0] = 1.0
    weight[512] = 1.0
    unpack = (packed * weight[:, None]).T / (N * N)
    rows_ext = (np.arange(N + 16) - 8) % N
    cos_t, sin_t = trig(quarter, fours, N)
    cos_c, sin_c = trig(256 + np.arange(128), fours, N)
    return {
        "m": np.stack(halves(cos_m) + halves(sin_m)),
        "f": np.stack(halves(cos_f) + halves(sin_f)),
        "pack": np.stack(halves(packed)),
        "unpack": np.stack(halves(unpack[rows_ext])),
        "tw_col": np.concatenate([cos_t, sin_t], 1).astype(np.float32),
        "tw_row": np.concatenate(
            [
                np.concatenate([cos_t, sin_t], 1).T,
                np.pad(np.concatenate([cos_c, sin_c], 1).T, ((0, 0), (0, 128))),
            ]
        ).astype(np.float32),
    }


def pupil_count(size_grid):
    coords = np.arange(size_grid) * 2 - size_grid + 1
    inside = (coords[:, None] ** 2 + coords[None, :] ** 2) * 4 <= size_grid * size_grid
    return float(np.sum(inside))


class Layout:
    def __init__(self, mesh):
        self.dp = mesh.shape["dp"]
        self.y = min(4, self.dp // 2)
        self.zh = self.dp // (2 * self.y)
        self.sp = mesh.shape["sp"]
        self.sizes = (2, self.zh, self.y, 2, self.sp)
        self.mesh = jax.sharding.Mesh(mesh.devices.reshape(self.sizes), AXES)

    def move(self, x, where):
        pairs = []
        for spot in itertools.product(*[range(n) for n in self.sizes]):
            goal = where(*spot)
            if goal is not None:
                pairs.append((self.flat(spot), self.flat(goal)))
        return lax.ppermute(x, AXES, pairs)

    def flat(self, spot):
        at = 0
        for place, size in zip(spot, self.sizes):
            at = at * size + place % size
        return at


def split(x):
    high = x.astype(BF16)
    return high, (x - high.astype(F32)).astype(BF16)


def dot(a, b):
    return lax.dot_general(a, b, (((1,), (0,)), ((), ())), preferred_element_type=F32)


def by_right(x, w_high, w_low):
    high, low = split(x)
    return dot(high, w_high) + (dot(high, w_low) + dot(low, w_high))


def by_left(w_high, w_low, x):
    high, low = split(x)
    return dot(w_high, high) + (dot(w_low, high) + dot(w_high, low))


def dft_right(re, im, mats, sign):
    rows = re.shape[0]
    both = jnp.concatenate([re, im], 0)
    by_cos = by_right(both, mats[0], mats[1])
    by_sin = by_right(both, mats[2], mats[3]) * sign
    return by_cos[:rows] - by_sin[rows:], by_cos[rows:] + by_sin[:rows]


def dft_left(re, im, mats, sign):
    cols = re.shape[1]
    both = jnp.concatenate([re, im], 1)
    by_cos = by_left(mats[0], mats[1], both)
    by_sin = by_left(mats[2], mats[3], both) * sign
    return by_cos[:, :cols] - by_sin[:, cols:], by_cos[:, cols:] + by_sin[:, :cols]


def turned(re, im, quarter_turns):
    quarter_turns %= 4
    if quarter_turns == 0:
        return re, im
    if quarter_turns == 1:
        return -im, re
    if quarter_turns == 2:
        return -re, -im
    return im, -re


def times(re, im, cos, sin):
    return re * cos - im * sin, re * sin + im * cos


def cos_sin(x):
    n = jnp.floor(x * (2.0 / np.pi) + 0.5)
    r = x - n * 1.5707963109016418
    r = r - n * 1.5893254712295857e-8
    q = n.astype(jnp.int32) & 3
    z = r * r
    sn = r + r * z * (-1.6666654611e-1 + z * (8.3321608736e-3 + z * -1.9515295891e-4))
    cs = 1.0 - 0.5 * z + z * z * (
        4.166664568298827e-2 + z * (-1.388731625493765e-3 + z * 2.443315711809948e-5)
    )
    odd = (q & 1) == 1
    c0 = jnp.where(odd, sn, cs)
    s0 = jnp.where(odd, cs, sn)
    cos = jnp.where((q == 1) | (q == 2), -c0, c0)
    sin = jnp.where(q >= 2, -s0, s0)
    return cos, sin


def spot_of(idx, d, e=0):
    return lax.rem(idx[0] + d, 4), lax.rem(idx[1] + e, 2)


def from_of(idx, d, e=0):
    return lax.rem(idx[0] + 4 - d, 4), lax.rem(idx[1] + 2 - e, 2)


def aligned(x, by):
    return pl.multiple_of(x * by, by)


def call(kernel, operands, in_smem, outs, scratch=(), spaces=None):
    specs = []
    for at in range(len(operands)):
        space = pltpu.SMEM if at in in_smem else pltpu.VMEM
        if spaces and at in spaces:
            space = spaces[at]
        specs.append(pl.BlockSpec(memory_space=space))
    return pl.pallas_call(
        kernel,
        out_shape=[jax.ShapeDtypeStruct(shape, F32) for shape in outs],
        in_specs=specs,
        out_specs=[pl.BlockSpec(memory_space=pltpu.VMEM) for _ in outs],
        scratch_shapes=list(scratch),
        compiler_params=pltpu.CompilerParams(vmem_limit_bytes=48 * 1024 * 1024),
    )(*operands)


relations = [(d, e) for e in range(2) for d in range(4)]


def mats_of(ref):
    return ref[0], ref[1], ref[2], ref[3]


def phase_kernel(idx, ratio, mask, offsets, own, one, two, three, grabbed, phases, sem):
    copy = pltpu.make_async_copy(offsets.at[idx[2], pl.ds(256, 512), :], grabbed, sem)
    copy.start()
    copy.wait()
    phases[...] = ratio[0] * (mask[pl.ds(256, 512), :] + 0.1 * grabbed[...].astype(F32))
    s = idx[0]
    left = s == 1
    own[...] = phases[pl.ds(aligned(s, 128), 128), :]
    one[...] = phases[pl.ds(aligned(jnp.where(left, 0, 3), 128), 128), :]
    two[...] = phases[pl.ds(aligned(3 - s, 128), 128), :]
    three[...] = phases[pl.ds(aligned(jnp.where(left, 3, 0), 128), 128), :]


def scene_kernel(idx, scene, other, o0, o1, o2, o3, strip, edge):
    owner = idx[3] == 1
    c = idx[1]
    for d, out in enumerate((o0, o1, o2, o3)):
        s = spot_of(idx, d)[0]
        out[...] = jnp.where(
            owner,
            scene[0, :, pl.ds(aligned(4 * c + s, 128), 128)],
            other[:, pl.ds(aligned(s, 128), 128)],
        )
    strip[...] = jnp.where(owner, scene[0, :, 256:384], other[:, 512:640])
    edge[...] = jnp.where(c == 0, strip[248:256, :], strip[0:8, :])


def pupil_kernel(idx, a0, a1, a2, a3, m, o0, o1, o2, o3, pupil, grid):
    s = idx[0]
    c = idx[1]
    a0, a1, a2, a3 = a0[...], a1[...], a2[...], a3[...]
    left = jnp.where(s == 0, a1, jnp.where(s == 1, a0, jnp.where(s == 2, a2, a3)))
    right = jnp.where(s == 0, a3, jnp.where(s == 1, a2, jnp.where(s == 2, a0, a1)))
    phase = jnp.concatenate([left, right], 1)
    rows = lax.broadcasted_iota(jnp.int32, (128, 512), 0) + s * 128
    cols = lax.broadcasted_iota(jnp.int32, (128, 512), 1)
    up = (rows + 256) * 2 - N + 1
    across = (cols + 256) * 2 - N + 1
    inside = (up * up + across * across) * 4 <= N * N
    cos, sin = cos_sin(phase)
    re = jnp.where(inside, cos, 0.0)
    im = jnp.where(inside, sin, 0.0)
    pupil[0] = re
    pupil[1] = im
    flip = jnp.where((cols & c) == 1, -1.0, 1.0)
    out_re, out_im = dft_right(re * flip, im * flip, mats_of(m), -1.0)
    grid[0] = out_re
    grid[1] = out_im
    for d, out in enumerate((o0, o1, o2, o3)):
        to = spot_of(idx, d)[0]
        out[...] = grid[:, :, pl.ds(aligned(to, 128), 128)]


def eight_rows(out, grid):
    for c in range(2):
        for s in range(4):
            out[4 * c + s] = grid[:, 128 * s + 64 * c : 128 * s + 64 * c + 64, :]


def eight_columns(out, grid):
    for at in range(8):
        out[at] = grid[:, :, 128 * at : 128 * at + 128]


def optics_kernel(scale, idx, b0, b1, b2, b3, f, tw, far, out, grid):
    mats = mats_of(f)
    for d, block in enumerate((b0, b1, b2, b3)):
        grid[:, pl.ds(aligned(from_of(idx, d)[0], 128), 128), :] = block[...]
    low = (grid[0, :256, :], grid[1, :256, :])
    high = (grid[0, 256:, :], grid[1, 256:, :])
    twists = [(tw[:, r : r + 1], tw[:, 4 + r : 5 + r]) for r in range(4)]
    res, ims = [], []
    for r in range(4):
        add = turned(high[0], high[1], -r)
        re, im = low[0] + add[0], low[1] + add[1]
        if r:
            re, im = times(re, im, twists[r][0], -twists[r][1])
        res.append(re)
        ims.append(im)
    far_re, far_im = dft_left(
        jnp.concatenate(res, 1), jnp.concatenate(ims, 1), mats, -1.0
    )
    far[0] = far_re
    far[1] = far_im
    psf = scale * (far_re * far_re + far_im * far_im)
    psf_high, psf_low = split(psf)
    z_re = dot(mats[0], psf_high) + (dot(mats[1], psf_high) + dot(mats[0], psf_low))
    z_im = -(dot(mats[2], psf_high) + (dot(mats[3], psf_high) + dot(mats[2], psf_low)))
    first = [None, None]
    second = [None, None]
    nyquist = None
    for r in range(4):
        re = z_re[:, r * 128 : r * 128 + 128]
        im = z_im[:, r * 128 : r * 128 + 128]
        top = re[0:1, :]
        nyquist = top if r == 0 else (nyquist + top if r % 2 == 0 else nyquist - top)
        if r:
            re, im = times(re, im, twists[r][0], -twists[r][1])
        more = turned(re, im, -r)
        first = [re, im] if r == 0 else [first[0] + re, first[1] + im]
        second = list(more) if r == 0 else [second[0] + more[0], second[1] + more[1]]
    row = lax.broadcasted_iota(jnp.int32, (256, 128), 0)
    grid[0, :256, :] = first[0]
    grid[1, :256, :] = jnp.where(row == 0, nyquist, first[1])
    grid[0, 256:, :] = second[0]
    grid[1, 256:, :] = second[1]
    eight_rows(out, grid)


def scene_columns_kernel(idx, b0, b1, b2, b3, w, out, image, grid):
    for d, block in enumerate((b0, b1, b2, b3)):
        image[pl.ds(aligned(from_of(idx, d)[0], 256), 256), :] = block[...]
    spectrum = by_left(w[0], w[1], image[...])
    grid[0] = spectrum[:512]
    grid[1] = spectrum[512:]
    eight_rows(out, grid)


def unpack_rows(idx, re, im, tail):
    rows = lax.broadcasted_iota(jnp.int32, re.shape, 0)
    first = (idx[0] + idx[1]) == 0
    nyquist = jnp.where(first, im[0:1, :], 0.0)
    tail_rows = lax.broadcasted_iota(jnp.int32, (tail, re.shape[1]), 0)
    extra = jnp.where(tail_rows == 0, nyquist, 0.0)
    im = jnp.where((rows == 0) & first, 0.0, im)
    return jnp.concatenate([re, extra], 0), jnp.concatenate([im, jnp.zeros_like(extra)], 0)


def repack_rows(idx, re, im):
    first = (idx[0] + idx[1]) == 0
    rows = lax.broadcasted_iota(jnp.int32, (64, re.shape[1]), 0)
    return re[:64], jnp.where((rows == 0) & first, re[64:65, :], im[:64])


def row_transform(idx, blocks, mats, tw, grid):
    for at in range(8):
        grid[:, :, 128 * at : 128 * at + 128] = blocks[at]
    re, im = unpack_rows(idx, grid[0], grid[1], 8)
    quarters = [(re[:, q * 256 : q * 256 + 256], im[:, q * 256 : q * 256 + 256]) for q in range(4)]
    sum02 = [quarters[0][p] + quarters[2][p] for p in range(2)]
    dif02 = [quarters[0][p] - quarters[2][p] for p in range(2)]
    sum13 = [quarters[1][p] + quarters[3][p] for p in range(2)]
    dif13 = [quarters[1][p] - quarters[3][p] for p in range(2)]
    step = turned(dif13[0], dif13[1], -1)
    parts = [
        (sum02[0] + sum13[0], sum02[1] + sum13[1]),
        (dif02[0] + step[0], dif02[1] + step[1]),
        (sum02[0] - sum13[0], sum02[1] - sum13[1]),
        (dif02[0] - step[0], dif02[1] - step[1]),
    ]
    for r in range(1, 4):
        parts[r] = times(parts[r][0], parts[r][1], tw[r : r + 1, :], -tw[4 + r : 5 + r, :])
    return dft_right(
        jnp.concatenate([p[0] for p in parts], 0),
        jnp.concatenate([p[1] for p in parts], 0),
        mats,
        -1.0,
    )


def scene_rows_kernel(idx, blocks, f, tw, out, grid):
    re, im = row_transform(idx, blocks, mats_of(f), tw, grid)
    out[0] = re
    out[1] = im


def blur_kernel(idx, blocks, f, tw, spectrum, out, grid):
    mats = mats_of(f)
    re, im = row_transform(idx, blocks, mats, tw, grid)
    re, im = times(re, im, spectrum[0], spectrum[1])
    mats = tuple(m[:, :128] for m in mats)
    re, im = dft_right(re, im, mats, 1.0)
    sum_re, sum_im = re[:72], im[:72]
    for r in range(1, 4):
        add = times(
            re[r * 72 : r * 72 + 72],
            im[r * 72 : r * 72 + 72],
            tw[8 + r : 9 + r, :128],
            tw[12 + r : 13 + r, :128],
        )
        sum_re = sum_re + add[0]
        sum_im = sum_im + add[1]
    re, im = repack_rows(idx, sum_re, sum_im)
    out[0] = re
    out[1] = im


def moved_lanes(x, e, lanes):
    if e == 0:
        return x
    rolled = pltpu.roll(x, (-e) % 128, 1)
    return jnp.where(lanes == (127 if e > 0 else 0), 0.0, rolled)


def moved_rows(x, a):
    if a == 0:
        return x
    return pltpu.roll(x, (-a) % x.shape[0], 0)


ROWS = 144


def net_kernel(pixel_count, idx, w1, b1, w2, *refs):
    blocks = refs[:2]
    v, strip, edge, g_out, acc, loss_out = refs[2:8]
    grid, win_taps, g_taps, hidden, sums = refs[8:]
    for d, e in relations:
        s, c = from_of(idx, d, e)
        at = 2 * s + c
        grid[pl.ds(aligned(at, 64), 64), :] = blocks[e][d, 0]
        grid[pl.ds(aligned(at + 8, 64), 64), :] = blocks[e][d, 1]
    target = jnp.where(
        idx[1] == 0,
        jnp.concatenate([edge[...], strip[0:136, :]], 0),
        jnp.concatenate([strip[120:256, :], edge[...]], 0),
    )
    rows = lax.broadcasted_iota(jnp.int32, (ROWS, 128), 0)
    lanes = lax.broadcasted_iota(jnp.int32, (ROWS, 128), 1)
    row_global = rows + (2 * idx[0] + idx[1]) * 128 - 8
    inside = (row_global >= 0) & (row_global < N)
    window = jnp.where(inside, by_left(v[0], v[1], grid[...]), 0.0)
    for e in (-1, 0, 1):
        side = moved_lanes(window, e, lanes)
        for a in (-1, 0, 1):
            win_taps[3 * (a + 1) + e + 1] = moved_rows(side, a)
    step = 16
    for k in range(ROWS // step):
        part = pl.ds(k * step, step)

        def forward(c, total, part=part):
            pre = jnp.full((step, 128), b1[c], F32)
            for t in range(9):
                pre = pre + w1[c, t] * win_taps[t, part, :]
            hid = jnp.maximum(pre, 0.0)
            hidden[c, part, :] = hid
            return tuple(total[t] + w2[t, c] * hid for t in range(9))

        total = lax.fori_loop(
            0, 32, forward, tuple(jnp.zeros((step, 128), F32) for _ in range(9))
        )
        for t in range(9):
            sums[t, part, :] = total[t]
    restored = window
    for e in (-1, 0, 1):
        side = None
        for a in (-1, 0, 1):
            part = moved_rows(jnp.where(inside, sums[3 * (a + 1) + e + 1], 0.0), a)
            side = part if side is None else side + part
        restored = restored + moved_lanes(side, e, lanes)
    residual = jnp.where(inside, restored - target, 0.0)
    own = (rows >= 8) & (rows < 136)
    own_residual = jnp.where(own, residual, 0.0)
    loss_out[...] = jnp.sum((own_residual * own_residual).reshape(ROWS // 8, 8, 128), 0)
    g_restored = (2.0 / pixel_count) * residual
    for e in (-1, 0, 1):
        side = moved_lanes(g_restored, -e, lanes)
        for a in (-1, 0, 1):
            g_taps[3 * (a + 1) + e + 1] = jnp.where(inside, moved_rows(side, -a), 0.0)
    acc[...] = jnp.zeros_like(acc)

    def folded(x):
        return x if x.shape[0] == 8 else x[:8] + x[8:]

    for start, step, mine in [(0, 8, False)] + [(8 + 16 * k, 16, True) for k in range(8)] + [
        (136, 8, False)
    ]:
        part = pl.ds(start, step)

        def backward(c, total, part=part, step=step, mine=mine):
            hid = hidden[c, part, :]
            gh = w2[0, c] * g_taps[0, part, :]
            for t in range(1, 9):
                gh = gh + w2[t, c] * g_taps[t, part, :]
            gp = jnp.where(hid > 0.0, gh, 0.0)
            if mine:
                for t in range(9):
                    acc[c, t] += folded(gp * win_taps[t, part, :])
                    acc[c, 9 + t] += folded(hid * g_taps[t, part, :])
                acc[c, 18] += folded(gp)
            return tuple(total[t] + w1[c, t] * gp for t in range(9))

        total = lax.fori_loop(
            0, 32, backward, tuple(jnp.zeros((step, 128), F32) for _ in range(9))
        )
        for t in range(9):
            sums[t, part, :] = total[t]
    g_window = g_restored
    for e in (-1, 0, 1):
        side = None
        for a in (-1, 0, 1):
            part = moved_rows(sums[3 * (a + 1) + e + 1], -a)
            side = part if side is None else side + part
        g_window = g_window + moved_lanes(side, -e, lanes)
    g_out[...] = g_window[8:136]


def otf_grad_kernel(idx, *refs):
    blocks = refs[:2]
    w, f, tw, spectrum, out, window, grid = refs[2:]
    for d, e in relations:
        s, c = from_of(idx, d, e)
        window[pl.ds(aligned(2 * s + c, 128), 128), :] = blocks[e][d]
    packed = by_left(w[0], w[1], window[...])
    re, im = unpack_rows(idx, packed[:64], packed[64:], 8)
    res, ims = [re], [im]
    for r in range(1, 4):
        a, b = times(re, im, tw[8 + r : 9 + r, :128], -tw[12 + r : 13 + r, :128])
        res.append(a)
        ims.append(b)
    mats = mats_of(f)
    top = tuple(m[:128, :] for m in mats)
    re, im = dft_right(jnp.concatenate(res, 0), jnp.concatenate(ims, 0), top, -1.0)
    re, im = times(re, im, spectrum[0], -spectrum[1])
    re, im = dft_right(re, im, mats, 1.0)
    parts = []
    for r in range(4):
        a, b = re[r * 72 : r * 72 + 72], im[r * 72 : r * 72 + 72]
        if r:
            a, b = times(a, b, tw[r : r + 1, :], tw[4 + r : 5 + r, :])
        parts.append((a, b))
    for q in range(4):
        a, b = parts[0]
        for r in range(1, 4):
            more = turned(parts[r][0], parts[r][1], q * r)
            a = a + more[0]
            b = b + more[1]
        a, b = repack_rows(idx, a, b)
        grid[0, :, q * 256 : q * 256 + 256] = a
        grid[1, :, q * 256 : q * 256 + 256] = b
    eight_columns(out, grid)


def psf_grad_kernel(idx, blocks, far, f, tw, small, o0, o1, o2, o3, grid):
    mats = mats_of(f)
    for c in range(2):
        for s in range(4):
            grid[:, 128 * s + 64 * c : 128 * s + 64 * c + 64, :] = blocks[4 * c + s]
    row = lax.broadcasted_iota(jnp.int32, (256, 128), 0)
    zero_row = row == 0
    low_re, low_im = grid[0, :256, :], grid[1, :256, :]
    nyquist = jnp.where(zero_row, 0.5 * low_im, 0.0)
    low_re = jnp.where(zero_row, 0.5 * low_re, low_re)
    low_im = jnp.where(zero_row, 0.0, low_im)
    high = (grid[0, 256:, :], grid[1, 256:, :])
    twists = [(tw[:, r : r + 1], tw[:, 4 + r : 5 + r]) for r in range(4)]
    res, ims = [], []
    for r in range(4):
        add = turned(high[0], high[1], r)
        re, im = low_re + add[0], low_im + add[1]
        if r:
            re, im = times(re, im, twists[r][0], twists[r][1])
        re = re + nyquist if r % 2 == 0 else re - nyquist
        res.append(re)
        ims.append(im)
    g_psf = 2.0 * (
        by_left(mats[0], mats[1], jnp.concatenate(res, 1))
        - by_left(mats[2], mats[3], jnp.concatenate(ims, 1))
    )
    re, im = dft_left(g_psf * far[0], g_psf * far[1], mats, 1.0)
    first, second = None, None
    for r in range(4):
        a, b = re[:, r * 128 : r * 128 + 128], im[:, r * 128 : r * 128 + 128]
        if r:
            a, b = times(a, b, twists[r][0], twists[r][1])
        more = turned(a, b, r)
        first = [a, b] if r == 0 else [first[0] + a, first[1] + b]
        second = list(more) if r == 0 else [second[0] + more[0], second[1] + more[1]]
    for p in range(2):
        grid[p, :256, :] = first[p]
        grid[p, 256:, :] = second[p]
    for d, out in enumerate((o0, o1, o2, o3)):
        out[:, 0:128, :] = grid[:, pl.ds(aligned(spot_of(idx, d)[0], 128), 128), :]
        out[0, 128:136, :] = small[...]
        out[1, 128:136, :] = jnp.zeros((8, 128), F32)


def mask_grad_kernel(scale, idx, ratio, b0, b1, b2, b3, m, pupil, keep, send, grid, whole):
    small = None
    for d, block in enumerate((b0, b1, b2, b3)):
        grid[:, :, pl.ds(aligned(from_of(idx, d)[0], 128), 128)] = block[:, 0:128, :]
        part = block[0, 128:136, :]
        small = part if small is None else small + part
    re, im = dft_right(grid[0], grid[1], mats_of(m), 1.0)
    cols = lax.broadcasted_iota(jnp.int32, (128, 512), 1)
    factor = ratio[0] * scale
    factor = jnp.where((cols & idx[1]) == 1, -factor, factor)
    whole[...] = factor * (im * pupil[0] - re * pupil[1])
    both = jnp.concatenate([small, small], 1)
    keep[0:128, :] = whole[:, pl.ds(aligned(idx[1], 256), 256)]
    send[0:128, :] = whole[:, pl.ds(aligned(1 - idx[1], 256), 256)]
    keep[128:136, :] = both
    send[128:136, :] = both


def cut_kernel(ways, idx, keep, other, *refs):
    outs = refs[:ways]
    whole = refs[ways]
    whole[...] = keep[...] + other[...]
    piece = 128 // ways
    for d, out in enumerate(outs):
        to = lax.rem(idx[4] + d, ways)
        out[0:piece, :] = whole[pl.ds(aligned(to, piece), piece), :]
        out[piece : piece + 8, :] = whole[128:136, :]


def home_kernel(ways, idx, *refs):
    near = refs[:ways]
    far = refs[ways : 2 * ways]
    out = refs[2 * ways]
    piece = 128 // ways
    at_home = idx[0] == 1 + idx[1]
    central = (idx[0] == 1) | (idx[0] == 2)
    out[0:256, :] = jnp.zeros((256, 256), F32)
    out[768:1024, :] = jnp.zeros((256, 256), F32)
    for back in range(ways):
        y = lax.rem(idx[4] + ways - back, ways)
        for d in range(4):
            s = from_of(idx, d)[0]
            row = 256 + 128 * s + piece * y
            block = jnp.where(at_home, near[back][d], far[back][d])
            out[pl.ds(aligned(8 + 4 * s + y, 32) if ways == 4 else row, piece), :] = jnp.where(
                central, block, 0.0
            )


def on_device(lay, phase_mask, height_offsets, sample_ids, wave_ids, scene, w1, b1, w2):
    con = constants()
    s = lax.axis_index("sp")
    c = lax.axis_index("core")
    y = lax.axis_index("y")
    owner = c == lax.axis_index("grp")
    pixel_count = float(lay.dp * N * 128)
    scale_psf = 1.0 / (N * N * pupil_count(N))

    def swap(g, zh, y, c, s):
        return (g, zh, y, 1 - c, s)

    def along_sp(blocks):
        return [blocks[0]] + [
            lay.move(blocks[d], lambda g, zh, y, c, s, d=d: (g, zh, y, c, s + d))
            for d in (1, 2, 3)
        ]

    def to_eight(blocks):
        return lax.all_to_all(blocks, ("core", "sp"), 0, 0, tiled=True)

    def gathered(block):
        near = jnp.stack(along_sp([block] * 4))
        return near, lay.move(near, swap)

    ids = jnp.concatenate([sample_ids, wave_ids])
    ids = jnp.where(owner, ids, lay.move(ids, swap))
    idx = jnp.stack([s, c, ids[0], owner.astype(jnp.int32), y]).astype(jnp.int32)
    ratio = (550.0 / (400.0 + 10.0 * ids[1].astype(F32))).reshape(1)
    other = lay.move(
        jnp.concatenate(
            [lax.dynamic_slice_in_dim(scene[0], 512 * (1 - c), 512, 1), scene[0, :, 256:384]], 1
        ),
        swap,
    )

    mine, *sent = call(
        phase_kernel,
        (idx, ratio, phase_mask, height_offsets),
        (0, 1),
        [(128, 256)] * 4,
        [pltpu.VMEM((512, 256), jnp.int32), pltpu.VMEM((512, 256), F32), pltpu.SemaphoreType.DMA],
        {3: pl.ANY},
    )
    tables = ({1: 0, 2: 3}, {1: 2, 2: 1}, {1: 3, 2: 0})
    pieces = [mine] + [
        lay.move(
            block,
            lambda g, zh, y, c, s, to=to: (g, zh, y, c, to[s]) if s in to else None,
        )
        for block, to in zip(sent, tables)
    ]

    *columns, strip, edge = call(
        scene_kernel,
        (idx, scene, other),
        (0,),
        [(256, 128)] * 4 + [(256, 128), (8, 128)],
    )
    columns = along_sp(columns)
    edge = lay.move(edge, lambda g, zh, y, c, s: (g, zh, y, c, s + 1 - 2 * c))

    slot = 2 * s + c
    unpack = lax.dynamic_slice_in_dim(jnp.asarray(con["unpack"]), 128 * slot, ROWS, 1)
    pack = jnp.asarray(con["pack"])
    pack_rows = jnp.concatenate(
        [
            lax.dynamic_slice_in_dim(pack, 64 * slot, 64, 1),
            lax.dynamic_slice_in_dim(pack, 512 + 64 * slot, 64, 1),
        ],
        1,
    )

    *field, pupil = call(
        pupil_kernel,
        (idx, *pieces, con["m"]),
        (0,),
        [(2, 128, 128)] * 4 + [(2, 128, 512)],
        [pltpu.VMEM((2, 128, 512), F32)],
    )
    field = along_sp(field)
    (scene_part,) = call(
        scene_columns_kernel,
        (idx, *columns, con["pack"]),
        (0,),
        [(8, 2, 64, 128)],
        [pltpu.VMEM((N, 128), F32), pltpu.VMEM((2, 512, 128), F32)],
    )
    scene_part = to_eight(scene_part)
    far, otf_part = call(
        functools.partial(optics_kernel, scale_psf),
        (idx, *field, con["f"], con["tw_col"]),
        (0,),
        [(2, 256, 512), (8, 2, 64, 128)],
        [pltpu.VMEM((2, 512, 128), F32)],
    )
    otf_part = to_eight(otf_part)
    row_scratch = [pltpu.VMEM((2, 64, N), F32)]
    (spectrum,) = call(
        scene_rows_kernel,
        (idx, scene_part, con["f"], con["tw_row"]),
        (0,),
        [(2, 288, 256)],
        row_scratch,
    )
    (half_window,) = call(
        blur_kernel,
        (idx, otf_part, con["f"], con["tw_row"], spectrum),
        (0,),
        [(2, 64, 128)],
        row_scratch,
    )
    window_parts = gathered(half_window)
    g_window, acc, loss_part = call(
        functools.partial(net_kernel, pixel_count),
        (idx, w1, b1, w2, *window_parts, unpack, strip, edge),
        (0, 1, 2, 3),
        [(128, 128), (32, 19, 8, 128), (8, 128)],
        [
            pltpu.VMEM((N, 128), F32),
            pltpu.VMEM((9, ROWS, 128), F32),
            pltpu.VMEM((9, ROWS, 128), F32),
            pltpu.VMEM((32, ROWS, 128), F32),
            pltpu.VMEM((9, ROWS, 128), F32),
        ],
    )
    small = jnp.concatenate(
        [jnp.sum(acc, (2, 3)).reshape(-1), jnp.sum(loss_part).reshape(1), jnp.zeros((415,), F32)]
    ).reshape(8, 128)
    g_parts = gathered(g_window)
    (otf_grad,) = call(
        otf_grad_kernel,
        (idx, *g_parts, pack_rows, con["f"], con["tw_row"], spectrum),
        (0,),
        [(8, 2, 64, 128)],
        [pltpu.VMEM((N, 128), F32), pltpu.VMEM((2, 64, N), F32)],
    )
    otf_grad = to_eight(otf_grad)
    field_grad = along_sp(
        call(
            psf_grad_kernel,
            (idx, otf_grad, far, con["f"], con["tw_col"], small),
            (0,),
            [(2, 136, 128)] * 4,
            [pltpu.VMEM((2, 512, 128), F32)],
        )
    )
    keep, send = call(
        functools.partial(mask_grad_kernel, 2.0 * scale_psf),
        (idx, ratio, *field_grad, con["m"], pupil),
        (0, 1),
        [(136, 256)] * 2,
        [pltpu.VMEM((2, 128, 512), F32), pltpu.VMEM((128, 512), F32)],
    )

    piece = 128 // lay.y
    blocks = call(
        functools.partial(cut_kernel, lay.y),
        (idx, keep, lay.move(send, swap)),
        (0,),
        [(piece + 8, 256)] * lay.y,
        [pltpu.VMEM((136, 256), F32)],
    )
    total = blocks[0]
    for d in range(1, lay.y):
        total = total + lay.move(
            blocks[d], lambda g, zh, y, c, s, d=d: (g, zh, y + d, c, s)
        )
    total = total + lay.move(total, lambda g, zh, y, c, s: (1 - g, zh, y, c, s))
    part = total
    for d in range(1, lay.zh):
        total = total + lay.move(part, lambda g, zh, y, c, s, d=d: (g, zh + d, y, c, s))
    small = total[piece:, :128].reshape(-1)
    total = total[:piece]
    home = jnp.stack(
        [total]
        + [
            lay.move(
                total,
                lambda g, zh, y, c, s, d=d: (
                    (g, zh, y, c, 1 + c) if (s + d - 1 - c) % 4 == 0 else None
                ),
            )
            for d in (1, 2, 3)
        ]
    )
    near = [home] + [
        lay.move(
            home,
            lambda g, zh, y, c, s, d=d: (g, zh, y + d, c, s) if s == 1 + c else None,
        )
        for d in range(1, lay.y)
    ]
    across = [
        lay.move(
            block, lambda g, zh, y, c, s: (g, zh, y, 1 - c, s) if s == 1 + c else None
        )
        for block in near
    ]
    (mask_grad,) = call(
        functools.partial(home_kernel, lay.y), (idx, *near, *across), (0,), [(N, 256)]
    )
    table = small[:608].reshape(32, 19)
    return (
        mask_grad,
        table[:, :9],
        table[:, 18],
        table[:, 9:18].T,
        small[608] / pixel_count,
    )


def solution(mesh):
    lay = Layout(mesh)
    images = ("zh", "y", "core")
    placed = (
        P(None, "sp"),
        P(None, None, "sp"),
        P(images),
        P(images),
        P(images, "sp", None),
        P(),
        P(),
        P(),
    )
    return jax.shard_map(
        functools.partial(on_device, lay),
        mesh=lay.mesh,
        in_specs=placed,
        out_specs=(P(None, "sp"), P(), P(), P(), P()),
        check_vma=False,
    )
```

profile of v0, /device:TPU:3, one launch (start us, length us, event | category | flops | bytes accessed | tf_op | source)
XLA Modules:
  0.0 218.7 jit_solution(11815387752682682922)
XLA Ops:
  11.9 2.5 %collective-permute-start.9 = (f32[256,128]{1,0:T(8,128)S(1)}, f32[256,128]{1,0:T(8,128)S(1)}, u32[]{:S(2)}, u32[]{:S(2)}) collective-permute-start(f32[256,128]{1,0:T(8,128)S(1)} %get-tuple-element.46), channel_id=1, source_target_pairs={{0,2},{1,3},{2,0},{3,1},{4,6},{5,7},{6,4},{7,5},{8,10},{9,11},{10,... | collective-permute-start | bytes 393224 | tf_op jit(solution)/shard_map/ppermute | solution.py:85
  20.6 3.2 %shard_map.177 = f32[8,2,64,128]{3,2,1,0:T(8,128)} custom-call(s32[5]{0:T(128)S(1)} %stack.68.idx, f32[256,128]{1,0:T(8,128)S(1)} %get-tuple-element.44.b0, f32[256,128]{1,0:T(8,128)S(1)} %collective-permute-done.8.b1, f32[256,128]{1,0:T(8,128)S(1)} %collective-permute-done.9.b2, f32[256,128]{1,0:T(8,128)S(1)} %collective-permute-done.10.b3, ...), custom_call_target="tpu_custom_call" | custom-call | tf_op jit(solution)/shard_map/pallas_call | solution.py:181
  23.8 7.6 %all-to-all-start.1 = ((f32[8,2,64,128]{3,2,1,0:T(8,128)}), f32[8,2,64,128]{3,2,1,0:T(8,128)S(1)}, u32[]{:S(2)}, u32[]{:S(2)}) async-start(f32[8,2,64,128]{3,2,1,0:T(8,128)} %shard_map.177), calls=%async_computation.1 | async-start | bytes 1048576 | tf_op jit(solution)/shard_map/all_to_all | solution.py:643
  38.4 3.9 %collective-permute-start.2 = (f32[128,256]{1,0:T(8,128)S(1)}, f32[128,256]{1,0:T(8,128)S(1)}, u32[]{:S(2)}, u32[]{:S(2)}) collective-permute-start(f32[128,256]{1,0:T(8,128)S(1)} %get-tuple-element.37), channel_id=1, source_target_pairs={{1,2},{2,1},{5,6},{6,5},{9,10},{10,9},{13,14},{14,13},{17,18},{18,... | collective-permute-start | bytes 393224 | tf_op jit(solution)/shard_map/ppermute | solution.py:85
  49.5 3.7 %collective-permute-start.5 = (f32[2,128,128]{2,1,0:T(8,128)S(1)}, f32[2,128,128]{2,1,0:T(8,128)S(1)}, u32[]{:S(2)}, u32[]{:S(2)}) collective-permute-start(f32[2,128,128]{2,1,0:T(8,128)S(1)} %get-tuple-element.41), channel_id=1, source_target_pairs={{0,2},{1,3},{2,0},{3,1},{4,6},{5,7},{6,4},{7,5},{8,10},{9,11},{10,... | collective-permute-start | bytes 393224 | tf_op jit(solution)/shard_map/ppermute | solution.py:85
  55.6 3.3 %collective-permute-done.6.b3 = f32[2,128,128]{2,1,0:T(8,128)S(1)} collective-permute-done((f32[2,128,128]{2,1,0:T(8,128)S(1)}, f32[2,128,128]{2,1,0:T(8,128)S(1)}, u32[]{:S(2)}, u32[]{:S(2)}) %collective-permute-start.6) | collective-permute-done | bytes 131104 | tf_op jit(solution)/shard_map/ppermute | solution.py:85
  58.9 2.6 %shard_map.175 = (f32[2,256,512]{2,1,0:T(8,128)S(1)}, f32[8,2,64,128]{3,2,1,0:T(8,128)S(1)}) custom-call(s32[5]{0:T(128)S(1)} %stack.68.idx, f32[2,128,128]{2,1,0:T(8,128)S(1)} %get-tuple-element.39.b0, f32[2,128,128]{2,1,0:T(8,128)S(1)} %collective-permute-done.4.b1, f32[2,128,128]{2,1,0:T(8,128)S(1)} %collective-permute-done.5.b2, ...), custom_call_target="tpu_custom_call" | custom-call | tf_op jit(solution)/shard_map/pallas_call | solution.py:181
  64.1 7.1 %all-to-all-start = ((f32[8,2,64,128]{3,2,1,0:T(8,128)}), f32[8,2,64,128]{3,2,1,0:T(8,128)}, u32[]{:S(2)}, u32[]{:S(2)}) async-start(f32[8,2,64,128]{3,2,1,0:T(8,128)} %copy-done.15), calls=%async_computation | async-start | bytes 1048576 | tf_op jit(solution)/shard_map/all_to_all | solution.py:643
  73.4 6.4 %all-to-all-done.blocks = f32[8,2,64,128]{3,2,1,0:T(8,128)} async-done(((f32[8,2,64,128]{3,2,1,0:T(8,128)}), f32[8,2,64,128]{3,2,1,0:T(8,128)}, u32[]{:S(2)}, u32[]{:S(2)}) %all-to-all-start) | async-done | bytes 524320 | tf_op jit(solution)/shard_map/all_to_all | solution.py:643
  79.9 3.1 %shard_map.179 = f32[2,64,128]{2,1,0:T(8,128)S(1)} custom-call(s32[5]{0:T(128)S(1)} %stack.68.idx, f32[8,2,64,128]{3,2,1,0:T(8,128)} %all-to-all-done.blocks, bf16[4,256,256]{2,1,0:T(8,128)(2,1)S(1)} %copy-done, f32[16,256]{1,0:T(8,128)S(1)} %copy-done.18, f32[2,288,256]{2,1,0:T(8,128)S(1)} %shard_map.178.spectrum.refs_5_), custom_call_target="tpu_custom_call" | custom-call | tf_op jit(solution)/shard_map/pallas_call | solution.py:181
  83.1 2.7 %collective-permute-start.12 = (f32[2,64,128]{2,1,0:T(8,128)S(1)}, f32[2,64,128]{2,1,0:T(8,128)S(1)}, u32[]{:S(2)}, u32[]{:S(2)}) collective-permute-start(f32[2,64,128]{2,1,0:T(8,128)S(1)} %shard_map.179), channel_id=1, source_target_pairs={{0,2},{1,3},{2,0},{3,1},{4,6},{5,7},{6,4},{7,5},{8,10},{9,11},{10,... | collective-permute-start | bytes 196616 | tf_op jit(solution)/shard_map/ppermute | solution.py:85
  96.0 17.9 %shard_map.180 = (f32[128,128]{1,0:T(8,128)S(1)}, f32[32,19,8,128]{3,2,1,0:T(8,128)S(1)}, f32[8,128]{1,0:T(8,128)S(1)}) custom-call(s32[5]{0:T(128)S(1)} %stack.68.idx, f32[32,9]{1,0:T(8,128)S(1)} %copy.23.w1, f32[32]{0:T(128)S(1)} %copy-done.22, f32[9,32]{1,0:T(8,128)S(1)} %copy-done.21, f32[4,2,64,128]{3,2,1,0:T(8,128)S(1)} %pad_maximum_fusion.2.refs_0_, ...), custom_call_target="tpu_custom_call" | custom-call | tf_op jit(solution)/shard_map/pallas_call | solution.py:181
  116.1 3.3 %collective-permute-start.17 = (f32[128,128]{1,0:T(8,128)S(1)}, f32[128,128]{1,0:T(8,128)S(1)}, u32[]{:S(2)}, u32[]{:S(2)}) collective-permute-start(f32[128,128]{1,0:T(8,128)S(1)} %get-tuple-element.50), channel_id=1, source_target_pairs={{0,2},{1,3},{2,0},{3,1},{4,6},{5,7},{6,4},{7,5},{8,10},{9,11},{10,... | collective-permute-start | bytes 196616 | tf_op jit(solution)/shard_map/ppermute | solution.py:85
  126.2 3.5 %shard_map.181 = f32[8,2,64,128]{3,2,1,0:T(8,128)S(1)} custom-call(s32[5]{0:T(128)S(1)} %stack.68.idx, f32[4,128,128]{2,1,0:T(8,128)S(1)} %pad_maximum_fusion.3.refs_0_, f32[4,128,128]{2,1,0:T(8,128)} %collective-permute-done.19.refs_1_, bf16[2,128,1024]{2,1,0:T(8,128)(2,1)S(1)} %pad_maximum_fusion.1.refs_2_, bf16[4,256,256]{2,1,0:T(8,128)(2,1)S(1)} %copy-done, ...), custom_call_target="tpu_custom_call" | custom-call | tf_op jit(solution)/shard_map/pallas_call | solution.py:181
  130.6 4.8 %all-to-all-start.2 = ((f32[8,2,64,128]{3,2,1,0:T(8,128)}), f32[8,2,64,128]{3,2,1,0:T(8,128)S(1)}, u32[]{:S(2)}, u32[]{:S(2)}) async-start(f32[8,2,64,128]{3,2,1,0:T(8,128)} %copy-done.9), calls=%async_computation.2 | async-start | bytes 1048576 | tf_op jit(solution)/shard_map/all_to_all | solution.py:643
  135.3 2.7 %reduce_sum.18 = f32[32,19]{1,0:T(8,128)S(1)} reduce(f32[32,19,8,128]{3,2,1,0:T(8,128)} %copy-done.5, f32[]{:T(128)} %constant.61.clone.1), dimensions={2,3}, to_apply=%region_0.1 | reduce | flops 621984 | bytes 2492804 | tf_op jit(solution)/shard_map/reduce_sum | solution.py:751
  139.5 4.4 %all-to-all-done.2.blocks = f32[8,2,64,128]{3,2,1,0:T(8,128)S(1)} async-done(((f32[8,2,64,128]{3,2,1,0:T(8,128)}), f32[8,2,64,128]{3,2,1,0:T(8,128)S(1)}, u32[]{:S(2)}, u32[]{:S(2)}) %all-to-all-start.2) | async-done | bytes 524320 | tf_op jit(solution)/shard_map/all_to_all | solution.py:643
  146.0 2.7 %shard_map.182 = (f32[2,136,128]{2,1,0:T(8,128)S(1)}, f32[2,136,128]{2,1,0:T(8,128)S(1)}, f32[2,136,128]{2,1,0:T(8,128)S(1)}, f32[2,136,128]{2,1,0:T(8,128)S(1)}) custom-call(s32[5]{0:T(128)S(1)} %stack.68.idx, f32[8,2,64,128]{3,2,1,0:T(8,128)S(1)} %all-to-all-done.2.blocks, f32[2,256,512]{2,1,0:T(8,128)S(1)} %copy-done.11, ...), custom_call_target="tpu_custom_call" | custom-call | tf_op jit(solution)/shard_map/pallas_call | solution.py:181
  148.8 2.7 %collective-permute-start.21 = (f32[2,136,128]{2,1,0:T(8,128)S(1)}, f32[2,136,128]{2,1,0:T(8,128)S(1)}, u32[]{:S(2)}, u32[]{:S(2)}) collective-permute-start(f32[2,136,128]{2,1,0:T(8,128)S(1)} %get-tuple-element.56), channel_id=1, source_target_pairs={{0,2},{1,3},{2,0},{3,1},{4,6},{5,7},{6,4},{7,5},{8,10},{9,11},{10,... | collective-permute-start | bytes 417800 | tf_op jit(solution)/shard_map/ppermute | solution.py:85
  155.3 3.6 %collective-permute-done.22.b3 = f32[2,136,128]{2,1,0:T(8,128)S(1)} collective-permute-done((f32[2,136,128]{2,1,0:T(8,128)S(1)}, f32[2,136,128]{2,1,0:T(8,128)S(1)}, u32[]{:S(2)}, u32[]{:S(2)}) %collective-permute-start.22) | collective-permute-done | bytes 139296 | tf_op jit(solution)/shard_map/ppermute | solution.py:85
  165.2 2.6 %collective-permute-start.25 = (f32[40,256]{1,0:T(8,128)S(1)}, f32[40,256]{1,0:T(8,128)S(1)}, u32[]{:S(2)}, u32[]{:S(2)}) collective-permute-start(f32[40,256]{1,0:T(8,128)S(1)} %get-tuple-element.63), channel_id=1, source_target_pairs={{0,16},{1,17},{2,18},{3,19},{4,20},{5,21},{6,22},{7,23},{8,24},{9,... | collective-permute-start | bytes 122888 | tf_op jit(solution)/shard_map/ppermute | solution.py:85
  174.1 3.0 %collective-permute-start.28 = (f32[40,256]{1,0:T(8,128)S(1)}, f32[40,256]{1,0:T(8,128)S(1)}, u32[]{:S(2)}, u32[]{:S(2)}) collective-permute-start(f32[40,256]{1,0:T(8,128)S(1)} %add.50), channel_id=1, source_target_pairs={{0,32},{1,33},{2,34},{3,35},{4,36},{5,37},{6,38},{7,39},{8,40},{9,... | collective-permute-start | bytes 122888 | tf_op jit(solution)/shard_map/ppermute | solution.py:85
  177.0 4.9 %collective-permute-start.29 = (f32[40,256]{1,0:T(8,128)S(1)}, f32[40,256]{1,0:T(8,128)S(1)}, u32[]{:S(2)}, u32[]{:S(2)}) collective-permute-start(f32[40,256]{1,0:T(8,128)S(1)} %add.50), channel_id=1, source_target_pairs={{0,64},{1,65},{2,66},{3,67},{4,68},{5,69},{6,70},{7,71},{8,72},{9,... | collective-permute-start | bytes 122888 | tf_op jit(solution)/shard_map/ppermute | solution.py:85
  200.1 11.2 %collective-permute-done.37.refs_4_ = f32[4,32,256]{2,1,0:T(8,128)S(1)} collective-permute-done((f32[4,32,256]{2,1,0:T(8,128)S(1)}, f32[4,32,256]{2,1,0:T(8,128)S(1)}, u32[]{:S(2)}, u32[]{:S(2)}) %collective-permute-start.37) | collective-permute-done | bytes 131104 | tf_op jit(solution)/shard_map/ppermute | solution.py:85
  (155 shorter events, 100.2 us)
Async XLA Ops:
  9.9 4.9 %collective-permute-start.10 = (f32[256,128]{1,0:T(8,128)S(1)}, f32[256,128]{1,0:T(8,128)S(1)}, u32[]{:S(2)}, u32[]{:S(2)}) collective-permute-start(f32[256,128]{1,0:T(8,128)S(1)} %get-tuple-element.47), channel_id=1, source_target_pairs={{0,3},{1,0},{2,1},{3,2},{4,7},{5,4},{6,5},{7,6},{8,11},{9,8},{10,9... | collective-permute-start | bytes 393224 | tf_op jit(solution)/shard_map/ppermute | solution.py:85
  11.9 6.6 %collective-permute-start.9 = (f32[256,128]{1,0:T(8,128)S(1)}, f32[256,128]{1,0:T(8,128)S(1)}, u32[]{:S(2)}, u32[]{:S(2)}) collective-permute-start(f32[256,128]{1,0:T(8,128)S(1)} %get-tuple-element.46), channel_id=1, source_target_pairs={{0,2},{1,3},{2,0},{3,1},{4,6},{5,7},{6,4},{7,5},{8,10},{9,11},{10,... | collective-permute-start | bytes 393224 | tf_op jit(solution)/shard_map/ppermute | solution.py:85
  23.8 39.4 %all-to-all-start.1 = ((f32[8,2,64,128]{3,2,1,0:T(8,128)}), f32[8,2,64,128]{3,2,1,0:T(8,128)S(1)}, u32[]{:S(2)}, u32[]{:S(2)}) async-start(f32[8,2,64,128]{3,2,1,0:T(8,128)} %shard_map.177), calls=%async_computation.1 | async-start | bytes 1048576 | tf_op jit(solution)/shard_map/all_to_all | solution.py:643
  36.3 7.2 %collective-permute-start.1 = (f32[128,256]{1,0:T(8,128)S(1)}, f32[128,256]{1,0:T(8,128)S(1)}, u32[]{:S(2)}, u32[]{:S(2)}) collective-permute-start(f32[128,256]{1,0:T(8,128)S(1)} %get-tuple-element.36), channel_id=1, source_target_pairs={{1,0},{2,3},{5,4},{6,7},{9,8},{10,11},{13,12},{14,15},{17,16},{18,... | collective-permute-start | bytes 393224 | tf_op jit(solution)/shard_map/ppermute | solution.py:85
  38.4 7.1 %collective-permute-start.2 = (f32[128,256]{1,0:T(8,128)S(1)}, f32[128,256]{1,0:T(8,128)S(1)}, u32[]{:S(2)}, u32[]{:S(2)}) collective-permute-start(f32[128,256]{1,0:T(8,128)S(1)} %get-tuple-element.37), channel_id=1, source_target_pairs={{1,2},{2,1},{5,6},{6,5},{9,10},{10,9},{13,14},{14,13},{17,18},{18,... | collective-permute-start | bytes 393224 | tf_op jit(solution)/shard_map/ppermute | solution.py:85
  48.6 5.8 %collective-permute-start.4 = (f32[2,128,128]{2,1,0:T(8,128)S(1)}, f32[2,128,128]{2,1,0:T(8,128)S(1)}, u32[]{:S(2)}, u32[]{:S(2)}) collective-permute-start(f32[2,128,128]{2,1,0:T(8,128)S(1)} %get-tuple-element.40), channel_id=1, source_target_pairs={{0,1},{1,2},{2,3},{3,0},{4,5},{5,6},{6,7},{7,4},{8,9},{9,10},{10,1... | collective-permute-start | bytes 393224 | tf_op jit(solution)/shard_map/ppermute | solution.py:85
  49.5 6.1 %collective-permute-start.5 = (f32[2,128,128]{2,1,0:T(8,128)S(1)}, f32[2,128,128]{2,1,0:T(8,128)S(1)}, u32[]{:S(2)}, u32[]{:S(2)}) collective-permute-start(f32[2,128,128]{2,1,0:T(8,128)S(1)} %get-tuple-element.41), channel_id=1, source_target_pairs={{0,2},{1,3},{2,0},{3,1},{4,6},{5,7},{6,4},{7,5},{8,10},{9,11},{10,... | collective-permute-start | bytes 393224 | tf_op jit(solution)/shard_map/ppermute | solution.py:85
  53.2 5.6 %collective-permute-start.6 = (f32[2,128,128]{2,1,0:T(8,128)S(1)}, f32[2,128,128]{2,1,0:T(8,128)S(1)}, u32[]{:S(2)}, u32[]{:S(2)}) collective-permute-start(f32[2,128,128]{2,1,0:T(8,128)S(1)} %get-tuple-element.42), channel_id=1, source_target_pairs={{0,3},{1,0},{2,1},{3,2},{4,7},{5,4},{6,5},{7,6},{8,11},{9,8},{10,9... | collective-permute-start | bytes 393224 | tf_op jit(solution)/shard_map/ppermute | solution.py:85
  64.1 15.8 %all-to-all-start = ((f32[8,2,64,128]{3,2,1,0:T(8,128)}), f32[8,2,64,128]{3,2,1,0:T(8,128)}, u32[]{:S(2)}, u32[]{:S(2)}) async-start(f32[8,2,64,128]{3,2,1,0:T(8,128)} %copy-done.15), calls=%async_computation | async-start | bytes 1048576 | tf_op jit(solution)/shard_map/all_to_all | solution.py:643
  83.1 4.7 %collective-permute-start.12 = (f32[2,64,128]{2,1,0:T(8,128)S(1)}, f32[2,64,128]{2,1,0:T(8,128)S(1)}, u32[]{:S(2)}, u32[]{:S(2)}) collective-permute-start(f32[2,64,128]{2,1,0:T(8,128)S(1)} %shard_map.179), channel_id=1, source_target_pairs={{0,2},{1,3},{2,0},{3,1},{4,6},{5,7},{6,4},{7,5},{8,10},{9,11},{10,... | collective-permute-start | bytes 196616 | tf_op jit(solution)/shard_map/ppermute | solution.py:85
  115.4 5.0 %collective-permute-start.16 = (f32[128,128]{1,0:T(8,128)S(1)}, f32[128,128]{1,0:T(8,128)S(1)}, u32[]{:S(2)}, u32[]{:S(2)}) collective-permute-start(f32[128,128]{1,0:T(8,128)S(1)} %get-tuple-element.50), channel_id=1, source_target_pairs={{0,1},{1,2},{2,3},{3,0},{4,5},{5,6},{6,7},{7,4},{8,9},{9,10},{10,1... | collective-permute-start | bytes 196616 | tf_op jit(solution)/shard_map/ppermute | solution.py:85
  116.1 5.0 %collective-permute-start.17 = (f32[128,128]{1,0:T(8,128)S(1)}, f32[128,128]{1,0:T(8,128)S(1)}, u32[]{:S(2)}, u32[]{:S(2)}) collective-permute-start(f32[128,128]{1,0:T(8,128)S(1)} %get-tuple-element.50), channel_id=1, source_target_pairs={{0,2},{1,3},{2,0},{3,1},{4,6},{5,7},{6,4},{7,5},{8,10},{9,11},{10,... | collective-permute-start | bytes 196616 | tf_op jit(solution)/shard_map/ppermute | solution.py:85
  130.6 13.3 %all-to-all-start.2 = ((f32[8,2,64,128]{3,2,1,0:T(8,128)}), f32[8,2,64,128]{3,2,1,0:T(8,128)S(1)}, u32[]{:S(2)}, u32[]{:S(2)}) async-start(f32[8,2,64,128]{3,2,1,0:T(8,128)} %copy-done.9), calls=%async_computation.2 | async-start | bytes 1048576 | tf_op jit(solution)/shard_map/all_to_all | solution.py:643
  148.7 5.1 %collective-permute-start.20 = (f32[2,136,128]{2,1,0:T(8,128)S(1)}, f32[2,136,128]{2,1,0:T(8,128)S(1)}, u32[]{:S(2)}, u32[]{:S(2)}) collective-permute-start(f32[2,136,128]{2,1,0:T(8,128)S(1)} %get-tuple-element.55), channel_id=1, source_target_pairs={{0,1},{1,2},{2,3},{3,0},{4,5},{5,6},{6,7},{7,4},{8,9},{9,10},{10,1... | collective-permute-start | bytes 417800 | tf_op jit(solution)/shard_map/ppermute | solution.py:85
  148.8 6.5 %collective-permute-start.21 = (f32[2,136,128]{2,1,0:T(8,128)S(1)}, f32[2,136,128]{2,1,0:T(8,128)S(1)}, u32[]{:S(2)}, u32[]{:S(2)}) collective-permute-start(f32[2,136,128]{2,1,0:T(8,128)S(1)} %get-tuple-element.56), channel_id=1, source_target_pairs={{0,2},{1,3},{2,0},{3,1},{4,6},{5,7},{6,4},{7,5},{8,10},{9,11},{10,... | collective-permute-start | bytes 417800 | tf_op jit(solution)/shard_map/ppermute | solution.py:85
  151.5 7.5 %collective-permute-start.22 = (f32[2,136,128]{2,1,0:T(8,128)S(1)}, f32[2,136,128]{2,1,0:T(8,128)S(1)}, u32[]{:S(2)}, u32[]{:S(2)}) collective-permute-start(f32[2,136,128]{2,1,0:T(8,128)S(1)} %get-tuple-element.57), channel_id=1, source_target_pairs={{0,3},{1,0},{2,1},{3,2},{4,7},{5,4},{6,5},{7,6},{8,11},{9,8},{10,9... | collective-permute-start | bytes 417800 | tf_op jit(solution)/shard_map/ppermute | solution.py:85
  163.8 5.1 %collective-permute-start.24 = (f32[40,256]{1,0:T(8,128)S(1)}, f32[40,256]{1,0:T(8,128)S(1)}, u32[]{:S(2)}, u32[]{:S(2)}) collective-permute-start(f32[40,256]{1,0:T(8,128)S(1)} %get-tuple-element.62), channel_id=1, source_target_pairs={{0,8},{1,9},{2,10},{3,11},{4,12},{5,13},{6,14},{7,15},{8,16},{9,17... | collective-permute-start | bytes 122888 | tf_op jit(solution)/shard_map/ppermute | solution.py:85
  174.1 10.3 %collective-permute-start.28 = (f32[40,256]{1,0:T(8,128)S(1)}, f32[40,256]{1,0:T(8,128)S(1)}, u32[]{:S(2)}, u32[]{:S(2)}) collective-permute-start(f32[40,256]{1,0:T(8,128)S(1)} %add.50), channel_id=1, source_target_pairs={{0,32},{1,33},{2,34},{3,35},{4,36},{5,37},{6,38},{7,39},{8,40},{9,... | collective-permute-start | bytes 122888 | tf_op jit(solution)/shard_map/ppermute | solution.py:85
  177.0 7.3 %collective-permute-start.29 = (f32[40,256]{1,0:T(8,128)S(1)}, f32[40,256]{1,0:T(8,128)S(1)}, u32[]{:S(2)}, u32[]{:S(2)}) collective-permute-start(f32[40,256]{1,0:T(8,128)S(1)} %add.50), channel_id=1, source_target_pairs={{0,64},{1,65},{2,66},{3,67},{4,68},{5,69},{6,70},{7,71},{8,72},{9,... | collective-permute-start | bytes 122888 | tf_op jit(solution)/shard_map/ppermute | solution.py:85
  190.7 4.7 %collective-permute-start.36 = (f32[4,32,256]{2,1,0:T(8,128)S(1)}, f32[4,32,256]{2,1,0:T(8,128)S(1)}, u32[]{:S(2)}, u32[]{:S(2)}) collective-permute-start(f32[4,32,256]{2,1,0:T(8,128)S(1)} %pad_maximum_fusion.4.refs_0_), channel_id=1, source_target_pairs={{1,25},{6,30},{9,1},{14,6},{17,9},{22,14},{25,17},{30,22},{33,57},... | collective-permute-start | bytes 393224 | tf_op jit(solution)/shard_map/ppermute | solution.py:85
  191.5 19.8 %collective-permute-start.37 = (f32[4,32,256]{2,1,0:T(8,128)S(1)}, f32[4,32,256]{2,1,0:T(8,128)S(1)}, u32[]{:S(2)}, u32[]{:S(2)}) collective-permute-start(f32[4,32,256]{2,1,0:T(8,128)S(1)} %pad_maximum_fusion.4.refs_0_), channel_id=1, source_target_pairs={{1,5},{6,2},{9,13},{14,10},{17,21},{22,18},{25,29},{30,26},{33,37}... | collective-permute-start | bytes 393224 | tf_op jit(solution)/shard_map/ppermute | solution.py:85
  192.8 19.8 %collective-permute-start.38 = (f32[4,32,256]{2,1,0:T(8,128)S(1)}, f32[4,32,256]{2,1,0:T(8,128)S(1)}, u32[]{:S(2)}, u32[]{:S(2)}) collective-permute-start(f32[4,32,256]{2,1,0:T(8,128)S(1)} %collective-permute-done.34.refs_1_), channel_id=1, source_target_pairs={{1,5},{6,2},{9,13},{14,10},{17,21},{22,18},{25,29},{30,26},{33,37}... | collective-permute-start | bytes 393224 | tf_op jit(solution)/shard_map/ppermute | solution.py:85
  194.1 19.8 %collective-permute-start.39 = (f32[4,32,256]{2,1,0:T(8,128)S(1)}, f32[4,32,256]{2,1,0:T(8,128)S(1)}, u32[]{:S(2)}, u32[]{:S(2)}) collective-permute-start(f32[4,32,256]{2,1,0:T(8,128)S(1)} %collective-permute-done.35.refs_2_), channel_id=1, source_target_pairs={{1,5},{6,2},{9,13},{14,10},{17,21},{22,18},{25,29},{30,26},{33,37}... | collective-permute-start | bytes 393224 | tf_op jit(solution)/shard_map/ppermute | solution.py:85
  195.4 20.6 %collective-permute-start.40 = (f32[4,32,256]{2,1,0:T(8,128)S(1)}, f32[4,32,256]{2,1,0:T(8,128)S(1)}, u32[]{:S(2)}, u32[]{:S(2)}) collective-permute-start(f32[4,32,256]{2,1,0:T(8,128)S(1)} %collective-permute-done.36.refs_3_), channel_id=1, source_target_pairs={{1,5},{6,2},{9,13},{14,10},{17,21},{22,18},{25,29},{30,26},{33,37}... | collective-permute-start | bytes 393224 | tf_op jit(solution)/shard_map/ppermute | solution.py:85
  (44 other events, 343.4 us)
where the time goes:
time: 222 us; the launch traced here: 219 us
  starting transfers between devices  81.5 us (37%)
  waiting for transfers between devices  57.9 us (26%)
  Pallas kernels  41.4 us (19%)
  local copies, waits for them, and re-layouts  28.6 us (13%)
  between operations  4.94 us (2%)
  other arithmetic  4.34 us (2%)
    ppermute x41, starting transfers between devices, move(): return lax.ppermute(x, AXES, pairs)  62 us
    ppermute x41, waiting for transfers between devices, move(): return lax.ppermute(x, AXES, pairs)  47.1 us
    pallas_call x13, Pallas kernels, call(): pl.pallas_call(kernel, out_shape=[jax.ShapeDtypeStruct(shape, F32) for sh...  41.4 us
    unnamed x51, local copies, waits for them, and re-layouts  20.7 us
    all_to_all x3, starting transfers between devices, to_eight(): return lax.all_to_all(blocks, ('core', 'sp'), 0, 0, tiled=True)  19.4 us
    all_to_all x3, waiting for transfers between devices, to_eight(): return lax.all_to_all(blocks, ('core', 'sp'), 0, 0, tiled=True)  10.9 us
  transfers between devices with their start and end apart: 44, of which 28 were waited for; matrix products, arithmetic and copies ran while one was open for 5% of the time, Pallas kernels for 3%

commit v1 on v0

--- a/solution.py
+++ b/solution.py
@@ -171,35 +171,64 @@
     return pl.multiple_of(x * by, by)
 
 
-def call(kernel, operands, in_smem, outs, scratch=(), spaces=None):
+def call(kernel, operands, in_smem, outs, scratch=(), apart=()):
     specs = []
     for at in range(len(operands)):
         space = pltpu.SMEM if at in in_smem else pltpu.VMEM
-        if spaces and at in spaces:
-            space = spaces[at]
-        specs.append(pl.BlockSpec(memory_space=space))
+        specs.append(pl.BlockSpec(memory_space=pl.ANY if at in apart else space))
     return pl.pallas_call(
         kernel,
         out_shape=[jax.ShapeDtypeStruct(shape, F32) for shape in outs],
         in_specs=specs,
         out_specs=[pl.BlockSpec(memory_space=pltpu.VMEM) for _ in outs],
         scratch_shapes=list(scratch),
-        compiler_params=pltpu.CompilerParams(vmem_limit_bytes=48 * 1024 * 1024),
+        compiler_params=pltpu.CompilerParams(vmem_limit_bytes=60 * 1024 * 1024),
     )(*operands)
 
 
 relations = [(d, e) for e in range(2) for d in range(4)]
+
+
+class Fetch:
+    def __init__(self, sems, *pairs):
+        self.copies = [
+            pltpu.make_async_copy(src, dst, sems.at[at]) for at, (src, dst) in enumerate(pairs)
+        ]
+        for copy in self.copies:
+            copy.start()
+
+    def wait(self, at):
+        self.copies[at].wait()
+
+
+def bf16_buffer(*shape):
+    return pltpu.VMEM(shape, BF16)
+
+
+def fetch_sems(count):
+    return pltpu.SemaphoreType.DMA((count,))
+
+
+def ratio_of(wave):
+    return 550.0 / (400.0 + 10.0 * jnp.full((8, 128), wave, jnp.int32).astype(F32))
 
 
 def mats_of(ref):
     return ref[0], ref[1], ref[2], ref[3]
 
 
-def phase_kernel(idx, ratio, mask, offsets, own, one, two, three, grabbed, phases, sem):
-    copy = pltpu.make_async_copy(offsets.at[idx[2], pl.ds(256, 512), :], grabbed, sem)
-    copy.start()
-    copy.wait()
-    phases[...] = ratio[0] * (mask[pl.ds(256, 512), :] + 0.1 * grabbed[...].astype(F32))
+def phase_kernel(idx, ids, got, mask, offsets, own, one, two, three, slab, grabbed, phases, sems):
+    owner = idx[2] == 1
+    sample = jnp.where(owner, ids[0], got[0])
+    fetch = Fetch(
+        sems,
+        (offsets.at[sample, pl.ds(256, 512), :], grabbed),
+        (mask.at[pl.ds(256, 512), :], slab),
+    )
+    ratio = ratio_of(jnp.where(owner, ids[1], got[1]))[0:1, 0:1]
+    fetch.wait(0)
+    fetch.wait(1)
+    phases[...] = ratio * (slab[...] + 0.1 * grabbed[...].astype(F32))
     s = idx[0]
     left = s == 1
     own[...] = phases[pl.ds(aligned(s, 128), 128), :]
@@ -209,7 +238,7 @@
 
 
 def scene_kernel(idx, scene, other, o0, o1, o2, o3, strip, edge):
-    owner = idx[3] == 1
+    owner = idx[2] == 1
     c = idx[1]
     for d, out in enumerate((o0, o1, o2, o3)):
         s = spot_of(idx, d)[0]
@@ -222,7 +251,8 @@
     edge[...] = jnp.where(c == 0, strip[248:256, :], strip[0:8, :])
 
 
-def pupil_kernel(idx, a0, a1, a2, a3, m, o0, o1, o2, o3, pupil, grid):
+def pupil_kernel(idx, a0, a1, a2, a3, m_far, o0, o1, o2, o3, pupil, grid, m, sems):
+    fetch = Fetch(sems, (m_far, m))
     s = idx[0]
     c = idx[1]
     a0, a1, a2, a3 = a0[...], a1[...], a2[...], a3[...]
@@ -240,6 +270,7 @@
     pupil[0] = re
     pupil[1] = im
     flip = jnp.where((cols & c) == 1, -1.0, 1.0)
+    fetch.wait(0)
     out_re, out_im = dft_right(re * flip, im * flip, mats_of(m), -1.0)
     grid[0] = out_re
     grid[1] = out_im
@@ -259,8 +290,8 @@
         out[at] = grid[:, :, 128 * at : 128 * at + 128]
 
 
-def optics_kernel(scale, idx, b0, b1, b2, b3, f, tw, far, out, grid):
-    mats = mats_of(f)
+def optics_kernel(scale, idx, b0, b1, b2, b3, f_far, tw, far, out, grid, f, sems):
+    fetch = Fetch(sems, (f_far, f))
     for d, block in enumerate((b0, b1, b2, b3)):
         grid[:, pl.ds(aligned(from_of(idx, d)[0], 128), 128), :] = block[...]
     low = (grid[0, :256, :], grid[1, :256, :])
@@ -274,6 +305,8 @@
             re, im = times(re, im, twists[r][0], -twists[r][1])
         res.append(re)
         ims.append(im)
+    fetch.wait(0)
+    mats = mats_of(f)
     far_re, far_im = dft_left(
         jnp.concatenate(res, 1), jnp.concatenate(ims, 1), mats, -1.0
     )
@@ -304,9 +337,11 @@
     eight_rows(out, grid)
 
 
-def scene_columns_kernel(idx, b0, b1, b2, b3, w, out, image, grid):
+def scene_columns_kernel(idx, b0, b1, b2, b3, w_far, out, image, grid, w, sems):
+    fetch = Fetch(sems, (w_far, w))
     for d, block in enumerate((b0, b1, b2, b3)):
         image[pl.ds(aligned(from_of(idx, d)[0], 256), 256), :] = block[...]
+    fetch.wait(0)
     spectrum = by_left(w[0], w[1], image[...])
     grid[0] = spectrum[:512]
     grid[1] = spectrum[512:]
@@ -329,7 +364,7 @@
     return re[:64], jnp.where((rows == 0) & first, re[64:65, :], im[:64])
 
 
-def row_transform(idx, blocks, mats, tw, grid):
+def row_transform(idx, blocks, fetch, f, tw, grid):
     for at in range(8):
         grid[:, :, 128 * at : 128 * at + 128] = blocks[at]
     re, im = unpack_rows(idx, grid[0], grid[1], 8)
@@ -347,6 +382,8 @@
     ]
     for r in range(1, 4):
         parts[r] = times(parts[r][0], parts[r][1], tw[r : r + 1, :], -tw[4 + r : 5 + r, :])
+    fetch.wait(0)
+    mats = mats_of(f)
     return dft_right(
         jnp.concatenate([p[0] for p in parts], 0),
         jnp.concatenate([p[1] for p in parts], 0),
@@ -355,15 +392,15 @@
     )
 
 
-def scene_rows_kernel(idx, blocks, f, tw, out, grid):
-    re, im = row_transform(idx, blocks, mats_of(f), tw, grid)
+def scene_rows_kernel(idx, blocks, f_far, tw, out, grid, f, sems):
+    re, im = row_transform(idx, blocks, Fetch(sems, (f_far, f)), f, tw, grid)
     out[0] = re
     out[1] = im
 
 
-def blur_kernel(idx, blocks, f, tw, spectrum, out, grid):
+def blur_kernel(idx, blocks, f_far, tw, spectrum, out, grid, f, sems):
+    re, im = row_transform(idx, blocks, Fetch(sems, (f_far, f)), f, tw, grid)
     mats = mats_of(f)
-    re, im = row_transform(idx, blocks, mats, tw, grid)
     re, im = times(re, im, spectrum[0], spectrum[1])
     mats = tuple(m[:, :128] for m in mats)
     re, im = dft_right(re, im, mats, 1.0)
@@ -400,8 +437,10 @@
 
 def net_kernel(pixel_count, idx, w1, b1, w2, *refs):
     blocks = refs[:2]
-    v, strip, edge, g_out, acc, loss_out = refs[2:8]
-    grid, win_taps, g_taps, hidden, sums = refs[8:]
+    v_far, strip, edge, g_out, sums_out = refs[2:7]
+    grid, win_taps, g_taps, hidden, sums, acc, v, sems = refs[7:]
+    slot = 2 * idx[0] + idx[1]
+    fetch = Fetch(sems, (v_far.at[:, pl.ds(aligned(slot, 128), ROWS), :], v))
     for d, e in relations:
         s, c = from_of(idx, d, e)
         at = 2 * s + c
@@ -416,25 +455,26 @@
     lanes = lax.broadcasted_iota(jnp.int32, (ROWS, 128), 1)
     row_global = rows + (2 * idx[0] + idx[1]) * 128 - 8
     inside = (row_global >= 0) & (row_global < N)
+    fetch.wait(0)
     window = jnp.where(inside, by_left(v[0], v[1], grid[...]), 0.0)
     for e in (-1, 0, 1):
         side = moved_lanes(window, e, lanes)
         for a in (-1, 0, 1):
             win_taps[3 * (a + 1) + e + 1] = moved_rows(side, a)
-    step = 16
+    step = 24
     for k in range(ROWS // step):
         part = pl.ds(k * step, step)
 
         def forward(c, total, part=part):
-            pre = jnp.full((step, 128), b1[c], F32)
-            for t in range(9):
+            pre = w1[c, 0] * win_taps[0, part, :]
+            for t in range(1, 9):
                 pre = pre + w1[c, t] * win_taps[t, part, :]
-            hid = jnp.maximum(pre, 0.0)
+            hid = jnp.maximum(pre + b1[c], 0.0)
             hidden[c, part, :] = hid
             return tuple(total[t] + w2[t, c] * hid for t in range(9))
 
         total = lax.fori_loop(
-            0, 32, forward, tuple(jnp.zeros((step, 128), F32) for _ in range(9))
+            0, 32, forward, tuple(jnp.zeros((step, 128), F32) for _ in range(9)), unroll=4
         )
         for t in range(9):
             sums[t, part, :] = total[t]
@@ -448,7 +488,7 @@
     residual = jnp.where(inside, restored - target, 0.0)
     own = (rows >= 8) & (rows < 136)
     own_residual = jnp.where(own, residual, 0.0)
-    loss_out[...] = jnp.sum((own_residual * own_residual).reshape(ROWS // 8, 8, 128), 0)
+    loss = jnp.sum(own_residual * own_residual, 0, keepdims=True)
     g_restored = (2.0 / pixel_count) * residual
     for e in (-1, 0, 1):
         side = moved_lanes(g_restored, -e, lanes)
@@ -457,9 +497,12 @@
     acc[...] = jnp.zeros_like(acc)
 
     def folded(x):
-        return x if x.shape[0] == 8 else x[:8] + x[8:]
-
-    for start, step, mine in [(0, 8, False)] + [(8 + 16 * k, 16, True) for k in range(8)] + [
+        total = x[:8]
+        for row in range(8, x.shape[0], 8):
+            total = total + x[row : row + 8]
+        return total
+
+    for start, step, mine in [(0, 8, False)] + [(8 + 32 * k, 32, True) for k in range(4)] + [
         (136, 8, False)
     ]:
         part = pl.ds(start, step)
@@ -478,7 +521,7 @@
             return tuple(total[t] + w1[c, t] * gp for t in range(9))
 
         total = lax.fori_loop(
-            0, 32, backward, tuple(jnp.zeros((step, 128), F32) for _ in range(9))
+            0, 32, backward, tuple(jnp.zeros((step, 128), F32) for _ in range(9)), unroll=4
         )
         for t in range(9):
             sums[t, part, :] = total[t]
@@ -490,14 +533,26 @@
             side = part if side is None else side + part
         g_window = g_window + moved_lanes(side, -e, lanes)
     g_out[...] = g_window[8:136]
+    for c in range(32):
+        sums_out[c, 0:19, :] = jnp.sum(acc[c], 1)
+        sums_out[c, 19:24, :] = jnp.broadcast_to(loss, (5, 128))
 
 
 def otf_grad_kernel(idx, *refs):
     blocks = refs[:2]
-    w, f, tw, spectrum, out, window, grid = refs[2:]
+    w_far, f_far, tw, spectrum, out, window, grid, w, f, sems = refs[2:]
+    slot = 2 * idx[0] + idx[1]
+    fetch = Fetch(
+        sems,
+        (w_far.at[:, pl.ds(aligned(slot, 64), 64), :], w.at[:, pl.ds(0, 64), :]),
+        (w_far.at[:, pl.ds(aligned(slot + 8, 64), 64), :], w.at[:, pl.ds(64, 64), :]),
+        (f_far, f),
+    )
     for d, e in relations:
         s, c = from_of(idx, d, e)
         window[pl.ds(aligned(2 * s + c, 128), 128), :] = blocks[e][d]
+    fetch.wait(0)
+    fetch.wait(1)
     packed = by_left(w[0], w[1], window[...])
     re, im = unpack_rows(idx, packed[:64], packed[64:], 8)
     res, ims = [re], [im]
@@ -505,6 +560,7 @@
         a, b = times(re, im, tw[8 + r : 9 + r, :128], -tw[12 + r : 13 + r, :128])
         res.append(a)
         ims.append(b)
+    fetch.wait(2)
     mats = mats_of(f)
     top = tuple(m[:128, :] for m in mats)
     re, im = dft_right(jnp.concatenate(res, 0), jnp.concatenate(ims, 0), top, -1.0)
@@ -528,8 +584,8 @@
     eight_columns(out, grid)
 
 
-def psf_grad_kernel(idx, blocks, far, f, tw, small, o0, o1, o2, o3, grid):
-    mats = mats_of(f)
+def psf_grad_kernel(idx, blocks, far_far, f_far, tw, small, o0, o1, o2, o3, grid, far, f, sems):
+    fetch = Fetch(sems, (f_far, f), (far_far, far))
     for c in range(2):
         for s in range(4):
             grid[:, 128 * s + 64 * c : 128 * s + 64 * c + 64, :] = blocks[4 * c + s]
@@ -550,10 +606,13 @@
         re = re + nyquist if r % 2 == 0 else re - nyquist
         res.append(re)
         ims.append(im)
+    fetch.wait(0)
+    mats = mats_of(f)
     g_psf = 2.0 * (
         by_left(mats[0], mats[1], jnp.concatenate(res, 1))
         - by_left(mats[2], mats[3], jnp.concatenate(ims, 1))
     )
+    fetch.wait(1)
     re, im = dft_left(g_psf * far[0], g_psf * far[1], mats, 1.0)
     first, second = None, None
     for r in range(4):
@@ -572,15 +631,19 @@
         out[1, 128:136, :] = jnp.zeros((8, 128), F32)
 
 
-def mask_grad_kernel(scale, idx, ratio, b0, b1, b2, b3, m, pupil, keep, send, grid, whole):
+def mask_grad_kernel(scale, idx, ids, got, *refs):
+    b0, b1, b2, b3, m_far, pupil_far, keep, send, grid, whole, m, pupil, sems = refs
+    fetch = Fetch(sems, (m_far, m), (pupil_far, pupil))
     small = None
     for d, block in enumerate((b0, b1, b2, b3)):
         grid[:, :, pl.ds(aligned(from_of(idx, d)[0], 128), 128)] = block[:, 0:128, :]
         part = block[0, 128:136, :]
         small = part if small is None else small + part
+    fetch.wait(0)
     re, im = dft_right(grid[0], grid[1], mats_of(m), 1.0)
+    fetch.wait(1)
     cols = lax.broadcasted_iota(jnp.int32, (128, 512), 1)
-    factor = ratio[0] * scale
+    factor = ratio_of(jnp.where(idx[2] == 1, ids[1], got[1]))[0:1, 0:1] * scale
     factor = jnp.where((cols & idx[1]) == 1, -factor, factor)
     whole[...] = factor * (im * pupil[0] - re * pupil[1])
     both = jnp.concatenate([small, small], 1)
@@ -596,28 +659,25 @@
     whole[...] = keep[...] + other[...]
     piece = 128 // ways
     for d, out in enumerate(outs):
-        to = lax.rem(idx[4] + d, ways)
+        to = lax.rem(idx[3] + d, ways)
         out[0:piece, :] = whole[pl.ds(aligned(to, piece), piece), :]
         out[piece : piece + 8, :] = whole[128:136, :]
 
 
 def home_kernel(ways, idx, *refs):
-    near = refs[:ways]
-    far = refs[ways : 2 * ways]
-    out = refs[2 * ways]
+    blocks = refs[:ways]
+    out = refs[ways]
     piece = 128 // ways
-    at_home = idx[0] == 1 + idx[1]
     central = (idx[0] == 1) | (idx[0] == 2)
     out[0:256, :] = jnp.zeros((256, 256), F32)
     out[768:1024, :] = jnp.zeros((256, 256), F32)
     for back in range(ways):
-        y = lax.rem(idx[4] + ways - back, ways)
+        y = lax.rem(idx[3] + ways - back, ways)
         for d in range(4):
             s = from_of(idx, d)[0]
-            row = 256 + 128 * s + piece * y
-            block = jnp.where(at_home, near[back][d], far[back][d])
-            out[pl.ds(aligned(8 + 4 * s + y, 32) if ways == 4 else row, piece), :] = jnp.where(
-                central, block, 0.0
+            at = (2 + s) * ways + y
+            out[pl.ds(aligned(at, piece), piece), :] = jnp.where(
+                central, blocks[back][d], 0.0
             )
 
 
@@ -629,6 +689,7 @@
     owner = c == lax.axis_index("grp")
     pixel_count = float(lay.dp * N * 128)
     scale_psf = 1.0 / (N * N * pupil_count(N))
+    idx = jnp.stack([s, c, owner.astype(jnp.int32), y]).astype(jnp.int32)
 
     def swap(g, zh, y, c, s):
         return (g, zh, y, 1 - c, s)
@@ -647,23 +708,20 @@
         return near, lay.move(near, swap)
 
     ids = jnp.concatenate([sample_ids, wave_ids])
-    ids = jnp.where(owner, ids, lay.move(ids, swap))
-    idx = jnp.stack([s, c, ids[0], owner.astype(jnp.int32), y]).astype(jnp.int32)
-    ratio = (550.0 / (400.0 + 10.0 * ids[1].astype(F32))).reshape(1)
-    other = lay.move(
-        jnp.concatenate(
-            [lax.dynamic_slice_in_dim(scene[0], 512 * (1 - c), 512, 1), scene[0, :, 256:384]], 1
-        ),
-        swap,
-    )
+    got = lay.move(ids, swap)
 
     mine, *sent = call(
         phase_kernel,
-        (idx, ratio, phase_mask, height_offsets),
-        (0, 1),
+        (idx, ids, got, phase_mask, height_offsets),
+        (0, 1, 2),
         [(128, 256)] * 4,
-        [pltpu.VMEM((512, 256), jnp.int32), pltpu.VMEM((512, 256), F32), pltpu.SemaphoreType.DMA],
-        {3: pl.ANY},
+        [
+            pltpu.VMEM((512, 256), F32),
+            pltpu.VMEM((512, 256), jnp.int32),
+            pltpu.VMEM((512, 256), F32),
+            fetch_sems(2),
+        ],
+        (3, 4),
     )
     tables = ({1: 0, 2: 3}, {1: 2, 2: 1}, {1: 3, 2: 0})
     pieces = [mine] + [
@@ -674,6 +732,14 @@
         for block, to in zip(sent, tables)
     ]
 
+    scene, mine = lax.optimization_barrier((scene, mine))
+    pieces[0] = mine
+    other = lay.move(
+        jnp.concatenate(
+            [lax.dynamic_slice_in_dim(scene[0], 512 * (1 - c), 512, 1), scene[0, :, 256:384]], 1
+        ),
+        swap,
+    )
     *columns, strip, edge = call(
         scene_kernel,
         (idx, scene, other),
@@ -683,23 +749,13 @@
     columns = along_sp(columns)
     edge = lay.move(edge, lambda g, zh, y, c, s: (g, zh, y, c, s + 1 - 2 * c))
 
-    slot = 2 * s + c
-    unpack = lax.dynamic_slice_in_dim(jnp.asarray(con["unpack"]), 128 * slot, ROWS, 1)
-    pack = jnp.asarray(con["pack"])
-    pack_rows = jnp.concatenate(
-        [
-            lax.dynamic_slice_in_dim(pack, 64 * slot, 64, 1),
-            lax.dynamic_slice_in_dim(pack, 512 + 64 * slot, 64, 1),
-        ],
-        1,
-    )
-
     *field, pupil = call(
         pupil_kernel,
         (idx, *pieces, con["m"]),
         (0,),
         [(2, 128, 128)] * 4 + [(2, 128, 512)],
-        [pltpu.VMEM((2, 128, 512), F32)],
+        [pltpu.VMEM((2, 128, 512), F32), bf16_buffer(4, 512, 512), fetch_sems(1)],
+        (5,),
     )
     field = along_sp(field)
     (scene_part,) = call(
@@ -707,7 +763,13 @@
         (idx, *columns, con["pack"]),
         (0,),
         [(8, 2, 64, 128)],
-        [pltpu.VMEM((N, 128), F32), pltpu.VMEM((2, 512, 128), F32)],
+        [
+            pltpu.VMEM((N, 128), F32),
+            pltpu.VMEM((2, 512, 128), F32),
+            bf16_buffer(2, N, N),
+            fetch_sems(1),
+        ],
+        (5,),
     )
     scene_part = to_eight(scene_part)
     far, otf_part = call(
@@ -715,16 +777,18 @@
         (idx, *field, con["f"], con["tw_col"]),
         (0,),
         [(2, 256, 512), (8, 2, 64, 128)],
-        [pltpu.VMEM((2, 512, 128), F32)],
+        [pltpu.VMEM((2, 512, 128), F32), bf16_buffer(4, 256, 256), fetch_sems(1)],
+        (5,),
     )
     otf_part = to_eight(otf_part)
-    row_scratch = [pltpu.VMEM((2, 64, N), F32)]
+    row_scratch = [pltpu.VMEM((2, 64, N), F32), bf16_buffer(4, 256, 256), fetch_sems(1)]
     (spectrum,) = call(
         scene_rows_kernel,
         (idx, scene_part, con["f"], con["tw_row"]),
         (0,),
         [(2, 288, 256)],
         row_scratch,
+        (2,),
     )
     (half_window,) = call(
         blur_kernel,
@@ -732,31 +796,41 @@
         (0,),
         [(2, 64, 128)],
         row_scratch,
+        (2,),
     )
     window_parts = gathered(half_window)
-    g_window, acc, loss_part = call(
+    g_window, sums = call(
         functools.partial(net_kernel, pixel_count),
-        (idx, w1, b1, w2, *window_parts, unpack, strip, edge),
+        (idx, w1, b1, w2, *window_parts, con["unpack"], strip, edge),
         (0, 1, 2, 3),
-        [(128, 128), (32, 19, 8, 128), (8, 128)],
+        [(128, 128), (32, 24, 128)],
         [
             pltpu.VMEM((N, 128), F32),
             pltpu.VMEM((9, ROWS, 128), F32),
             pltpu.VMEM((9, ROWS, 128), F32),
             pltpu.VMEM((32, ROWS, 128), F32),
             pltpu.VMEM((9, ROWS, 128), F32),
+            pltpu.VMEM((32, 19, 8, 128), F32),
+            bf16_buffer(2, ROWS, N),
+            fetch_sems(1),
         ],
-    )
-    small = jnp.concatenate(
-        [jnp.sum(acc, (2, 3)).reshape(-1), jnp.sum(loss_part).reshape(1), jnp.zeros((415,), F32)]
-    ).reshape(8, 128)
+        (6,),
+    )
+    small = jnp.pad(jnp.sum(sums, 2).reshape(6, 128), ((0, 2), (0, 0)))
     g_parts = gathered(g_window)
     (otf_grad,) = call(
         otf_grad_kernel,
-        (idx, *g_parts, pack_rows, con["f"], con["tw_row"], spectrum),
+        (idx, *g_parts, con["pack"], con["f"], con["tw_row"], spectrum),
         (0,),
         [(8, 2, 64, 128)],
-        [pltpu.VMEM((N, 128), F32), pltpu.VMEM((2, 64, N), F32)],
+        [
+            pltpu.VMEM((N, 128), F32),
+            pltpu.VMEM((2, 64, N), F32),
+            bf16_buffer(2, 128, N),
+            bf16_buffer(4, 256, 256),
+            fetch_sems(3),
+        ],
+        (3, 4),
     )
     otf_grad = to_eight(otf_grad)
     field_grad = along_sp(
@@ -765,15 +839,28 @@
             (idx, otf_grad, far, con["f"], con["tw_col"], small),
             (0,),
             [(2, 136, 128)] * 4,
-            [pltpu.VMEM((2, 512, 128), F32)],
+            [
+                pltpu.VMEM((2, 512, 128), F32),
+                pltpu.VMEM((2, 256, 512), F32),
+                bf16_buffer(4, 256, 256),
+                fetch_sems(2),
+            ],
+            (2, 3),
         )
     )
     keep, send = call(
         functools.partial(mask_grad_kernel, 2.0 * scale_psf),
-        (idx, ratio, *field_grad, con["m"], pupil),
-        (0, 1),
+        (idx, ids, got, *field_grad, con["m"], pupil),
+        (0, 1, 2),
         [(136, 256)] * 2,
-        [pltpu.VMEM((2, 128, 512), F32), pltpu.VMEM((128, 512), F32)],
+        [
+            pltpu.VMEM((2, 128, 512), F32),
+            pltpu.VMEM((128, 512), F32),
+            bf16_buffer(4, 512, 512),
+            pltpu.VMEM((2, 128, 512), F32),
+            fetch_sems(2),
+        ],
+        (7, 8),
     )
 
     piece = 128 // lay.y
@@ -807,29 +894,23 @@
             for d in (1, 2, 3)
         ]
     )
+    at_home = s == 1 + c
+    crossed = lay.move(home, lambda g, zh, y, c, s: (g, zh, y, 1 - c, s) if s == 1 + c else None)
+    home = jnp.where(at_home, home, crossed)
     near = [home] + [
         lay.move(
-            home,
-            lambda g, zh, y, c, s, d=d: (g, zh, y + d, c, s) if s == 1 + c else None,
+            home, lambda g, zh, y, c, s, d=d: (g, zh, y + d, c, s) if s in (1, 2) else None
         )
         for d in range(1, lay.y)
     ]
-    across = [
-        lay.move(
-            block, lambda g, zh, y, c, s: (g, zh, y, 1 - c, s) if s == 1 + c else None
-        )
-        for block in near
-    ]
-    (mask_grad,) = call(
-        functools.partial(home_kernel, lay.y), (idx, *near, *across), (0,), [(N, 256)]
-    )
-    table = small[:608].reshape(32, 19)
+    (mask_grad,) = call(functools.partial(home_kernel, lay.y), (idx, *near), (0,), [(N, 256)])
+    table = small[:768].reshape(32, 24)
     return (
         mask_grad,
         table[:, :9],
         table[:, 18],
         table[:, 9:18].T,
-        small[608] / pixel_count,
+        table[0, 19] / pixel_count,
     )
 
 

time: 222 us -> 235 us (1.059)
  Pallas kernels: 41.4 us -> 63.7 us
  local copies, waits for them, and re-layouts: 28.6 us -> 13.2 us
  waiting for transfers between devices: 57.9 us -> 67.7 us
    pallas_call x13, Pallas kernels: 41.4 us -> 63.7 us  [call(): pl.pallas_call(kernel, out_shape=[jax.ShapeDtypeStruct(shape, F32) for sh...]
    unnamed x51 -> x73, local copies, waits for them, and re-layouts: 20.7 us -> 11 us
    ppermute x41 -> x38, waiting for transfers between devices: 47.1 us -> 55 us  [move(): return lax.ppermute(x, AXES, pairs)]
    reduce_sum x2 -> x1, other arithmetic: 3.3 us -> 0.17 us  [on_device(): small = jnp.pad(jnp.sum(sums, 2).reshape(6, 128), ((0, 2), (0, 0)))]
    dynamic_slice x2 -> x0, local copies, waits for them, and re-layouts: 3.04 us -> none  [the longest x1 1.98 us: on_device(): lax.dynamic_slice_in_dim(jnp.asarray(con['unpack']), 128 * slot, ROWS, 1)]
    all_to_all x3, starting transfers between devices: 19.4 us -> 16.7 us  [to_eight(): return lax.all_to_all(blocks, ('core', 'sp'), 0, 0, tiled=True)]
    ppermute x41 -> x38, starting transfers between devices: 62 us -> 64.8 us  [move(): return lax.ppermute(x, AXES, pairs)]
  transfers between devices with their start and end apart: 44 -> 41, of which waited for: 28 -> 32; matrix products, arithmetic and copies ran while one was open for 5% -> 2% of each run, Pallas kernels for 3% -> 6%
where the time goes in v1:
time: 235 us; the launch traced here: 234 us
  starting transfers between devices  81.5 us (35%)
  waiting for transfers between devices  67.7 us (29%)
  Pallas kernels  63.7 us (27%)
  local copies, waits for them, and re-layouts  13.2 us (6%)
  between operations  4.25 us (2%)
  other arithmetic  3.47 us (1%)
    ppermute x38, starting transfers between devices, move(): return lax.ppermute(x, AXES, pairs)  64.8 us
    pallas_call x13, Pallas kernels, call(): pl.pallas_call(kernel, out_shape=[jax.ShapeDtypeStruct(shape, F32) for sh...  63.7 us
    ppermute x38, waiting for transfers between devices, move(): return lax.ppermute(x, AXES, pairs)  55 us
    all_to_all x3, starting transfers between devices, to_eight(): return lax.all_to_all(blocks, ('core', 'sp'), 0, 0, tiled=True)  16.7 us
    all_to_all x3, waiting for transfers between devices, to_eight(): return lax.all_to_all(blocks, ('core', 'sp'), 0, 0, tiled=True)  12.7 us
    unnamed x73, local copies, waits for them, and re-layouts  11 us
  transfers between devices with their start and end apart: 41, of which 32 were waited for; matrix products, arithmetic and copies ran while one was open for 2% of the time, Pallas kernels for 6%

profile of v1, /device:TPU:3, one launch (start us, length us, event | category | flops | bytes accessed | tf_op | source)
XLA Modules:
  0.0 233.8 jit_solution(14289432824042571022)
XLA Ops:
  19.9 3.5 %collective-permute-done.10.b3 = f32[256,128]{1,0:T(8,128)S(1)} collective-permute-done((f32[256,128]{1,0:T(8,128)}, f32[256,128]{1,0:T(8,128)S(1)}, u32[]{:S(2)}, u32[]{:S(2)}) %collective-permute-start.10) | collective-permute-done | bytes 131104 | tf_op jit(solution)/shard_map/ppermute | solution.py:85
  24.0 5.9 %shard_map.177 = f32[8,2,64,128]{3,2,1,0:T(8,128)} custom-call(s32[4]{0:T(128)} %pad_add_fusion.idx, f32[256,128]{1,0:T(8,128)} %get-tuple-element.47.b0, f32[256,128]{1,0:T(8,128)} %copy-done.21, f32[256,128]{1,0:T(8,128)} %copy-done.24, f32[256,128]{1,0:T(8,128)} %copy-done.26, bf16[2,1024,1024]{2,1,0:T(8,128)(2,1)} %constant.45.clone.w_far.refs_2_), custom_call_target="tpu_custom_call" | custom-call | tf_op jit(solution)/shard_map/pallas_call | solution.py:179
  30.0 5.7 %all-to-all-start.1 = ((f32[8,2,64,128]{3,2,1,0:T(8,128)}), f32[8,2,64,128]{3,2,1,0:T(8,128)S(1)}, u32[]{:S(2)}, u32[]{:S(2)}) async-start(f32[8,2,64,128]{3,2,1,0:T(8,128)} %shard_map.177), calls=%async_computation.1 | async-start | bytes 1048576 | tf_op jit(solution)/shard_map/all_to_all | solution.py:704
  37.6 3.9 %collective-permute-start.2 = (f32[128,256]{1,0:T(8,128)S(1)}, f32[128,256]{1,0:T(8,128)S(1)}, u32[]{:S(2)}, u32[]{:S(2)}) collective-permute-start(f32[128,256]{1,0:T(8,128)S(1)} %copy-done.32), channel_id=1, source_target_pairs={{1,2},{2,1},{5,6},{6,5},{9,10},{10,9},{13,14},{14,13},{17,18},{18,... | collective-permute-start | bytes 393224 | tf_op jit(solution)/shard_map/ppermute | solution.py:85
  48.5 4.8 %shard_map.174 = (f32[2,128,128]{2,1,0:T(8,128)}, f32[2,128,128]{2,1,0:T(8,128)}, f32[2,128,128]{2,1,0:T(8,128)}, f32[2,128,128]{2,1,0:T(8,128)}, f32[2,128,512]{2,1,0:T(8,128)}) custom-call(s32[4]{0:T(128)} %pad_add_fusion.idx, f32[128,256]{1,0:T(8,128)} %get-tuple-element.37.a0, f32[128,256]{1,0:T(8,128)} %copy-done.17, f32[128,256]{1,0:T(8,128)} %copy-done.19, ...), custom_call_target="tpu_custom_call" | custom-call | tf_op jit(solution)/shard_map/pallas_call | solution.py:179
  53.9 4.3 %collective-permute-start.5 = (f32[2,128,128]{2,1,0:T(8,128)}, f32[2,128,128]{2,1,0:T(8,128)S(1)}, u32[]{:S(2)}, u32[]{:S(2)}) collective-permute-start(f32[2,128,128]{2,1,0:T(8,128)} %get-tuple-element.43), channel_id=1, source_target_pairs={{0,2},{1,3},{2,0},{3,1},{4,6},{5,7},{6,4},{7,5},{8,10},{9,11},{10,... | collective-permute-start | bytes 393224 | tf_op jit(solution)/shard_map/ppermute | solution.py:85
  64.9 4.8 %shard_map.175 = (f32[2,256,512]{2,1,0:T(8,128)}, f32[8,2,64,128]{3,2,1,0:T(8,128)}) custom-call(s32[4]{0:T(128)} %pad_add_fusion.idx, f32[2,128,128]{2,1,0:T(8,128)} %get-tuple-element.41.b0, f32[2,128,128]{2,1,0:T(8,128)} %copy-done.20, f32[2,128,128]{2,1,0:T(8,128)} %copy-done.23, f32[2,128,128]{2,1,0:T(8,128)} %copy-done.25, ...), custom_call_target="tpu_custom_call" | custom-call | tf_op jit(solution)/shard_map/pallas_call | solution.py:179
  69.7 6.4 %all-to-all-start = ((f32[8,2,64,128]{3,2,1,0:T(8,128)}), f32[8,2,64,128]{3,2,1,0:T(8,128)S(1)}, u32[]{:S(2)}, u32[]{:S(2)}) async-start(f32[8,2,64,128]{3,2,1,0:T(8,128)} %get-tuple-element.45), calls=%async_computation | async-start | bytes 1048576 | tf_op jit(solution)/shard_map/all_to_all | solution.py:704
  76.1 3.6 %shard_map.178.spectrum.refs_5_ = f32[2,288,256]{2,1,0:T(8,128)} custom-call(s32[4]{0:T(128)} %pad_add_fusion.idx, f32[8,2,64,128]{3,2,1,0:T(8,128)} %copy-done.2, bf16[4,256,256]{2,1,0:T(8,128)(2,1)} %constant.46.clone.f_far.refs_3_, f32[16,256]{1,0:T(8,128)} %constant.48.clone.tw.refs_4_), custom_call_target="tpu_custom_call" | custom-call | tf_op jit(solution)/shard_map/pallas_call | solution.py:179
  79.7 5.0 %all-to-all-done.blocks = f32[8,2,64,128]{3,2,1,0:T(8,128)S(1)} async-done(((f32[8,2,64,128]{3,2,1,0:T(8,128)}), f32[8,2,64,128]{3,2,1,0:T(8,128)S(1)}, u32[]{:S(2)}, u32[]{:S(2)}) %all-to-all-start) | async-done | bytes 524320 | tf_op jit(solution)/shard_map/all_to_all | solution.py:704
  85.5 5.0 %shard_map.179 = f32[2,64,128]{2,1,0:T(8,128)} custom-call(s32[4]{0:T(128)} %pad_add_fusion.idx, f32[8,2,64,128]{3,2,1,0:T(8,128)} %copy-done.3, bf16[4,256,256]{2,1,0:T(8,128)(2,1)} %constant.46.clone.f_far.refs_3_, f32[16,256]{1,0:T(8,128)} %constant.48.clone.tw.refs_4_, f32[2,288,256]{2,1,0:T(8,128)} %shard_map.178.spectrum.refs_5_), custom_call_target="tpu_custom_call" | custom-call | tf_op jit(solution)/shard_map/pallas_call | solution.py:179
  102.9 15.7 %shard_map.180 = (f32[128,128]{1,0:T(8,128)}, f32[32,24,128]{2,1,0:T(8,128)}) custom-call(s32[4]{0:T(128)} %pad_add_fusion.idx, f32[32,9]{1,0:T(8,128)} %copy.26.w1, f32[32]{0:T(128)} %b1.1, f32[9,32]{1,0:T(8,128)} %w2.1, f32[4,2,64,128]{3,2,1,0:T(8,128)} %copy-done.4, f32[4,2,64,128]{3,2,1,0:T(8,128)} %copy-done.9, ...), custom_call_target="tpu_custom_call" | custom-call | tf_op jit(solution)/shard_map/pallas_call | solution.py:179
  126.1 4.2 %collective-permute-start.19 = (f32[4,128,128]{2,1,0:T(8,128)S(1)}, f32[4,128,128]{2,1,0:T(8,128)S(1)}, u32[]{:S(2)}, u32[]{:S(2)}) collective-permute-start(f32[4,128,128]{2,1,0:T(8,128)S(1)} %pad_maximum_fusion.2.refs_0_), channel_id=1, source_target_pairs={{0,4},{1,5},{2,6},{3,7},{4,0},{5,1},{6,2},{7,3},{8,12},{9,13},{10,... | collective-permute-start | bytes 786440 | tf_op jit(solution)/shard_map/ppermute | solution.py:85
  132.1 5.7 %shard_map.181 = f32[8,2,64,128]{3,2,1,0:T(8,128)} custom-call(s32[4]{0:T(128)} %pad_add_fusion.idx, f32[4,128,128]{2,1,0:T(8,128)} %copy-done.5, f32[4,128,128]{2,1,0:T(8,128)} %copy-done.10, bf16[2,1024,1024]{2,1,0:T(8,128)(2,1)} %constant.45.clone.w_far.refs_2_, bf16[4,256,256]{2,1,0:T(8,128)(2,1)} %constant.46.clone.f_far.refs_3_, ...), custom_call_target="tpu_custom_call" | custom-call | tf_op jit(solution)/shard_map/pallas_call | solution.py:179
  137.8 4.6 %all-to-all-start.2 = ((f32[8,2,64,128]{3,2,1,0:T(8,128)}), f32[8,2,64,128]{3,2,1,0:T(8,128)S(1)}, u32[]{:S(2)}, u32[]{:S(2)}) async-start(f32[8,2,64,128]{3,2,1,0:T(8,128)} %shard_map.181), calls=%async_computation.2 | async-start | bytes 1048576 | tf_op jit(solution)/shard_map/all_to_all | solution.py:704
  143.3 7.7 %all-to-all-done.2.blocks = f32[8,2,64,128]{3,2,1,0:T(8,128)S(1)} async-done(((f32[8,2,64,128]{3,2,1,0:T(8,128)}), f32[8,2,64,128]{3,2,1,0:T(8,128)S(1)}, u32[]{:S(2)}, u32[]{:S(2)}) %all-to-all-start.2) | async-done | bytes 524320 | tf_op jit(solution)/shard_map/all_to_all | solution.py:704
  151.8 4.9 %shard_map.182 = (f32[2,136,128]{2,1,0:T(8,128)}, f32[2,136,128]{2,1,0:T(8,128)}, f32[2,136,128]{2,1,0:T(8,128)}, f32[2,136,128]{2,1,0:T(8,128)}) custom-call(s32[4]{0:T(128)} %pad_add_fusion.idx, f32[8,2,64,128]{3,2,1,0:T(8,128)} %copy-done.1, f32[2,256,512]{2,1,0:T(8,128)} %get-tuple-element.54.far_far, bf16[4,256,256]{2,1,0:T(8,128)(2,1)} %constant.46.clone.f_far.refs_3_, ...), custom_call_target="tpu_custom_call" | custom-call | tf_op jit(solution)/shard_map/pallas_call | solution.py:179
  163.5 3.6 %collective-permute-done.22.refs_3_ = f32[2,136,128]{2,1,0:T(8,128)S(1)} collective-permute-done((f32[2,136,128]{2,1,0:T(8,128)}, f32[2,136,128]{2,1,0:T(8,128)S(1)}, u32[]{:S(2)}, u32[]{:S(2)}) %collective-permute-start.22) | collective-permute-done | bytes 139296 | tf_op jit(solution)/shard_map/ppermute | solution.py:85
  167.8 4.5 %shard_map.183 = (f32[136,256]{1,0:T(8,128)}, f32[136,256]{1,0:T(8,128)}) custom-call(s32[4]{0:T(128)} %pad_add_fusion.idx, s32[2]{0:T(128)} %copy-done.29, s32[2]{0:T(128)} %copy-done.30, f32[2,136,128]{2,1,0:T(8,128)} %get-tuple-element.56.refs_0_, f32[2,136,128]{2,1,0:T(8,128)} %copy-done.11, f32[2,136,128]{2,1,0:T(8,128)} %copy-done.12, ...), custom_call_target="tpu_custom_call" | custom-call | tf_op jit(solution)/shard_map/pallas_call | solution.py:179
  186.3 5.8 %collective-permute-start.30 = (f32[40,256]{1,0:T(8,128)S(1)}, f32[40,256]{1,0:T(8,128)S(1)}, u32[]{:S(2)}, u32[]{:S(2)}) collective-permute-start(f32[40,256]{1,0:T(8,128)S(1)} %add.34), channel_id=1, source_target_pairs={{0,96},{1,97},{2,98},{3,99},{4,100},{5,101},{6,102},{7,103},{8,104... | collective-permute-start | bytes 122888 | tf_op jit(solution)/shard_map/ppermute | solution.py:85
  195.4 3.6 %collective-permute-done.29 = f32[40,256]{1,0:T(8,128)S(1)} collective-permute-done((f32[40,256]{1,0:T(8,128)S(1)}, f32[40,256]{1,0:T(8,128)S(1)}, u32[]{:S(2)}, u32[]{:S(2)}) %collective-permute-start.29) | collective-permute-done | bytes 40992 | tf_op jit(solution)/shard_map/ppermute | solution.py:85
  205.1 9.1 %collective-permute-done.34 = f32[4,32,256]{2,1,0:T(8,128)S(1)} collective-permute-done((f32[4,32,256]{2,1,0:T(8,128)S(1)}, f32[4,32,256]{2,1,0:T(8,128)S(1)}, u32[]{:S(2)}, u32[]{:S(2)}) %collective-permute-start.34) | collective-permute-done | bytes 131104 | tf_op jit(solution)/shard_map/ppermute | solution.py:85
  214.2 4.2 %collective-permute-start.37 = (f32[4,32,256]{2,1,0:T(8,128)S(1)}, f32[4,32,256]{2,1,0:T(8,128)S(1)}, u32[]{:S(2)}, u32[]{:S(2)}) collective-permute-start(f32[4,32,256]{2,1,0:T(8,128)S(1)} %broadcast_select_fusion.refs_0_), channel_id=1, source_target_pairs={{1,25},{2,26},{5,29},{6,30},{9,1},{10,2},{13,5},{14,6},{17,9},{18,... | collective-permute-start | bytes 393224 | tf_op jit(solution)/shard_map/ppermute | solution.py:85
  226.5 3.4 %collective-permute-done.35.refs_1_ = f32[4,32,256]{2,1,0:T(8,128)S(1)} collective-permute-done((f32[4,32,256]{2,1,0:T(8,128)S(1)}, f32[4,32,256]{2,1,0:T(8,128)S(1)}, u32[]{:S(2)}, u32[]{:S(2)}) %collective-permute-start.35) | collective-permute-done | bytes 131104 | tf_op jit(solution)/shard_map/ppermute | solution.py:85
  (165 shorter events, 99.7 us)
Async XLA Ops:
  12.5 5.8 %collective-permute-start.8 = (f32[256,128]{1,0:T(8,128)}, f32[256,128]{1,0:T(8,128)S(1)}, u32[]{:S(2)}, u32[]{:S(2)}) collective-permute-start(f32[256,128]{1,0:T(8,128)} %get-tuple-element.48), channel_id=1, source_target_pairs={{0,1},{1,2},{2,3},{3,0},{4,5},{5,6},{6,7},{7,4},{8,9},{9,10},{10,1... | collective-permute-start | bytes 393224 | tf_op jit(solution)/shard_map/ppermute | solution.py:85
  13.7 6.2 %collective-permute-start.9 = (f32[256,128]{1,0:T(8,128)}, f32[256,128]{1,0:T(8,128)S(1)}, u32[]{:S(2)}, u32[]{:S(2)}) collective-permute-start(f32[256,128]{1,0:T(8,128)} %get-tuple-element.49), channel_id=1, source_target_pairs={{0,2},{1,3},{2,0},{3,1},{4,6},{5,7},{6,4},{7,5},{8,10},{9,11},{10,... | collective-permute-start | bytes 393224 | tf_op jit(solution)/shard_map/ppermute | solution.py:85
  16.2 7.2 %collective-permute-start.10 = (f32[256,128]{1,0:T(8,128)}, f32[256,128]{1,0:T(8,128)S(1)}, u32[]{:S(2)}, u32[]{:S(2)}) collective-permute-start(f32[256,128]{1,0:T(8,128)} %get-tuple-element.50), channel_id=1, source_target_pairs={{0,3},{1,0},{2,1},{3,2},{4,7},{5,4},{6,5},{7,6},{8,11},{9,8},{10,9... | collective-permute-start | bytes 393224 | tf_op jit(solution)/shard_map/ppermute | solution.py:85
  30.0 39.7 %all-to-all-start.1 = ((f32[8,2,64,128]{3,2,1,0:T(8,128)}), f32[8,2,64,128]{3,2,1,0:T(8,128)S(1)}, u32[]{:S(2)}, u32[]{:S(2)}) async-start(f32[8,2,64,128]{3,2,1,0:T(8,128)} %shard_map.177), calls=%async_computation.1 | async-start | bytes 1048576 | tf_op jit(solution)/shard_map/all_to_all | solution.py:704
  35.6 8.7 %collective-permute-start.1 = (f32[128,256]{1,0:T(8,128)S(1)}, f32[128,256]{1,0:T(8,128)S(1)}, u32[]{:S(2)}, u32[]{:S(2)}) collective-permute-start(f32[128,256]{1,0:T(8,128)S(1)} %copy-done.33), channel_id=1, source_target_pairs={{1,0},{2,3},{5,4},{6,7},{9,8},{10,11},{13,12},{14,15},{17,16},{18,... | collective-permute-start | bytes 393224 | tf_op jit(solution)/shard_map/ppermute | solution.py:85
  37.6 9.6 %collective-permute-start.2 = (f32[128,256]{1,0:T(8,128)S(1)}, f32[128,256]{1,0:T(8,128)S(1)}, u32[]{:S(2)}, u32[]{:S(2)}) collective-permute-start(f32[128,256]{1,0:T(8,128)S(1)} %copy-done.32), channel_id=1, source_target_pairs={{1,2},{2,1},{5,6},{6,5},{9,10},{10,9},{13,14},{14,13},{17,18},{18,... | collective-permute-start | bytes 393224 | tf_op jit(solution)/shard_map/ppermute | solution.py:85
  41.6 5.7 %collective-permute-start.3 = (f32[128,256]{1,0:T(8,128)S(1)}, f32[128,256]{1,0:T(8,128)S(1)}, u32[]{:S(2)}, u32[]{:S(2)}) collective-permute-start(f32[128,256]{1,0:T(8,128)S(1)} %copy-done.31), channel_id=1, source_target_pairs={{1,3},{2,0},{5,7},{6,4},{9,11},{10,8},{13,15},{14,12},{17,19},{18,... | collective-permute-start | bytes 393224 | tf_op jit(solution)/shard_map/ppermute | solution.py:85
  53.3 6.3 %collective-permute-start.4 = (f32[2,128,128]{2,1,0:T(8,128)}, f32[2,128,128]{2,1,0:T(8,128)S(1)}, u32[]{:S(2)}, u32[]{:S(2)}) collective-permute-start(f32[2,128,128]{2,1,0:T(8,128)} %get-tuple-element.42), channel_id=1, source_target_pairs={{0,1},{1,2},{2,3},{3,0},{4,5},{5,6},{6,7},{7,4},{8,9},{9,10},{10,1... | collective-permute-start | bytes 393224 | tf_op jit(solution)/shard_map/ppermute | solution.py:85
  53.9 7.2 %collective-permute-start.5 = (f32[2,128,128]{2,1,0:T(8,128)}, f32[2,128,128]{2,1,0:T(8,128)S(1)}, u32[]{:S(2)}, u32[]{:S(2)}) collective-permute-start(f32[2,128,128]{2,1,0:T(8,128)} %get-tuple-element.43), channel_id=1, source_target_pairs={{0,2},{1,3},{2,0},{3,1},{4,6},{5,7},{6,4},{7,5},{8,10},{9,11},{10,... | collective-permute-start | bytes 393224 | tf_op jit(solution)/shard_map/ppermute | solution.py:85
  58.2 6.1 %collective-permute-start.6 = (f32[2,128,128]{2,1,0:T(8,128)}, f32[2,128,128]{2,1,0:T(8,128)S(1)}, u32[]{:S(2)}, u32[]{:S(2)}) collective-permute-start(f32[2,128,128]{2,1,0:T(8,128)} %get-tuple-element.44), channel_id=1, source_target_pairs={{0,3},{1,0},{2,1},{3,2},{4,7},{5,4},{6,5},{7,6},{8,11},{9,8},{10,9... | collective-permute-start | bytes 393224 | tf_op jit(solution)/shard_map/ppermute | solution.py:85
  69.7 15.0 %all-to-all-start = ((f32[8,2,64,128]{3,2,1,0:T(8,128)}), f32[8,2,64,128]{3,2,1,0:T(8,128)S(1)}, u32[]{:S(2)}, u32[]{:S(2)}) async-start(f32[8,2,64,128]{3,2,1,0:T(8,128)} %get-tuple-element.45), calls=%async_computation | async-start | bytes 1048576 | tf_op jit(solution)/shard_map/all_to_all | solution.py:704
  91.7 5.5 %collective-permute-start.11 = (f32[2,64,128]{2,1,0:T(8,128)}, f32[2,64,128]{2,1,0:T(8,128)S(1)}, u32[]{:S(2)}, u32[]{:S(2)}) collective-permute-start(f32[2,64,128]{2,1,0:T(8,128)} %shard_map.179), channel_id=1, source_target_pairs={{0,1},{1,2},{2,3},{3,0},{4,5},{5,6},{6,7},{7,4},{8,9},{9,10},{10,1... | collective-permute-start | bytes 196616 | tf_op jit(solution)/shard_map/ppermute | solution.py:85
  126.1 5.4 %collective-permute-start.19 = (f32[4,128,128]{2,1,0:T(8,128)S(1)}, f32[4,128,128]{2,1,0:T(8,128)S(1)}, u32[]{:S(2)}, u32[]{:S(2)}) collective-permute-start(f32[4,128,128]{2,1,0:T(8,128)S(1)} %pad_maximum_fusion.2.refs_0_), channel_id=1, source_target_pairs={{0,4},{1,5},{2,6},{3,7},{4,0},{5,1},{6,2},{7,3},{8,12},{9,13},{10,... | collective-permute-start | bytes 786440 | tf_op jit(solution)/shard_map/ppermute | solution.py:85
  137.8 13.2 %all-to-all-start.2 = ((f32[8,2,64,128]{3,2,1,0:T(8,128)}), f32[8,2,64,128]{3,2,1,0:T(8,128)S(1)}, u32[]{:S(2)}, u32[]{:S(2)}) async-start(f32[8,2,64,128]{3,2,1,0:T(8,128)} %shard_map.181), calls=%async_computation.2 | async-start | bytes 1048576 | tf_op jit(solution)/shard_map/all_to_all | solution.py:704
  156.7 5.3 %collective-permute-start.20 = (f32[2,136,128]{2,1,0:T(8,128)}, f32[2,136,128]{2,1,0:T(8,128)S(1)}, u32[]{:S(2)}, u32[]{:S(2)}) collective-permute-start(f32[2,136,128]{2,1,0:T(8,128)} %get-tuple-element.57), channel_id=1, source_target_pairs={{0,1},{1,2},{2,3},{3,0},{4,5},{5,6},{6,7},{7,4},{8,9},{9,10},{10,1... | collective-permute-start | bytes 417800 | tf_op jit(solution)/shard_map/ppermute | solution.py:85
  156.8 6.7 %collective-permute-start.21 = (f32[2,136,128]{2,1,0:T(8,128)}, f32[2,136,128]{2,1,0:T(8,128)S(1)}, u32[]{:S(2)}, u32[]{:S(2)}) collective-permute-start(f32[2,136,128]{2,1,0:T(8,128)} %get-tuple-element.58), channel_id=1, source_target_pairs={{0,2},{1,3},{2,0},{3,1},{4,6},{5,7},{6,4},{7,5},{8,10},{9,11},{10,... | collective-permute-start | bytes 417800 | tf_op jit(solution)/shard_map/ppermute | solution.py:85
  159.4 7.7 %collective-permute-start.22 = (f32[2,136,128]{2,1,0:T(8,128)}, f32[2,136,128]{2,1,0:T(8,128)S(1)}, u32[]{:S(2)}, u32[]{:S(2)}) collective-permute-start(f32[2,136,128]{2,1,0:T(8,128)} %get-tuple-element.59), channel_id=1, source_target_pairs={{0,3},{1,0},{2,1},{3,2},{4,7},{5,4},{6,5},{7,6},{8,11},{9,8},{10,9... | collective-permute-start | bytes 417800 | tf_op jit(solution)/shard_map/ppermute | solution.py:85
  186.3 9.1 %collective-permute-start.30 = (f32[40,256]{1,0:T(8,128)S(1)}, f32[40,256]{1,0:T(8,128)S(1)}, u32[]{:S(2)}, u32[]{:S(2)}) collective-permute-start(f32[40,256]{1,0:T(8,128)S(1)} %add.34), channel_id=1, source_target_pairs={{0,96},{1,97},{2,98},{3,99},{4,100},{5,101},{6,102},{7,103},{8,104... | collective-permute-start | bytes 122888 | tf_op jit(solution)/shard_map/ppermute | solution.py:85
  192.1 6.8 %collective-permute-start.29 = (f32[40,256]{1,0:T(8,128)S(1)}, f32[40,256]{1,0:T(8,128)S(1)}, u32[]{:S(2)}, u32[]{:S(2)}) collective-permute-start(f32[40,256]{1,0:T(8,128)S(1)} %add.34), channel_id=1, source_target_pairs={{0,64},{1,65},{2,66},{3,67},{4,68},{5,69},{6,70},{7,71},{8,72},{9,... | collective-permute-start | bytes 122888 | tf_op jit(solution)/shard_map/ppermute | solution.py:85
  193.1 6.0 %collective-permute-start.28 = (f32[40,256]{1,0:T(8,128)S(1)}, f32[40,256]{1,0:T(8,128)S(1)}, u32[]{:S(2)}, u32[]{:S(2)}) collective-permute-start(f32[40,256]{1,0:T(8,128)S(1)} %add.34), channel_id=1, source_target_pairs={{0,32},{1,33},{2,34},{3,35},{4,36},{5,37},{6,38},{7,39},{8,40},{9,... | collective-permute-start | bytes 122888 | tf_op jit(solution)/shard_map/ppermute | solution.py:85
  203.7 10.5 %collective-permute-start.34 = (f32[4,32,256]{2,1,0:T(8,128)S(1)}, f32[4,32,256]{2,1,0:T(8,128)S(1)}, u32[]{:S(2)}, u32[]{:S(2)}) collective-permute-start(f32[4,32,256]{2,1,0:T(8,128)S(1)} %pad_maximum_fusion.3), channel_id=1, source_target_pairs={{1,5},{6,2},{9,13},{14,10},{17,21},{22,18},{25,29},{30,26},{33,37}... | collective-permute-start | bytes 393224 | tf_op jit(solution)/shard_map/ppermute | solution.py:85
  214.2 12.0 %collective-permute-start.37 = (f32[4,32,256]{2,1,0:T(8,128)S(1)}, f32[4,32,256]{2,1,0:T(8,128)S(1)}, u32[]{:S(2)}, u32[]{:S(2)}) collective-permute-start(f32[4,32,256]{2,1,0:T(8,128)S(1)} %broadcast_select_fusion.refs_0_), channel_id=1, source_target_pairs={{1,25},{2,26},{5,29},{6,30},{9,1},{10,2},{13,5},{14,6},{17,9},{18,... | collective-permute-start | bytes 393224 | tf_op jit(solution)/shard_map/ppermute | solution.py:85
  218.4 8.0 %collective-permute-start.36 = (f32[4,32,256]{2,1,0:T(8,128)S(1)}, f32[4,32,256]{2,1,0:T(8,128)S(1)}, u32[]{:S(2)}, u32[]{:S(2)}) collective-permute-start(f32[4,32,256]{2,1,0:T(8,128)S(1)} %broadcast_select_fusion.refs_0_), channel_id=1, source_target_pairs={{1,17},{2,18},{5,21},{6,22},{9,25},{10,26},{13,29},{14,30},{17,1},... | collective-permute-start | bytes 393224 | tf_op jit(solution)/shard_map/ppermute | solution.py:85
  220.4 9.5 %collective-permute-start.35 = (f32[4,32,256]{2,1,0:T(8,128)S(1)}, f32[4,32,256]{2,1,0:T(8,128)S(1)}, u32[]{:S(2)}, u32[]{:S(2)}) collective-permute-start(f32[4,32,256]{2,1,0:T(8,128)S(1)} %broadcast_select_fusion.refs_0_), channel_id=1, source_target_pairs={{1,9},{2,10},{5,13},{6,14},{9,17},{10,18},{13,21},{14,22},{17,25},... | collective-permute-start | bytes 393224 | tf_op jit(solution)/shard_map/ppermute | solution.py:85
  (52 other events, 378.3 us)

commit v2 on v1

--- a/solution.py
+++ b/solution.py
@@ -175,14 +175,14 @@
     specs = []
     for at in range(len(operands)):
         space = pltpu.SMEM if at in in_smem else pltpu.VMEM
-        specs.append(pl.BlockSpec(memory_space=pl.ANY if at in apart else space))
+        specs.append(pl.BlockSpec(memory_space=pltpu.HBM if at in apart else space))
     return pl.pallas_call(
         kernel,
         out_shape=[jax.ShapeDtypeStruct(shape, F32) for shape in outs],
         in_specs=specs,
         out_specs=[pl.BlockSpec(memory_space=pltpu.VMEM) for _ in outs],
         scratch_shapes=list(scratch),
-        compiler_params=pltpu.CompilerParams(vmem_limit_bytes=60 * 1024 * 1024),
+        compiler_params=pltpu.CompilerParams(vmem_limit_bytes=20 * 1024 * 1024),
     )(*operands)
 
 
@@ -217,18 +217,7 @@
     return ref[0], ref[1], ref[2], ref[3]
 
 
-def phase_kernel(idx, ids, got, mask, offsets, own, one, two, three, slab, grabbed, phases, sems):
-    owner = idx[2] == 1
-    sample = jnp.where(owner, ids[0], got[0])
-    fetch = Fetch(
-        sems,
-        (offsets.at[sample, pl.ds(256, 512), :], grabbed),
-        (mask.at[pl.ds(256, 512), :], slab),
-    )
-    ratio = ratio_of(jnp.where(owner, ids[1], got[1]))[0:1, 0:1]
-    fetch.wait(0)
-    fetch.wait(1)
-    phases[...] = ratio * (slab[...] + 0.1 * grabbed[...].astype(F32))
+def phase_kernel(idx, phases, own, one, two, three):
     s = idx[0]
     left = s == 1
     own[...] = phases[pl.ds(aligned(s, 128), 128), :]
@@ -251,11 +240,13 @@
     edge[...] = jnp.where(c == 0, strip[248:256, :], strip[0:8, :])
 
 
-def pupil_kernel(idx, a0, a1, a2, a3, m_far, o0, o1, o2, o3, pupil, grid, m, sems):
+def pupil_kernel(idx, *refs):
+    m_far, o0, o1, o2, o3, pupil, grid, m, sems = refs[8:]
     fetch = Fetch(sems, (m_far, m))
     s = idx[0]
     c = idx[1]
-    a0, a1, a2, a3 = a0[...], a1[...], a2[...], a3[...]
+    owner = idx[2] == 1
+    a0, a1, a2, a3 = [jnp.where(owner, refs[at][...], refs[at + 4][...]) for at in range(4)]
     left = jnp.where(s == 0, a1, jnp.where(s == 1, a0, jnp.where(s == 2, a2, a3)))
     right = jnp.where(s == 0, a3, jnp.where(s == 1, a2, jnp.where(s == 2, a0, a1)))
     phase = jnp.concatenate([left, right], 1)
@@ -279,10 +270,11 @@
         out[...] = grid[:, :, pl.ds(aligned(to, 128), 128)]
 
 
-def eight_rows(out, grid):
+def eight_rows(out, grid, at):
     for c in range(2):
         for s in range(4):
-            out[4 * c + s] = grid[:, 128 * s + 64 * c : 128 * s + 64 * c + 64, :]
+            row = 128 * s + 64 * c
+            out[4 * c + s, at : at + 2] = grid[:, row : row + 64, :]
 
 
 def eight_columns(out, grid):
@@ -290,12 +282,14 @@
         out[at] = grid[:, :, 128 * at : 128 * at + 128]
 
 
-def optics_kernel(scale, idx, b0, b1, b2, b3, f_far, tw, far, out, grid, f, sems):
-    fetch = Fetch(sems, (f_far, f))
+def optics_kernel(scale, idx, b0, b1, b2, b3, *refs):
+    i0, i1, i2, i3, f_far, tw_far, w_far, far, out, grid, image, f, tw, w, sems = refs
+    fetch = Fetch(sems, (tw_far, tw), (f_far, f), (w_far, w))
     for d, block in enumerate((b0, b1, b2, b3)):
         grid[:, pl.ds(aligned(from_of(idx, d)[0], 128), 128), :] = block[...]
     low = (grid[0, :256, :], grid[1, :256, :])
     high = (grid[0, 256:, :], grid[1, 256:, :])
+    fetch.wait(0)
     twists = [(tw[:, r : r + 1], tw[:, 4 + r : 5 + r]) for r in range(4)]
     res, ims = [], []
     for r in range(4):
@@ -305,7 +299,7 @@
             re, im = times(re, im, twists[r][0], -twists[r][1])
         res.append(re)
         ims.append(im)
-    fetch.wait(0)
+    fetch.wait(1)
     mats = mats_of(f)
     far_re, far_im = dft_left(
         jnp.concatenate(res, 1), jnp.concatenate(ims, 1), mats, -1.0
@@ -334,18 +328,14 @@
     grid[1, :256, :] = jnp.where(row == 0, nyquist, first[1])
     grid[0, 256:, :] = second[0]
     grid[1, 256:, :] = second[1]
-    eight_rows(out, grid)
-
-
-def scene_columns_kernel(idx, b0, b1, b2, b3, w_far, out, image, grid, w, sems):
-    fetch = Fetch(sems, (w_far, w))
-    for d, block in enumerate((b0, b1, b2, b3)):
+    eight_rows(out, grid, 0)
+    for d, block in enumerate((i0, i1, i2, i3)):
         image[pl.ds(aligned(from_of(idx, d)[0], 256), 256), :] = block[...]
-    fetch.wait(0)
+    fetch.wait(2)
     spectrum = by_left(w[0], w[1], image[...])
     grid[0] = spectrum[:512]
     grid[1] = spectrum[512:]
-    eight_rows(out, grid)
+    eight_rows(out, grid, 2)
 
 
 def unpack_rows(idx, re, im, tail):
@@ -364,9 +354,9 @@
     return re[:64], jnp.where((rows == 0) & first, re[64:65, :], im[:64])
 
 
-def row_transform(idx, blocks, fetch, f, tw, grid):
+def row_transform(idx, blocks, first, mats, tw, grid):
     for at in range(8):
-        grid[:, :, 128 * at : 128 * at + 128] = blocks[at]
+        grid[:, :, 128 * at : 128 * at + 128] = blocks[at, first : first + 2]
     re, im = unpack_rows(idx, grid[0], grid[1], 8)
     quarters = [(re[:, q * 256 : q * 256 + 256], im[:, q * 256 : q * 256 + 256]) for q in range(4)]
     sum02 = [quarters[0][p] + quarters[2][p] for p in range(2)]
@@ -382,8 +372,6 @@
     ]
     for r in range(1, 4):
         parts[r] = times(parts[r][0], parts[r][1], tw[r : r + 1, :], -tw[4 + r : 5 + r, :])
-    fetch.wait(0)
-    mats = mats_of(f)
     return dft_right(
         jnp.concatenate([p[0] for p in parts], 0),
         jnp.concatenate([p[1] for p in parts], 0),
@@ -392,16 +380,16 @@
     )
 
 
-def scene_rows_kernel(idx, blocks, f_far, tw, out, grid, f, sems):
-    re, im = row_transform(idx, blocks, Fetch(sems, (f_far, f)), f, tw, grid)
-    out[0] = re
-    out[1] = im
-
-
-def blur_kernel(idx, blocks, f_far, tw, spectrum, out, grid, f, sems):
-    re, im = row_transform(idx, blocks, Fetch(sems, (f_far, f)), f, tw, grid)
+def blur_kernel(idx, blocks, f_far, tw_far, out, spectrum, grid, f, tw, sems):
+    fetch = Fetch(sems, (tw_far, tw), (f_far, f))
+    fetch.wait(0)
+    fetch.wait(1)
     mats = mats_of(f)
-    re, im = times(re, im, spectrum[0], spectrum[1])
+    scene_re, scene_im = row_transform(idx, blocks, 2, mats, tw, grid)
+    spectrum[0] = scene_re
+    spectrum[1] = scene_im
+    re, im = row_transform(idx, blocks, 0, mats, tw, grid)
+    re, im = times(re, im, scene_re, scene_im)
     mats = tuple(m[:, :128] for m in mats)
     re, im = dft_right(re, im, mats, 1.0)
     sum_re, sum_im = re[:72], im[:72]
@@ -437,10 +425,8 @@
 
 def net_kernel(pixel_count, idx, w1, b1, w2, *refs):
     blocks = refs[:2]
-    v_far, strip, edge, g_out, sums_out = refs[2:7]
-    grid, win_taps, g_taps, hidden, sums, acc, v, sems = refs[7:]
-    slot = 2 * idx[0] + idx[1]
-    fetch = Fetch(sems, (v_far.at[:, pl.ds(aligned(slot, 128), ROWS), :], v))
+    v, strip, edge, g_out, sums_out = refs[2:7]
+    grid, win_taps, g_taps, hidden, sums, acc = refs[7:]
     for d, e in relations:
         s, c = from_of(idx, d, e)
         at = 2 * s + c
@@ -455,7 +441,6 @@
     lanes = lax.broadcasted_iota(jnp.int32, (ROWS, 128), 1)
     row_global = rows + (2 * idx[0] + idx[1]) * 128 - 8
     inside = (row_global >= 0) & (row_global < N)
-    fetch.wait(0)
     window = jnp.where(inside, by_left(v[0], v[1], grid[...]), 0.0)
     for e in (-1, 0, 1):
         side = moved_lanes(window, e, lanes)
@@ -540,27 +525,20 @@
 
 def otf_grad_kernel(idx, *refs):
     blocks = refs[:2]
-    w_far, f_far, tw, spectrum, out, window, grid, w, f, sems = refs[2:]
-    slot = 2 * idx[0] + idx[1]
-    fetch = Fetch(
-        sems,
-        (w_far.at[:, pl.ds(aligned(slot, 64), 64), :], w.at[:, pl.ds(0, 64), :]),
-        (w_far.at[:, pl.ds(aligned(slot + 8, 64), 64), :], w.at[:, pl.ds(64, 64), :]),
-        (f_far, f),
-    )
+    w, f_far, tw_far, spectrum, out, window, grid, f, tw, sems = refs[2:]
+    fetch = Fetch(sems, (f_far, f), (tw_far, tw))
     for d, e in relations:
         s, c = from_of(idx, d, e)
         window[pl.ds(aligned(2 * s + c, 128), 128), :] = blocks[e][d]
+    packed = by_left(w[0], w[1], window[...])
     fetch.wait(0)
     fetch.wait(1)
-    packed = by_left(w[0], w[1], window[...])
     re, im = unpack_rows(idx, packed[:64], packed[64:], 8)
     res, ims = [re], [im]
     for r in range(1, 4):
         a, b = times(re, im, tw[8 + r : 9 + r, :128], -tw[12 + r : 13 + r, :128])
         res.append(a)
         ims.append(b)
-    fetch.wait(2)
     mats = mats_of(f)
     top = tuple(m[:128, :] for m in mats)
     re, im = dft_right(jnp.concatenate(res, 0), jnp.concatenate(ims, 0), top, -1.0)
@@ -584,8 +562,8 @@
     eight_columns(out, grid)
 
 
-def psf_grad_kernel(idx, blocks, far_far, f_far, tw, small, o0, o1, o2, o3, grid, far, f, sems):
-    fetch = Fetch(sems, (f_far, f), (far_far, far))
+def psf_grad_kernel(idx, blocks, far, f_far, tw_far, small, o0, o1, o2, o3, grid, f, tw, sems):
+    fetch = Fetch(sems, (f_far, f), (tw_far, tw))
     for c in range(2):
         for s in range(4):
             grid[:, 128 * s + 64 * c : 128 * s + 64 * c + 64, :] = blocks[4 * c + s]
@@ -596,6 +574,7 @@
     low_re = jnp.where(zero_row, 0.5 * low_re, low_re)
     low_im = jnp.where(zero_row, 0.0, low_im)
     high = (grid[0, 256:, :], grid[1, 256:, :])
+    fetch.wait(1)
     twists = [(tw[:, r : r + 1], tw[:, 4 + r : 5 + r]) for r in range(4)]
     res, ims = [], []
     for r in range(4):
@@ -612,7 +591,6 @@
         by_left(mats[0], mats[1], jnp.concatenate(res, 1))
         - by_left(mats[2], mats[3], jnp.concatenate(ims, 1))
     )
-    fetch.wait(1)
     re, im = dft_left(g_psf * far[0], g_psf * far[1], mats, 1.0)
     first, second = None, None
     for r in range(4):
@@ -632,8 +610,8 @@
 
 
 def mask_grad_kernel(scale, idx, ids, got, *refs):
-    b0, b1, b2, b3, m_far, pupil_far, keep, send, grid, whole, m, pupil, sems = refs
-    fetch = Fetch(sems, (m_far, m), (pupil_far, pupil))
+    b0, b1, b2, b3, m_far, pupil, keep, send, grid, whole, m, sems = refs
+    fetch = Fetch(sems, (m_far, m))
     small = None
     for d, block in enumerate((b0, b1, b2, b3)):
         grid[:, :, pl.ds(aligned(from_of(idx, d)[0], 128), 128)] = block[:, 0:128, :]
@@ -641,7 +619,6 @@
         small = part if small is None else small + part
     fetch.wait(0)
     re, im = dft_right(grid[0], grid[1], mats_of(m), 1.0)
-    fetch.wait(1)
     cols = lax.broadcasted_iota(jnp.int32, (128, 512), 1)
     factor = ratio_of(jnp.where(idx[2] == 1, ids[1], got[1]))[0:1, 0:1] * scale
     factor = jnp.where((cols & idx[1]) == 1, -factor, factor)
@@ -664,21 +641,17 @@
         out[piece : piece + 8, :] = whole[128:136, :]
 
 
-def home_kernel(ways, idx, *refs):
-    blocks = refs[:ways]
-    out = refs[ways]
+def home_kernel(ways, idx, near, far, out):
     piece = 128 // ways
+    at_home = idx[0] == 1 + idx[1]
     central = (idx[0] == 1) | (idx[0] == 2)
     out[0:256, :] = jnp.zeros((256, 256), F32)
     out[768:1024, :] = jnp.zeros((256, 256), F32)
-    for back in range(ways):
-        y = lax.rem(idx[3] + ways - back, ways)
-        for d in range(4):
-            s = from_of(idx, d)[0]
-            at = (2 + s) * ways + y
-            out[pl.ds(aligned(at, piece), piece), :] = jnp.where(
-                central, blocks[back][d], 0.0
-            )
+    for y in range(ways):
+        for s in range(4):
+            row = 256 + 128 * s + piece * y
+            block = jnp.where(at_home, near[4 * y + s], far[4 * y + s])
+            out[row : row + piece, :] = jnp.where(central, block, 0.0)
 
 
 def on_device(lay, phase_mask, height_offsets, sample_ids, wave_ids, scene, w1, b1, w2):
@@ -709,31 +682,31 @@
 
     ids = jnp.concatenate([sample_ids, wave_ids])
     got = lay.move(ids, swap)
+    grabbed = lax.dynamic_slice(height_offsets, (ids[0], 256, 0), (1, 512, 256))[0]
+    ratio = 550.0 / (400.0 + 10.0 * ids[1].astype(F32))
+    phases = ratio * (phase_mask[256:768] + 0.1 * grabbed.astype(F32))
 
     mine, *sent = call(
         phase_kernel,
-        (idx, ids, got, phase_mask, height_offsets),
-        (0, 1, 2),
+        (idx, phases),
+        (0,),
         [(128, 256)] * 4,
-        [
-            pltpu.VMEM((512, 256), F32),
-            pltpu.VMEM((512, 256), jnp.int32),
-            pltpu.VMEM((512, 256), F32),
-            fetch_sems(2),
-        ],
-        (3, 4),
     )
     tables = ({1: 0, 2: 3}, {1: 2, 2: 1}, {1: 3, 2: 0})
     pieces = [mine] + [
         lay.move(
             block,
-            lambda g, zh, y, c, s, to=to: (g, zh, y, c, to[s]) if s in to else None,
+            lambda g, zh, y, c, s, to=to: (
+                (g, zh, y, c, to[s]) if s in to and c == g else None
+            ),
         )
         for block, to in zip(sent, tables)
     ]
-
-    scene, mine = lax.optimization_barrier((scene, mine))
-    pieces[0] = mine
+    pieces += [
+        lay.move(block, lambda g, zh, y, c, s: (g, zh, y, 1 - c, s) if c == g else None)
+        for block in pieces
+    ]
+
     other = lay.move(
         jnp.concatenate(
             [lax.dynamic_slice_in_dim(scene[0], 512 * (1 - c), 512, 1), scene[0, :, 256:384]], 1
@@ -749,59 +722,50 @@
     columns = along_sp(columns)
     edge = lay.move(edge, lambda g, zh, y, c, s: (g, zh, y, c, s + 1 - 2 * c))
 
+    unpack = lax.dynamic_slice_in_dim(jnp.asarray(con["unpack"]), 128 * (2 * s + c), ROWS, 1)
+    pack = jnp.asarray(con["pack"]).reshape(4, 512, N)
+    pack_rows = lax.dynamic_slice_in_dim(pack, 64 * (2 * s + c), 64, 1).reshape(2, 128, N)
     *field, pupil = call(
         pupil_kernel,
         (idx, *pieces, con["m"]),
         (0,),
         [(2, 128, 128)] * 4 + [(2, 128, 512)],
         [pltpu.VMEM((2, 128, 512), F32), bf16_buffer(4, 512, 512), fetch_sems(1)],
-        (5,),
+        (9,),
     )
     field = along_sp(field)
-    (scene_part,) = call(
-        scene_columns_kernel,
-        (idx, *columns, con["pack"]),
+    far, parts = call(
+        functools.partial(optics_kernel, scale_psf),
+        (idx, *field, *columns, con["f"], con["tw_col"], con["pack"]),
         (0,),
-        [(8, 2, 64, 128)],
+        [(2, 256, 512), (8, 4, 64, 128)],
         [
+            pltpu.VMEM((2, 512, 128), F32),
             pltpu.VMEM((N, 128), F32),
-            pltpu.VMEM((2, 512, 128), F32),
+            bf16_buffer(4, 256, 256),
+            pltpu.VMEM((256, 8), F32),
             bf16_buffer(2, N, N),
-            fetch_sems(1),
+            fetch_sems(3),
         ],
-        (5,),
-    )
-    scene_part = to_eight(scene_part)
-    far, otf_part = call(
-        functools.partial(optics_kernel, scale_psf),
-        (idx, *field, con["f"], con["tw_col"]),
+        (9, 10, 11),
+    )
+    half_window, spectrum = call(
+        blur_kernel,
+        (idx, to_eight(parts), con["f"], con["tw_row"]),
         (0,),
-        [(2, 256, 512), (8, 2, 64, 128)],
-        [pltpu.VMEM((2, 512, 128), F32), bf16_buffer(4, 256, 256), fetch_sems(1)],
-        (5,),
-    )
-    otf_part = to_eight(otf_part)
-    row_scratch = [pltpu.VMEM((2, 64, N), F32), bf16_buffer(4, 256, 256), fetch_sems(1)]
-    (spectrum,) = call(
-        scene_rows_kernel,
-        (idx, scene_part, con["f"], con["tw_row"]),
-        (0,),
-        [(2, 288, 256)],
-        row_scratch,
-        (2,),
-    )
-    (half_window,) = call(
-        blur_kernel,
-        (idx, otf_part, con["f"], con["tw_row"], spectrum),
-        (0,),
-        [(2, 64, 128)],
-        row_scratch,
-        (2,),
+        [(2, 288, 256), (2, 64, 128)][::-1],
+        [
+            pltpu.VMEM((2, 64, N), F32),
+            bf16_buffer(4, 256, 256),
+            pltpu.VMEM((16, 256), F32),
+            fetch_sems(2),
+        ],
+        (2, 3),
     )
     window_parts = gathered(half_window)
     g_window, sums = call(
         functools.partial(net_kernel, pixel_count),
-        (idx, w1, b1, w2, *window_parts, con["unpack"], strip, edge),
+        (idx, w1, b1, w2, *window_parts, unpack, strip, edge),
         (0, 1, 2, 3),
         [(128, 128), (32, 24, 128)],
         [
@@ -811,26 +775,23 @@
             pltpu.VMEM((32, ROWS, 128), F32),
             pltpu.VMEM((9, ROWS, 128), F32),
             pltpu.VMEM((32, 19, 8, 128), F32),
-            bf16_buffer(2, ROWS, N),
-            fetch_sems(1),
         ],
-        (6,),
     )
     small = jnp.pad(jnp.sum(sums, 2).reshape(6, 128), ((0, 2), (0, 0)))
     g_parts = gathered(g_window)
     (otf_grad,) = call(
         otf_grad_kernel,
-        (idx, *g_parts, con["pack"], con["f"], con["tw_row"], spectrum),
+        (idx, *g_parts, pack_rows, con["f"], con["tw_row"], spectrum),
         (0,),
         [(8, 2, 64, 128)],
         [
             pltpu.VMEM((N, 128), F32),
             pltpu.VMEM((2, 64, N), F32),
-            bf16_buffer(2, 128, N),
             bf16_buffer(4, 256, 256),
-            fetch_sems(3),
+            pltpu.VMEM((16, 256), F32),
+            fetch_sems(2),
         ],
-        (3, 4),
+        (4, 5),
     )
     otf_grad = to_eight(otf_grad)
     field_grad = along_sp(
@@ -841,11 +802,11 @@
             [(2, 136, 128)] * 4,
             [
                 pltpu.VMEM((2, 512, 128), F32),
-                pltpu.VMEM((2, 256, 512), F32),
                 bf16_buffer(4, 256, 256),
+                pltpu.VMEM((256, 8), F32),
                 fetch_sems(2),
             ],
-            (2, 3),
+            (3, 4),
         )
     )
     keep, send = call(
@@ -857,10 +818,9 @@
             pltpu.VMEM((2, 128, 512), F32),
             pltpu.VMEM((128, 512), F32),
             bf16_buffer(4, 512, 512),
-            pltpu.VMEM((2, 128, 512), F32),
-            fetch_sems(2),
+            fetch_sems(1),
         ],
-        (7, 8),
+        (7,),
     )
 
     piece = 128 // lay.y
@@ -882,28 +842,12 @@
         total = total + lay.move(part, lambda g, zh, y, c, s, d=d: (g, zh + d, y, c, s))
     small = total[piece:, :128].reshape(-1)
     total = total[:piece]
-    home = jnp.stack(
-        [total]
-        + [
-            lay.move(
-                total,
-                lambda g, zh, y, c, s, d=d: (
-                    (g, zh, y, c, 1 + c) if (s + d - 1 - c) % 4 == 0 else None
-                ),
-            )
-            for d in (1, 2, 3)
-        ]
-    )
-    at_home = s == 1 + c
-    crossed = lay.move(home, lambda g, zh, y, c, s: (g, zh, y, 1 - c, s) if s == 1 + c else None)
-    home = jnp.where(at_home, home, crossed)
-    near = [home] + [
-        lay.move(
-            home, lambda g, zh, y, c, s, d=d: (g, zh, y + d, c, s) if s in (1, 2) else None
-        )
-        for d in range(1, lay.y)
-    ]
-    (mask_grad,) = call(functools.partial(home_kernel, lay.y), (idx, *near), (0,), [(N, 256)])
+    ways = 4 * lay.y
+    near = lax.all_to_all(
+        jnp.broadcast_to(total, (ways, piece, 256)), ("y", "sp"), 0, 0, tiled=True
+    )
+    far = lay.move(near, lambda g, zh, y, c, s: (g, zh, y, 1 - c, s) if s == 1 + c else None)
+    (mask_grad,) = call(functools.partial(home_kernel, lay.y), (idx, near, far), (0,), [(N, 256)])
     table = small[:768].reshape(32, 24)
     return (
         mask_grad,

time: 235 us -> 194 us (0.83)
  blocking collectives: 0 us -> 33.5 us
  Pallas kernels: 63.7 us -> 35.4 us
  starting transfers between devices: 81.5 us -> 55.4 us
  waiting for transfers between devices: 67.7 us -> 44.5 us
    all_to_all x0 -> x2, blocking collectives: none -> 33.5 us  [the longest x1 19.9 us: to_eight(): return lax.all_to_all(blocks, ('core', 'sp'), 0, 0, tiled=True)]
    pallas_call x13 -> x11, Pallas kernels: 63.7 us -> 35.4 us  [call(): pl.pallas_call(kernel, out_shape=[jax.ShapeDtypeStruct(shape, F32) for sh...]
    ppermute x38 -> x36, waiting for transfers between devices: 55 us -> 37.2 us  [move(): return lax.ppermute(x, AXES, pairs)]
    ppermute x38 -> x36, starting transfers between devices: 64.8 us -> 51 us  [move(): return lax.ppermute(x, AXES, pairs)]
    all_to_all x3 -> x1, starting transfers between devices: 16.7 us -> 4.44 us  [to_eight(): return lax.all_to_all(blocks, ('core', 'sp'), 0, 0, tiled=True)]
    all_to_all x3 -> x1, waiting for transfers between devices: 12.7 us -> 7.3 us  [to_eight(): return lax.all_to_all(blocks, ('core', 'sp'), 0, 0, tiled=True)]
    unnamed x73 -> x43, local copies, waits for them, and re-layouts: 11 us -> 8.73 us
  transfers between devices with their start and end apart: 41 -> 37, of which waited for: 32 -> 23; matrix products, arithmetic and copies ran while one was open for 2% -> 4% of each run, Pallas kernels for 6% -> 2%
where the time goes in v2:
time: 194 us; the launch traced here: 191 us
  starting transfers between devices  55.4 us (29%)
  waiting for transfers between devices  44.5 us (23%)
  Pallas kernels  35.4 us (18%)
  blocking collectives  33.5 us (17%)
  local copies, waits for them, and re-layouts  14.6 us (8%)
  between operations  4.21 us (2%)
  other arithmetic  3.7 us (2%)
    ppermute x36, starting transfers between devices, move(): return lax.ppermute(x, AXES, pairs)  51 us
    ppermute x36, waiting for transfers between devices, move(): return lax.ppermute(x, AXES, pairs)  37.2 us
    pallas_call x11, Pallas kernels, call(): pl.pallas_call(kernel, out_shape=[jax.ShapeDtypeStruct(shape, F32) for sh...  35.4 us
    all_to_all x1, blocking collectives, to_eight(): return lax.all_to_all(blocks, ('core', 'sp'), 0, 0, tiled=True)  19.9 us
    all_to_all x1, blocking collectives, on_device(): lax.all_to_all(jnp.broadcast_to(total, (ways, piece, 256)), ('y', 'sp'),...  13.5 us
    unnamed x43, local copies, waits for them, and re-layouts  8.73 us
    all_to_all x1, waiting for transfers between devices, to_eight(): return lax.all_to_all(blocks, ('core', 'sp'), 0, 0, tiled=True)  7.3 us
    all_to_all x1, starting transfers between devices, to_eight(): return lax.all_to_all(blocks, ('core', 'sp'), 0, 0, tiled=True)  4.44 us
  transfers between devices with their start and end apart: 37, of which 23 were waited for; matrix products, arithmetic and copies ran while one was open for 4% of the time, Pallas kernels for 2%

profile of v2, /device:TPU:3, one launch (start us, length us, event | category | flops | bytes accessed | tf_op | source)
XLA Modules:
  0.0 191.3 jit_solution(6836300921091492158)
XLA Ops:
  15.1 2.7 %collective-permute-done.4.refs_4_ = f32[128,256]{1,0:T(8,128)S(1)} collective-permute-done((f32[128,256]{1,0:T(8,128)S(1)}, f32[128,256]{1,0:T(8,128)S(1)}, u32[]{:S(2)}, u32[]{:S(2)}) %collective-permute-start.4) | collective-permute-done | bytes 131104 | tf_op jit(solution)/shard_map/ppermute | solution.py:85
  26.5 2.5 %collective-permute-start.9 = (f32[2,128,128]{2,1,0:T(8,128)S(1)}, f32[2,128,128]{2,1,0:T(8,128)S(1)}, u32[]{:S(2)}, u32[]{:S(2)}) collective-permute-start(f32[2,128,128]{2,1,0:T(8,128)S(1)} %get-tuple-element.42), channel_id=1, source_target_pairs={{0,2},{1,3},{2,0},{3,1},{4,6},{5,7},{6,4},{7,5},{8,10},{9,11},{10,... | collective-permute-start | bytes 393224 | tf_op jit(solution)/shard_map/ppermute | solution.py:85
  32.9 3.9 %collective-permute-done.12.refs_1_ = f32[256,128]{1,0:T(8,128)S(1)} collective-permute-done((f32[256,128]{1,0:T(8,128)S(1)}, f32[256,128]{1,0:T(8,128)S(1)}, u32[]{:S(2)}, u32[]{:S(2)}) %collective-permute-start.12) | collective-permute-done | bytes 131104 | tf_op jit(solution)/shard_map/ppermute | solution.py:85
  36.8 2.7 %collective-permute-done.14.refs_3_ = f32[256,128]{1,0:T(8,128)S(1)} collective-permute-done((f32[256,128]{1,0:T(8,128)S(1)}, f32[256,128]{1,0:T(8,128)S(1)}, u32[]{:S(2)}, u32[]{:S(2)}) %collective-permute-start.14) | collective-permute-done | bytes 131104 | tf_op jit(solution)/shard_map/ppermute | solution.py:85
  39.5 5.0 %shard_map.176 = (f32[2,256,512]{2,1,0:T(8,128)S(1)}, f32[8,4,64,128]{3,2,1,0:T(8,128)S(1)}) custom-call(s32[4]{0:T(128)S(1)} %pad_add_fusion.idx, f32[2,128,128]{2,1,0:T(8,128)S(1)} %get-tuple-element.40.b0, f32[2,128,128]{2,1,0:T(8,128)S(1)} %collective-permute-done.8.b1, f32[2,128,128]{2,1,0:T(8,128)S(1)} %collective-permute-done.9.b2, ...), custom_call_target="tpu_custom_call" | custom-call | tf_op jit(solution)/shard_map/pallas_call | solution.py:179
  44.5 19.9 %all_to_all.15.blocks = f32[8,4,64,128]{3,2,1,0:T(8,128)S(1)} all-to-all(f32[8,4,64,128]{3,2,1,0:T(8,128)S(1)} %get-tuple-element.48), channel_id=1, replica_groups=mesh['grp'=2,'zh'=4,'y'=4,'core'=2,'sp'=4] {'core','sp'}, dimensions={0} | all-to-all | bytes 2097152 | tf_op jit(solution)/shard_map/all_to_all | solution.py:677
  64.5 3.2 %shard_map.177 = (f32[2,64,128]{2,1,0:T(8,128)S(1)}, f32[2,288,256]{2,1,0:T(8,128)S(1)}) custom-call(s32[4]{0:T(128)S(1)} %pad_add_fusion.idx, f32[8,4,64,128]{3,2,1,0:T(8,128)S(1)} %all_to_all.15.blocks, bf16[4,256,256]{2,1,0:T(8,128)(2,1)S(1)} %copy-done, f32[16,256]{1,0:T(8,128)S(1)} %copy-done.16), custom_call_target="tpu_custom_call" | custom-call | tf_op jit(solution)/shard_map/pallas_call | solution.py:179
  68.5 2.7 %collective-permute-start.16 = (f32[2,64,128]{2,1,0:T(8,128)S(1)}, f32[2,64,128]{2,1,0:T(8,128)S(1)}, u32[]{:S(2)}, u32[]{:S(2)}) collective-permute-start(f32[2,64,128]{2,1,0:T(8,128)S(1)} %get-tuple-element.49), channel_id=1, source_target_pairs={{0,2},{1,3},{2,0},{3,1},{4,6},{5,7},{6,4},{7,5},{8,10},{9,11},{10,... | collective-permute-start | bytes 196616 | tf_op jit(solution)/shard_map/ppermute | solution.py:85
  79.9 13.6 %shard_map.178 = (f32[128,128]{1,0:T(8,128)S(1)}, f32[32,24,128]{2,1,0:T(8,128)S(1)}) custom-call(s32[4]{0:T(128)S(1)} %pad_add_fusion.idx, f32[32,9]{1,0:T(8,128)S(1)} %copy.26.w1, f32[32]{0:T(128)S(1)} %copy-done.18, f32[9,32]{1,0:T(8,128)S(1)} %copy-done.17, f32[4,2,64,128]{3,2,1,0:T(8,128)S(1)} %pad_maximum_fusion.1.refs_0_, ...), custom_call_target="tpu_custom_call" | custom-call | tf_op jit(solution)/shard_map/pallas_call | solution.py:179
  95.4 2.5 %collective-permute-start.21 = (f32[128,128]{1,0:T(8,128)S(1)}, f32[128,128]{1,0:T(8,128)S(1)}, u32[]{:S(2)}, u32[]{:S(2)}) collective-permute-start(f32[128,128]{1,0:T(8,128)S(1)} %get-tuple-element.52), channel_id=1, source_target_pairs={{0,2},{1,3},{2,0},{3,1},{4,6},{5,7},{6,4},{7,5},{8,10},{9,11},{10,... | collective-permute-start | bytes 196616 | tf_op jit(solution)/shard_map/ppermute | solution.py:85
  101.8 2.7 %collective-permute-start.23 = (f32[4,128,128]{2,1,0:T(8,128)S(1)}, f32[4,128,128]{2,1,0:T(8,128)S(1)}, u32[]{:S(2)}, u32[]{:S(2)}) collective-permute-start(f32[4,128,128]{2,1,0:T(8,128)S(1)} %pad_maximum_fusion.2.refs_0_), channel_id=1, source_target_pairs={{0,4},{1,5},{2,6},{3,7},{4,0},{5,1},{6,2},{7,3},{8,12},{9,13},{10,... | collective-permute-start | bytes 786440 | tf_op jit(solution)/shard_map/ppermute | solution.py:85
  106.7 3.2 %shard_map.179 = f32[8,2,64,128]{3,2,1,0:T(8,128)S(1)} custom-call(s32[4]{0:T(128)S(1)} %pad_add_fusion.idx, f32[4,128,128]{2,1,0:T(8,128)S(1)} %pad_maximum_fusion.2.refs_0_, f32[4,128,128]{2,1,0:T(8,128)S(1)} %collective-permute-done.23.refs_1_, bf16[2,128,1024]{2,1,0:T(8,128)(2,1)S(1)} %bitcast.29, bf16[4,256,256]{2,1,0:T(8,128)(2,1)S(1)} %copy-done, ...), custom_call_target="tpu_custom_call" | custom-call | tf_op jit(solution)/shard_map/pallas_call | solution.py:179
  110.8 4.4 %all-to-all-start.1 = ((f32[8,2,64,128]{3,2,1,0:T(8,128)}), f32[8,2,64,128]{3,2,1,0:T(8,128)S(1)}, u32[]{:S(2)}, u32[]{:S(2)}) async-start(f32[8,2,64,128]{3,2,1,0:T(8,128)} %copy-done.4), calls=%async_computation.1 | async-start | bytes 1048576 | tf_op jit(solution)/shard_map/all_to_all | solution.py:677
  116.5 7.3 %all-to-all-done.1.blocks = f32[8,2,64,128]{3,2,1,0:T(8,128)S(1)} async-done(((f32[8,2,64,128]{3,2,1,0:T(8,128)}), f32[8,2,64,128]{3,2,1,0:T(8,128)S(1)}, u32[]{:S(2)}, u32[]{:S(2)}) %all-to-all-start.1) | async-done | bytes 524320 | tf_op jit(solution)/shard_map/all_to_all | solution.py:677
  125.0 3.0 %shard_map.180 = (f32[2,136,128]{2,1,0:T(8,128)S(1)}, f32[2,136,128]{2,1,0:T(8,128)S(1)}, f32[2,136,128]{2,1,0:T(8,128)S(1)}, f32[2,136,128]{2,1,0:T(8,128)S(1)}) custom-call(s32[4]{0:T(128)S(1)} %pad_add_fusion.idx, f32[8,2,64,128]{3,2,1,0:T(8,128)S(1)} %all-to-all-done.1.blocks, f32[2,256,512]{2,1,0:T(8,128)S(1)} %copy-done.6, ...), custom_call_target="tpu_custom_call" | custom-call | tf_op jit(solution)/shard_map/pallas_call | solution.py:179
  128.1 2.7 %collective-permute-start.25 = (f32[2,136,128]{2,1,0:T(8,128)S(1)}, f32[2,136,128]{2,1,0:T(8,128)S(1)}, u32[]{:S(2)}, u32[]{:S(2)}) collective-permute-start(f32[2,136,128]{2,1,0:T(8,128)S(1)} %get-tuple-element.58), channel_id=1, source_target_pairs={{0,2},{1,3},{2,0},{3,1},{4,6},{5,7},{6,4},{7,5},{8,10},{9,11},{10,... | collective-permute-start | bytes 417800 | tf_op jit(solution)/shard_map/ppermute | solution.py:85
  134.6 3.6 %collective-permute-done.26.refs_3_ = f32[2,136,128]{2,1,0:T(8,128)S(1)} collective-permute-done((f32[2,136,128]{2,1,0:T(8,128)S(1)}, f32[2,136,128]{2,1,0:T(8,128)S(1)}, u32[]{:S(2)}, u32[]{:S(2)}) %collective-permute-start.26) | collective-permute-done | bytes 139296 | tf_op jit(solution)/shard_map/ppermute | solution.py:85
  144.7 2.6 %collective-permute-start.29 = (f32[40,256]{1,0:T(8,128)S(1)}, f32[40,256]{1,0:T(8,128)S(1)}, u32[]{:S(2)}, u32[]{:S(2)}) collective-permute-start(f32[40,256]{1,0:T(8,128)S(1)} %get-tuple-element.65), channel_id=1, source_target_pairs={{0,16},{1,17},{2,18},{3,19},{4,20},{5,21},{6,22},{7,23},{8,24},{9,... | collective-permute-start | bytes 122888 | tf_op jit(solution)/shard_map/ppermute | solution.py:85
  150.9 2.5 %collective-permute-done.31 = f32[40,256]{1,0:T(8,128)S(1)} collective-permute-done((f32[40,256]{1,0:T(8,128)S(1)}, f32[40,256]{1,0:T(8,128)S(1)}, u32[]{:S(2)}, u32[]{:S(2)}) %collective-permute-start.31) | collective-permute-done | bytes 40992 | tf_op jit(solution)/shard_map/ppermute | solution.py:85
  153.4 3.0 %collective-permute-start.32 = (f32[40,256]{1,0:T(8,128)S(1)}, f32[40,256]{1,0:T(8,128)S(1)}, u32[]{:S(2)}, u32[]{:S(2)}) collective-permute-start(f32[40,256]{1,0:T(8,128)S(1)} %add.51), channel_id=1, source_target_pairs={{0,32},{1,33},{2,34},{3,35},{4,36},{5,37},{6,38},{7,39},{8,40},{9,... | collective-permute-start | bytes 122888 | tf_op jit(solution)/shard_map/ppermute | solution.py:85
  156.3 5.1 %collective-permute-start.33 = (f32[40,256]{1,0:T(8,128)S(1)}, f32[40,256]{1,0:T(8,128)S(1)}, u32[]{:S(2)}, u32[]{:S(2)}) collective-permute-start(f32[40,256]{1,0:T(8,128)S(1)} %add.51), channel_id=1, source_target_pairs={{0,64},{1,65},{2,66},{3,67},{4,68},{5,69},{6,70},{7,71},{8,72},{9,... | collective-permute-start | bytes 122888 | tf_op jit(solution)/shard_map/ppermute | solution.py:85
  161.5 2.4 %collective-permute-start.34 = (f32[40,256]{1,0:T(8,128)S(1)}, f32[40,256]{1,0:T(8,128)S(1)}, u32[]{:S(2)}, u32[]{:S(2)}) collective-permute-start(f32[40,256]{1,0:T(8,128)S(1)} %add.51), channel_id=1, source_target_pairs={{0,96},{1,97},{2,98},{3,99},{4,100},{5,101},{6,102},{7,103},{8,104... | collective-permute-start | bytes 122888 | tf_op jit(solution)/shard_map/ppermute | solution.py:85
  166.2 13.5 %all_to_all.16.near = f32[16,32,256]{2,1,0:T(8,128)S(1)} all-to-all(f32[16,32,256]{2,1,0:T(8,128)S(1)} %broadcast_in_dim.3), channel_id=1, replica_groups=mesh['grp'=2,'zh'=4,'y'=4,'core'=2,'sp'=4] {'y','sp'}, dimensions={0} | all-to-all | bytes 1048576 | tf_op jit(solution)/shard_map/all_to_all | solution.py:846
  184.5 4.1 %collective-permute-done.35.far = f32[16,32,256]{2,1,0:T(8,128)S(1)} collective-permute-done((f32[16,32,256]{2,1,0:T(8,128)S(1)}, f32[16,32,256]{2,1,0:T(8,128)S(1)}, u32[]{:S(2)}, u32[]{:S(2)}) %collective-permute-start.35) | collective-permute-done | bytes 524320 | tf_op jit(solution)/shard_map/ppermute | solution.py:85
  (129 shorter events, 68.2 us)
Async XLA Ops:
  3.7 25.3 %collective-permute-start.11 = (f32[256,640]{1,0:T(8,128)}, f32[256,640]{1,0:T(8,128)S(1)}, u32[]{:S(2)}, u32[]{:S(2)}) collective-permute-start(f32[256,640]{1,0:T(8,128)} %pad_maximum_fusion), channel_id=1, source_target_pairs={{0,4},{1,5},{2,6},{3,7},{4,0},{5,1},{6,2},{7,3},{8,12},{9,13},{10,... | collective-permute-start | bytes 1966088 | tf_op jit(solution)/shard_map/ppermute | solution.py:85
  9.2 4.6 %collective-permute-start.3 = (f32[128,256]{1,0:T(8,128)S(1)}, f32[128,256]{1,0:T(8,128)S(1)}, u32[]{:S(2)}, u32[]{:S(2)}) collective-permute-start(f32[128,256]{1,0:T(8,128)S(1)} %get-tuple-element.39), channel_id=1, source_target_pairs={{1,3},{2,0},{9,11},{10,8},{17,19},{18,16},{25,27},{26,24},{33,35},... | collective-permute-start | bytes 393224 | tf_op jit(solution)/shard_map/ppermute | solution.py:85
  9.9 7.9 %collective-permute-start.4 = (f32[128,256]{1,0:T(8,128)S(1)}, f32[128,256]{1,0:T(8,128)S(1)}, u32[]{:S(2)}, u32[]{:S(2)}) collective-permute-start(f32[128,256]{1,0:T(8,128)S(1)} %get-tuple-element.36.refs_0_), channel_id=1, source_target_pairs={{0,4},{1,5},{2,6},{3,7},{8,12},{9,13},{10,14},{11,15},{16,20},{17,... | collective-permute-start | bytes 393224 | tf_op jit(solution)/shard_map/ppermute | solution.py:85
  11.2 7.9 %collective-permute-start.5 = (f32[128,256]{1,0:T(8,128)S(1)}, f32[128,256]{1,0:T(8,128)S(1)}, u32[]{:S(2)}, u32[]{:S(2)}) collective-permute-start(f32[128,256]{1,0:T(8,128)S(1)} %collective-permute-done.1.refs_1_), channel_id=1, source_target_pairs={{0,4},{1,5},{2,6},{3,7},{8,12},{9,13},{10,14},{11,15},{16,20},{17,... | collective-permute-start | bytes 393224 | tf_op jit(solution)/shard_map/ppermute | solution.py:85
  12.5 8.5 %collective-permute-start.6 = (f32[128,256]{1,0:T(8,128)S(1)}, f32[128,256]{1,0:T(8,128)S(1)}, u32[]{:S(2)}, u32[]{:S(2)}) collective-permute-start(f32[128,256]{1,0:T(8,128)S(1)} %collective-permute-done.2.refs_2_), channel_id=1, source_target_pairs={{0,4},{1,5},{2,6},{3,7},{8,12},{9,13},{10,14},{11,15},{16,20},{17,... | collective-permute-start | bytes 393224 | tf_op jit(solution)/shard_map/ppermute | solution.py:85
  13.8 8.5 %collective-permute-start.7 = (f32[128,256]{1,0:T(8,128)S(1)}, f32[128,256]{1,0:T(8,128)S(1)}, u32[]{:S(2)}, u32[]{:S(2)}) collective-permute-start(f32[128,256]{1,0:T(8,128)S(1)} %collective-permute-done.3.refs_3_), channel_id=1, source_target_pairs={{0,4},{1,5},{2,6},{3,7},{8,12},{9,13},{10,14},{11,15},{16,20},{17,... | collective-permute-start | bytes 393224 | tf_op jit(solution)/shard_map/ppermute | solution.py:85
  24.6 7.2 %collective-permute-start.10 = (f32[2,128,128]{2,1,0:T(8,128)S(1)}, f32[2,128,128]{2,1,0:T(8,128)S(1)}, u32[]{:S(2)}, u32[]{:S(2)}) collective-permute-start(f32[2,128,128]{2,1,0:T(8,128)S(1)} %get-tuple-element.43), channel_id=1, source_target_pairs={{0,3},{1,0},{2,1},{3,2},{4,7},{5,4},{6,5},{7,6},{8,11},{9,8},{10,9... | collective-permute-start | bytes 393224 | tf_op jit(solution)/shard_map/ppermute | solution.py:85
  26.5 6.4 %collective-permute-start.8 = (f32[2,128,128]{2,1,0:T(8,128)S(1)}, f32[2,128,128]{2,1,0:T(8,128)S(1)}, u32[]{:S(2)}, u32[]{:S(2)}) collective-permute-start(f32[2,128,128]{2,1,0:T(8,128)S(1)} %get-tuple-element.41), channel_id=1, source_target_pairs={{0,1},{1,2},{2,3},{3,0},{4,5},{5,6},{6,7},{7,4},{8,9},{9,10},{10,1... | collective-permute-start | bytes 393224 | tf_op jit(solution)/shard_map/ppermute | solution.py:85
  26.5 6.4 %collective-permute-start.9 = (f32[2,128,128]{2,1,0:T(8,128)S(1)}, f32[2,128,128]{2,1,0:T(8,128)S(1)}, u32[]{:S(2)}, u32[]{:S(2)}) collective-permute-start(f32[2,128,128]{2,1,0:T(8,128)S(1)} %get-tuple-element.42), channel_id=1, source_target_pairs={{0,2},{1,3},{2,0},{3,1},{4,6},{5,7},{6,4},{7,5},{8,10},{9,11},{10,... | collective-permute-start | bytes 393224 | tf_op jit(solution)/shard_map/ppermute | solution.py:85
  30.3 6.4 %collective-permute-start.12 = (f32[256,128]{1,0:T(8,128)S(1)}, f32[256,128]{1,0:T(8,128)S(1)}, u32[]{:S(2)}, u32[]{:S(2)}) collective-permute-start(f32[256,128]{1,0:T(8,128)S(1)} %get-tuple-element.45), channel_id=1, source_target_pairs={{0,1},{1,2},{2,3},{3,0},{4,5},{5,6},{6,7},{7,4},{8,9},{9,10},{10,1... | collective-permute-start | bytes 393224 | tf_op jit(solution)/shard_map/ppermute | solution.py:85
  30.4 6.3 %collective-permute-start.13 = (f32[256,128]{1,0:T(8,128)S(1)}, f32[256,128]{1,0:T(8,128)S(1)}, u32[]{:S(2)}, u32[]{:S(2)}) collective-permute-start(f32[256,128]{1,0:T(8,128)S(1)} %get-tuple-element.46), channel_id=1, source_target_pairs={{0,2},{1,3},{2,0},{3,1},{4,6},{5,7},{6,4},{7,5},{8,10},{9,11},{10,... | collective-permute-start | bytes 393224 | tf_op jit(solution)/shard_map/ppermute | solution.py:85
  31.8 7.7 %collective-permute-start.14 = (f32[256,128]{1,0:T(8,128)S(1)}, f32[256,128]{1,0:T(8,128)S(1)}, u32[]{:S(2)}, u32[]{:S(2)}) collective-permute-start(f32[256,128]{1,0:T(8,128)S(1)} %get-tuple-element.47), channel_id=1, source_target_pairs={{0,3},{1,0},{2,1},{3,2},{4,7},{5,4},{6,5},{7,6},{8,11},{9,8},{10,9... | collective-permute-start | bytes 393224 | tf_op jit(solution)/shard_map/ppermute | solution.py:85
  68.5 4.6 %collective-permute-start.16 = (f32[2,64,128]{2,1,0:T(8,128)S(1)}, f32[2,64,128]{2,1,0:T(8,128)S(1)}, u32[]{:S(2)}, u32[]{:S(2)}) collective-permute-start(f32[2,64,128]{2,1,0:T(8,128)S(1)} %get-tuple-element.49), channel_id=1, source_target_pairs={{0,2},{1,3},{2,0},{3,1},{4,6},{5,7},{6,4},{7,5},{8,10},{9,11},{10,... | collective-permute-start | bytes 196616 | tf_op jit(solution)/shard_map/ppermute | solution.py:85
  94.2 5.5 %collective-permute-start.20 = (f32[128,128]{1,0:T(8,128)S(1)}, f32[128,128]{1,0:T(8,128)S(1)}, u32[]{:S(2)}, u32[]{:S(2)}) collective-permute-start(f32[128,128]{1,0:T(8,128)S(1)} %get-tuple-element.52), channel_id=1, source_target_pairs={{0,1},{1,2},{2,3},{3,0},{4,5},{5,6},{6,7},{7,4},{8,9},{9,10},{10,1... | collective-permute-start | bytes 196616 | tf_op jit(solution)/shard_map/ppermute | solution.py:85
  95.4 4.6 %collective-permute-start.21 = (f32[128,128]{1,0:T(8,128)S(1)}, f32[128,128]{1,0:T(8,128)S(1)}, u32[]{:S(2)}, u32[]{:S(2)}) collective-permute-start(f32[128,128]{1,0:T(8,128)S(1)} %get-tuple-element.52), channel_id=1, source_target_pairs={{0,2},{1,3},{2,0},{3,1},{4,6},{5,7},{6,4},{7,5},{8,10},{9,11},{10,... | collective-permute-start | bytes 196616 | tf_op jit(solution)/shard_map/ppermute | solution.py:85
  110.8 13.0 %all-to-all-start.1 = ((f32[8,2,64,128]{3,2,1,0:T(8,128)}), f32[8,2,64,128]{3,2,1,0:T(8,128)S(1)}, u32[]{:S(2)}, u32[]{:S(2)}) async-start(f32[8,2,64,128]{3,2,1,0:T(8,128)} %copy-done.4), calls=%async_computation.1 | async-start | bytes 1048576 | tf_op jit(solution)/shard_map/all_to_all | solution.py:677
  128.0 5.8 %collective-permute-start.24 = (f32[2,136,128]{2,1,0:T(8,128)S(1)}, f32[2,136,128]{2,1,0:T(8,128)S(1)}, u32[]{:S(2)}, u32[]{:S(2)}) collective-permute-start(f32[2,136,128]{2,1,0:T(8,128)S(1)} %get-tuple-element.57), channel_id=1, source_target_pairs={{0,1},{1,2},{2,3},{3,0},{4,5},{5,6},{6,7},{7,4},{8,9},{9,10},{10,1... | collective-permute-start | bytes 417800 | tf_op jit(solution)/shard_map/ppermute | solution.py:85
  128.1 6.5 %collective-permute-start.25 = (f32[2,136,128]{2,1,0:T(8,128)S(1)}, f32[2,136,128]{2,1,0:T(8,128)S(1)}, u32[]{:S(2)}, u32[]{:S(2)}) collective-permute-start(f32[2,136,128]{2,1,0:T(8,128)S(1)} %get-tuple-element.58), channel_id=1, source_target_pairs={{0,2},{1,3},{2,0},{3,1},{4,6},{5,7},{6,4},{7,5},{8,10},{9,11},{10,... | collective-permute-start | bytes 417800 | tf_op jit(solution)/shard_map/ppermute | solution.py:85
  130.8 7.5 %collective-permute-start.26 = (f32[2,136,128]{2,1,0:T(8,128)S(1)}, f32[2,136,128]{2,1,0:T(8,128)S(1)}, u32[]{:S(2)}, u32[]{:S(2)}) collective-permute-start(f32[2,136,128]{2,1,0:T(8,128)S(1)} %get-tuple-element.59), channel_id=1, source_target_pairs={{0,3},{1,0},{2,1},{3,2},{4,7},{5,4},{6,5},{7,6},{8,11},{9,8},{10,9... | collective-permute-start | bytes 417800 | tf_op jit(solution)/shard_map/ppermute | solution.py:85
  143.3 5.1 %collective-permute-start.28 = (f32[40,256]{1,0:T(8,128)S(1)}, f32[40,256]{1,0:T(8,128)S(1)}, u32[]{:S(2)}, u32[]{:S(2)}) collective-permute-start(f32[40,256]{1,0:T(8,128)S(1)} %get-tuple-element.64), channel_id=1, source_target_pairs={{0,8},{1,9},{2,10},{3,11},{4,12},{5,13},{6,14},{7,15},{8,16},{9,17... | collective-permute-start | bytes 122888 | tf_op jit(solution)/shard_map/ppermute | solution.py:85
  153.4 10.5 %collective-permute-start.32 = (f32[40,256]{1,0:T(8,128)S(1)}, f32[40,256]{1,0:T(8,128)S(1)}, u32[]{:S(2)}, u32[]{:S(2)}) collective-permute-start(f32[40,256]{1,0:T(8,128)S(1)} %add.51), channel_id=1, source_target_pairs={{0,32},{1,33},{2,34},{3,35},{4,36},{5,37},{6,38},{7,39},{8,40},{9,... | collective-permute-start | bytes 122888 | tf_op jit(solution)/shard_map/ppermute | solution.py:85
  156.3 7.5 %collective-permute-start.33 = (f32[40,256]{1,0:T(8,128)S(1)}, f32[40,256]{1,0:T(8,128)S(1)}, u32[]{:S(2)}, u32[]{:S(2)}) collective-permute-start(f32[40,256]{1,0:T(8,128)S(1)} %add.51), channel_id=1, source_target_pairs={{0,64},{1,65},{2,66},{3,67},{4,68},{5,69},{6,70},{7,71},{8,72},{9,... | collective-permute-start | bytes 122888 | tf_op jit(solution)/shard_map/ppermute | solution.py:85
  161.5 4.6 %collective-permute-start.34 = (f32[40,256]{1,0:T(8,128)S(1)}, f32[40,256]{1,0:T(8,128)S(1)}, u32[]{:S(2)}, u32[]{:S(2)}) collective-permute-start(f32[40,256]{1,0:T(8,128)S(1)} %add.51), channel_id=1, source_target_pairs={{0,96},{1,97},{2,98},{3,99},{4,100},{5,101},{6,102},{7,103},{8,104... | collective-permute-start | bytes 122888 | tf_op jit(solution)/shard_map/ppermute | solution.py:85
  179.7 8.9 %collective-permute-start.35 = (f32[16,32,256]{2,1,0:T(8,128)S(1)}, f32[16,32,256]{2,1,0:T(8,128)S(1)}, u32[]{:S(2)}, u32[]{:S(2)}) collective-permute-start(f32[16,32,256]{2,1,0:T(8,128)S(1)} %all_to_all.16.near), channel_id=1, source_target_pairs={{1,5},{6,2},{9,13},{14,10},{17,21},{22,18},{25,29},{30,26},{33,37}... | collective-permute-start | bytes 1572872 | tf_op jit(solution)/shard_map/ppermute | solution.py:85
  (33 other events, 409.1 us)

commit v3 on v2

--- a/solution.py
+++ b/solution.py
@@ -33,7 +33,8 @@
     half = np.arange(512)
     quarter = np.arange(256)
     fours = np.arange(4)
-    cos_m, sin_m = trig(half, half, N)
+    spread = (np.arange(4)[:, None] * 256 + np.arange(128)).reshape(-1)
+    cos_m, sin_m = trig(half, spread, N)
     cos_f, sin_f = trig(quarter, quarter, 256)
     cos_w, sin_w = trig(half, np.arange(N), N)
     sin_w = -sin_w
@@ -43,21 +44,21 @@
     weight[0] = 1.0
     weight[512] = 1.0
     unpack = (packed * weight[:, None]).T / (N * N)
-    rows_ext = (np.arange(N + 16) - 8) % N
+    blocks = [np.r_[64 * q : 64 * q + 64, 512 + 64 * q : 576 + 64 * q] for q in range(8)]
+    by_at = np.concatenate([blocks[2 * s + c] for c in range(2) for s in range(4)])
+    near = packed[np.concatenate(blocks), 256:384].reshape(8, 128, 128).transpose(0, 2, 1)
+    cos_e, sin_e = trig([0, 1], half, 8)
     cos_t, sin_t = trig(quarter, fours, N)
-    cos_c, sin_c = trig(256 + np.arange(128), fours, N)
     return {
         "m": np.stack(halves(cos_m) + halves(sin_m)),
+        "m_back": np.stack(halves(cos_m.T) + halves(sin_m.T)),
         "f": np.stack(halves(cos_f) + halves(sin_f)),
         "pack": np.stack(halves(packed)),
-        "unpack": np.stack(halves(unpack[rows_ext])),
+        "window": np.stack(halves(unpack[256:384, by_at].T)),
+        "near": np.stack(halves(near)),
+        "eighth": np.stack([cos_e, sin_e], 1).astype(np.float32),
         "tw_col": np.concatenate([cos_t, sin_t], 1).astype(np.float32),
-        "tw_row": np.concatenate(
-            [
-                np.concatenate([cos_t, sin_t], 1).T,
-                np.pad(np.concatenate([cos_c, sin_c], 1).T, ((0, 0), (0, 128))),
-            ]
-        ).astype(np.float32),
+        "tw_row": np.concatenate([cos_t, sin_t], 1).T.astype(np.float32).copy(),
     }
 
 
@@ -217,52 +218,60 @@
     return ref[0], ref[1], ref[2], ref[3]
 
 
-def phase_kernel(idx, phases, own, one, two, three):
-    s = idx[0]
-    left = s == 1
-    own[...] = phases[pl.ds(aligned(s, 128), 128), :]
-    one[...] = phases[pl.ds(aligned(jnp.where(left, 0, 3), 128), 128), :]
-    two[...] = phases[pl.ds(aligned(3 - s, 128), 128), :]
-    three[...] = phases[pl.ds(aligned(jnp.where(left, 3, 0), 128), 128), :]
-
-
-def scene_kernel(idx, scene, other, o0, o1, o2, o3, strip, edge):
+def phase_kernel(idx, phases, own0, own1, sent0, sent1, grid):
+    grid[...] = jnp.transpose(phases[...])
+    kept = aligned(jnp.where(idx[0] == 1, 1, 0), 128)
+    given = aligned(jnp.where(idx[0] == 1, 0, 1), 128)
+    own0[...] = grid[pl.ds(kept, 128), 0:256]
+    own1[...] = grid[pl.ds(kept, 128), 256:512]
+    sent0[...] = grid[pl.ds(given, 128), 0:256]
+    sent1[...] = grid[pl.ds(given, 128), 256:512]
+
+
+def scene_kernel(idx, scene, other, w_far, out, strip, edge, image, grid, w, sems):
+    fetch = Fetch(sems, (w_far, w))
     owner = idx[2] == 1
     c = idx[1]
-    for d, out in enumerate((o0, o1, o2, o3)):
-        s = spot_of(idx, d)[0]
-        out[...] = jnp.where(
-            owner,
-            scene[0, :, pl.ds(aligned(4 * c + s, 128), 128)],
-            other[:, pl.ds(aligned(s, 128), 128)],
-        )
-    strip[...] = jnp.where(owner, scene[0, :, 256:384], other[:, 512:640])
-    edge[...] = jnp.where(c == 0, strip[248:256, :], strip[0:8, :])
+    rows = jnp.where(
+        owner,
+        scene[0, pl.ds(aligned(15 * c, 8), 136), :],
+        other[...],
+    )
+    strip[...] = rows[:, 256:384]
+    edge[...] = jnp.where(c == 0, rows[0:8, 256:384], rows[128:136, 256:384])
+    image[...] = jnp.transpose(jnp.where(c == 0, rows[0:128], rows[8:136]))
+    fetch.wait(0)
+    spectrum = by_left(w[0], w[1], image[...])
+    grid[0] = spectrum[:512]
+    grid[1] = spectrum[512:]
+    eight_rows(out, grid)
 
 
 def pupil_kernel(idx, *refs):
-    m_far, o0, o1, o2, o3, pupil, grid, m, sems = refs[8:]
+    m_far, e, o0, o1, o2, o3, pupil, grid, m, sems = refs[8:]
     fetch = Fetch(sems, (m_far, m))
     s = idx[0]
     c = idx[1]
     owner = idx[2] == 1
-    a0, a1, a2, a3 = [jnp.where(owner, refs[at][...], refs[at + 4][...]) for at in range(4)]
-    left = jnp.where(s == 0, a1, jnp.where(s == 1, a0, jnp.where(s == 2, a2, a3)))
-    right = jnp.where(s == 0, a3, jnp.where(s == 1, a2, jnp.where(s == 2, a0, a1)))
-    phase = jnp.concatenate([left, right], 1)
+    central = (s == 1) | (s == 2)
+    own = jnp.concatenate([refs[0][...], refs[1][...]], 1)
+    got = jnp.concatenate([refs[2][...], refs[3][...]], 1)
+    own_far = jnp.concatenate([refs[4][...], refs[5][...]], 1)
+    got_far = jnp.concatenate([refs[6][...], refs[7][...]], 1)
+    phase = jnp.where(central, jnp.where(owner, own, own_far), jnp.where(owner, got, got_far))
     rows = lax.broadcasted_iota(jnp.int32, (128, 512), 0) + s * 128
     cols = lax.broadcasted_iota(jnp.int32, (128, 512), 1)
-    up = (rows + 256) * 2 - N + 1
-    across = (cols + 256) * 2 - N + 1
-    inside = (up * up + across * across) * 4 <= N * N
+    across = (rows + 256) * 2 - N + 1
+    down = (cols + 256) * 2 - N + 1
+    inside = (down * down + across * across) * 4 <= N * N
     cos, sin = cos_sin(phase)
     re = jnp.where(inside, cos, 0.0)
     im = jnp.where(inside, sin, 0.0)
     pupil[0] = re
     pupil[1] = im
-    flip = jnp.where((cols & c) == 1, -1.0, 1.0)
+    re, im = times(re, im, e[c, 0:1, :], -e[c, 1:2, :])
     fetch.wait(0)
-    out_re, out_im = dft_right(re * flip, im * flip, mats_of(m), -1.0)
+    out_re, out_im = dft_right(re, im, mats_of(m), -1.0)
     grid[0] = out_re
     grid[1] = out_im
     for d, out in enumerate((o0, o1, o2, o3)):
@@ -270,21 +279,23 @@
         out[...] = grid[:, :, pl.ds(aligned(to, 128), 128)]
 
 
-def eight_rows(out, grid, at):
+def eight_rows(out, grid):
     for c in range(2):
         for s in range(4):
             row = 128 * s + 64 * c
-            out[4 * c + s, at : at + 2] = grid[:, row : row + 64, :]
+            out[4 * c + s, 0:2] = grid[:, row : row + 64, :]
 
 
 def eight_columns(out, grid):
-    for at in range(8):
-        out[at] = grid[:, :, 128 * at : 128 * at + 128]
-
-
-def optics_kernel(scale, idx, b0, b1, b2, b3, *refs):
-    i0, i1, i2, i3, f_far, tw_far, w_far, far, out, grid, image, f, tw, w, sems = refs
-    fetch = Fetch(sems, (tw_far, tw), (f_far, f), (w_far, w))
+    for c in range(2):
+        for s in range(4):
+            col = 128 * (2 * s + c)
+            out[4 * c + s] = grid[:, :, col : col + 128]
+
+
+def optics_kernel(scale, idx, b0, b1, b2, b3, scene, *refs):
+    f_far, tw_far, far, out, grid, f, tw, sems = refs
+    fetch = Fetch(sems, (tw_far, tw), (f_far, f))
     for d, block in enumerate((b0, b1, b2, b3)):
         grid[:, pl.ds(aligned(from_of(idx, d)[0], 128), 128), :] = block[...]
     low = (grid[0, :256, :], grid[1, :256, :])
@@ -328,14 +339,9 @@
     grid[1, :256, :] = jnp.where(row == 0, nyquist, first[1])
     grid[0, 256:, :] = second[0]
     grid[1, 256:, :] = second[1]
-    eight_rows(out, grid, 0)
-    for d, block in enumerate((i0, i1, i2, i3)):
-        image[pl.ds(aligned(from_of(idx, d)[0], 256), 256), :] = block[...]
-    fetch.wait(2)
-    spectrum = by_left(w[0], w[1], image[...])
-    grid[0] = spectrum[:512]
-    grid[1] = spectrum[512:]
-    eight_rows(out, grid, 2)
+    eight_rows(out, grid)
+    for at in range(8):
+        out[at, 2:4] = scene[at]
 
 
 def unpack_rows(idx, re, im, tail):
@@ -355,9 +361,34 @@
 
 
 def row_transform(idx, blocks, first, mats, tw, grid):
-    for at in range(8):
-        grid[:, :, 128 * at : 128 * at + 128] = blocks[at, first : first + 2]
-    re, im = unpack_rows(idx, grid[0], grid[1], 8)
+    for c in range(2):
+        for s in range(4):
+            col = 128 * (2 * s + c)
+            grid[:, :, col : col + 128] = blocks[4 * c + s, first : first + 2]
+    return rows_out(idx, grid[0], grid[1], mats, tw)
+
+
+def rows_back(idx, re, im, mats, tw, grid):
+    re, im = dft_right(re, im, mats, 1.0)
+    parts = []
+    for r in range(4):
+        a, b = re[r * 72 : r * 72 + 72], im[r * 72 : r * 72 + 72]
+        if r:
+            a, b = times(a, b, tw[r : r + 1, :], tw[4 + r : 5 + r, :])
+        parts.append((a, b))
+    for q in range(4):
+        a, b = parts[0]
+        for r in range(1, 4):
+            more = turned(parts[r][0], parts[r][1], q * r)
+            a = a + more[0]
+            b = b + more[1]
+        a, b = repack_rows(idx, a, b)
+        grid[0, :, q * 256 : q * 256 + 256] = a
+        grid[1, :, q * 256 : q * 256 + 256] = b
+
+
+def rows_out(idx, re, im, mats, tw):
+    re, im = unpack_rows(idx, re, im, 8)
     quarters = [(re[:, q * 256 : q * 256 + 256], im[:, q * 256 : q * 256 + 256]) for q in range(4)]
     sum02 = [quarters[0][p] + quarters[2][p] for p in range(2)]
     dif02 = [quarters[0][p] - quarters[2][p] for p in range(2)]
@@ -380,31 +411,25 @@
     )
 
 
-def blur_kernel(idx, blocks, f_far, tw_far, out, spectrum, grid, f, tw, sems):
+def blur_kernel(idx, blocks, f_far, tw_far, out, spectrum, grid, turned_grid, f, tw, sems):
     fetch = Fetch(sems, (tw_far, tw), (f_far, f))
     fetch.wait(0)
     fetch.wait(1)
     mats = mats_of(f)
-    scene_re, scene_im = row_transform(idx, blocks, 2, mats, tw, grid)
-    spectrum[0] = scene_re
-    spectrum[1] = scene_im
+    re, im = row_transform(idx, blocks, 2, mats, tw, grid)
+    spectrum[0] = re
+    spectrum[1] = im
     re, im = row_transform(idx, blocks, 0, mats, tw, grid)
-    re, im = times(re, im, scene_re, scene_im)
-    mats = tuple(m[:, :128] for m in mats)
-    re, im = dft_right(re, im, mats, 1.0)
-    sum_re, sum_im = re[:72], im[:72]
-    for r in range(1, 4):
-        add = times(
-            re[r * 72 : r * 72 + 72],
-            im[r * 72 : r * 72 + 72],
-            tw[8 + r : 9 + r, :128],
-            tw[12 + r : 13 + r, :128],
-        )
-        sum_re = sum_re + add[0]
-        sum_im = sum_im + add[1]
-    re, im = repack_rows(idx, sum_re, sum_im)
-    out[0] = re
-    out[1] = im
+    re, im = times(re, im, spectrum[0], spectrum[1])
+    rows_back(idx, re, im, mats, tw, grid)
+    both = jnp.transpose(jnp.concatenate([grid[0], grid[1]], 0))
+    turned_grid[8 : N + 8, :] = both
+    turned_grid[0:8, :] = both[N - 8 :, :]
+    turned_grid[N + 8 :, :] = both[:8, :]
+    for c in range(2):
+        for s in range(4):
+            row = 128 * (2 * s + c)
+            out[4 * c + s] = turned_grid[row : row + ROWS, :]
 
 
 def moved_lanes(x, e, lanes):
@@ -424,24 +449,21 @@
 
 
 def net_kernel(pixel_count, idx, w1, b1, w2, *refs):
-    blocks = refs[:2]
-    v, strip, edge, g_out, sums_out = refs[2:7]
-    grid, win_taps, g_taps, hidden, sums, acc = refs[7:]
-    for d, e in relations:
-        s, c = from_of(idx, d, e)
-        at = 2 * s + c
-        grid[pl.ds(aligned(at, 64), 64), :] = blocks[e][d, 0]
-        grid[pl.ds(aligned(at + 8, 64), 64), :] = blocks[e][d, 1]
+    blocks, v_far, strip, edge, g_out, sums_out = refs[:6]
+    win_taps, g_taps, hidden, sums, acc, v, sems = refs[6:]
+    fetch = Fetch(sems, (v_far, v))
     target = jnp.where(
         idx[1] == 0,
-        jnp.concatenate([edge[...], strip[0:136, :]], 0),
-        jnp.concatenate([strip[120:256, :], edge[...]], 0),
-    )
+        jnp.concatenate([edge[...], strip[...]], 0),
+        jnp.concatenate([strip[...], edge[...]], 0),
+    )
+    spectra = jnp.concatenate([blocks[at] for at in range(8)], 1)
+    fetch.wait(0)
     rows = lax.broadcasted_iota(jnp.int32, (ROWS, 128), 0)
     lanes = lax.broadcasted_iota(jnp.int32, (ROWS, 128), 1)
     row_global = rows + (2 * idx[0] + idx[1]) * 128 - 8
     inside = (row_global >= 0) & (row_global < N)
-    window = jnp.where(inside, by_left(v[0], v[1], grid[...]), 0.0)
+    window = jnp.where(inside, by_right(spectra, v[0], v[1]), 0.0)
     for e in (-1, 0, 1):
         side = moved_lanes(window, e, lanes)
         for a in (-1, 0, 1):
@@ -524,41 +546,21 @@
 
 
 def otf_grad_kernel(idx, *refs):
-    blocks = refs[:2]
-    w, f_far, tw_far, spectrum, out, window, grid, f, tw, sems = refs[2:]
-    fetch = Fetch(sems, (f_far, f), (tw_far, tw))
+    blocks = refs[:8]
+    w_far, f_far, tw_far, spectrum, out, window, grid, f, tw, w, sems = refs[8:]
+    fetch = Fetch(
+        sems, (f_far, f), (tw_far, tw), (w_far.at[:, 2 * idx[0] + idx[1]], w)
+    )
     for d, e in relations:
         s, c = from_of(idx, d, e)
-        window[pl.ds(aligned(2 * s + c, 128), 128), :] = blocks[e][d]
-    packed = by_left(w[0], w[1], window[...])
-    fetch.wait(0)
-    fetch.wait(1)
-    re, im = unpack_rows(idx, packed[:64], packed[64:], 8)
-    res, ims = [re], [im]
-    for r in range(1, 4):
-        a, b = times(re, im, tw[8 + r : 9 + r, :128], -tw[12 + r : 13 + r, :128])
-        res.append(a)
-        ims.append(b)
+        window[pl.ds(aligned(2 * s + c, 128), 128), :] = blocks[4 * e + d][...]
+    for at in range(3):
+        fetch.wait(at)
+    packed = jnp.transpose(by_right(window[...], w[0], w[1]))
     mats = mats_of(f)
-    top = tuple(m[:128, :] for m in mats)
-    re, im = dft_right(jnp.concatenate(res, 0), jnp.concatenate(ims, 0), top, -1.0)
+    re, im = rows_out(idx, packed[:64], packed[64:], mats, tw)
     re, im = times(re, im, spectrum[0], -spectrum[1])
-    re, im = dft_right(re, im, mats, 1.0)
-    parts = []
-    for r in range(4):
-        a, b = re[r * 72 : r * 72 + 72], im[r * 72 : r * 72 + 72]
-        if r:
-            a, b = times(a, b, tw[r : r + 1, :], tw[4 + r : 5 + r, :])
-        parts.append((a, b))
-    for q in range(4):
-        a, b = parts[0]
-        for r in range(1, 4):
-            more = turned(parts[r][0], parts[r][1], q * r)
-            a = a + more[0]
-            b = b + more[1]
-        a, b = repack_rows(idx, a, b)
-        grid[0, :, q * 256 : q * 256 + 256] = a
-        grid[1, :, q * 256 : q * 256 + 256] = b
+    rows_back(idx, re, im, mats, tw, grid)
     eight_columns(out, grid)
 
 
@@ -605,29 +607,27 @@
         grid[p, 256:, :] = second[p]
     for d, out in enumerate((o0, o1, o2, o3)):
         out[:, 0:128, :] = grid[:, pl.ds(aligned(spot_of(idx, d)[0], 128), 128), :]
-        out[0, 128:136, :] = small[...]
-        out[1, 128:136, :] = jnp.zeros((8, 128), F32)
+        out[0, 128:144, :] = small[0:16, :]
+        out[1, 128:144, :] = small[16:32, :]
 
 
 def mask_grad_kernel(scale, idx, ids, got, *refs):
-    b0, b1, b2, b3, m_far, pupil, keep, send, grid, whole, m, sems = refs
+    b0, b1, b2, b3, m_far, e, pupil, keep, send, grid, whole, m, sems = refs
     fetch = Fetch(sems, (m_far, m))
     small = None
     for d, block in enumerate((b0, b1, b2, b3)):
         grid[:, :, pl.ds(aligned(from_of(idx, d)[0], 128), 128)] = block[:, 0:128, :]
-        part = block[0, 128:136, :]
+        part = jnp.concatenate([block[0, 128:144, :], block[1, 128:144, :]], 1)
         small = part if small is None else small + part
     fetch.wait(0)
     re, im = dft_right(grid[0], grid[1], mats_of(m), 1.0)
-    cols = lax.broadcasted_iota(jnp.int32, (128, 512), 1)
+    re, im = times(re, im, e[idx[1], 0:1, :], e[idx[1], 1:2, :])
     factor = ratio_of(jnp.where(idx[2] == 1, ids[1], got[1]))[0:1, 0:1] * scale
-    factor = jnp.where((cols & idx[1]) == 1, -factor, factor)
     whole[...] = factor * (im * pupil[0] - re * pupil[1])
-    both = jnp.concatenate([small, small], 1)
     keep[0:128, :] = whole[:, pl.ds(aligned(idx[1], 256), 256)]
     send[0:128, :] = whole[:, pl.ds(aligned(1 - idx[1], 256), 256)]
-    keep[128:136, :] = both
-    send[128:136, :] = both
+    keep[128:144, :] = small
+    send[128:144, :] = small
 
 
 def cut_kernel(ways, idx, keep, other, *refs):
@@ -638,20 +638,29 @@
     for d, out in enumerate(outs):
         to = lax.rem(idx[3] + d, ways)
         out[0:piece, :] = whole[pl.ds(aligned(to, piece), piece), :]
-        out[piece : piece + 8, :] = whole[128:136, :]
-
-
-def home_kernel(ways, idx, near, far, out):
+        out[piece : piece + 16, :] = whole[128:144, :]
+
+
+def home_kernel(ways, pixel_count, idx, small, *refs):
+    near, far, out, w1_out, b1_out, w2_out, loss_out, grid = refs
     piece = 128 // ways
-    at_home = idx[0] == 1 + idx[1]
+    first = idx[1] == 0
+    for y in range(ways):
+        for h in range(2):
+            row = 128 * h + piece * y
+            a, b = near[y, h], far[y, h]
+            grid[row : row + piece, 0:256] = jnp.where(first, a, b)
+            grid[row : row + piece, 256:512] = jnp.where(first, b, a)
     central = (idx[0] == 1) | (idx[0] == 2)
     out[0:256, :] = jnp.zeros((256, 256), F32)
     out[768:1024, :] = jnp.zeros((256, 256), F32)
-    for y in range(ways):
-        for s in range(4):
-            row = 256 + 128 * s + piece * y
-            block = jnp.where(at_home, near[4 * y + s], far[4 * y + s])
-            out[row : row + piece, :] = jnp.where(central, block, 0.0)
+    out[256:768, :] = jnp.where(central, jnp.transpose(grid[...]), 0.0)
+    table = jnp.concatenate([small[:, :128], small[:, 128:]], 0)
+    flat = jnp.transpose(table)
+    w1_out[...] = table[:, 0:9]
+    w2_out[...] = flat[9:18, :]
+    b1_out[...] = flat[18:19, :]
+    loss_out[...] = table[0:1, 19:20] / pixel_count
 
 
 def on_device(lay, phase_mask, height_offsets, sample_ids, wave_ids, scene, w1, b1, w2):
@@ -677,8 +686,8 @@
         return lax.all_to_all(blocks, ("core", "sp"), 0, 0, tiled=True)
 
     def gathered(block):
-        near = jnp.stack(along_sp([block] * 4))
-        return near, lay.move(near, swap)
+        near = along_sp([block] * 4)
+        return near + [lay.move(part, swap) for part in near]
 
     ids = jnp.concatenate([sample_ids, wave_ids])
     got = lay.move(ids, swap)
@@ -686,112 +695,124 @@
     ratio = 550.0 / (400.0 + 10.0 * ids[1].astype(F32))
     phases = ratio * (phase_mask[256:768] + 0.1 * grabbed.astype(F32))
 
-    mine, *sent = call(
+    mine = call(
         phase_kernel,
         (idx, phases),
         (0,),
         [(128, 256)] * 4,
-    )
-    tables = ({1: 0, 2: 3}, {1: 2, 2: 1}, {1: 3, 2: 0})
-    pieces = [mine] + [
+        [pltpu.VMEM((256, 512), F32)],
+    )
+    pieces = list(mine[:2]) + [
         lay.move(
             block,
-            lambda g, zh, y, c, s, to=to: (
-                (g, zh, y, c, to[s]) if s in to and c == g else None
+            lambda g, zh, y, c, s: (
+                (g, zh, y, c, {1: 0, 2: 3}[s]) if s in (1, 2) and c == g else None
             ),
         )
-        for block, to in zip(sent, tables)
+        for block in mine[2:]
     ]
     pieces += [
-        lay.move(block, lambda g, zh, y, c, s: (g, zh, y, 1 - c, s) if c == g else None)
-        for block in pieces
+        lay.move(
+            block,
+            lambda g, zh, y, c, s, inner=inner: (
+                (g, zh, y, 1 - c, s) if c == g and (s in (1, 2)) == inner else None
+            ),
+        )
+        for block, inner in zip(pieces, (True, True, False, False))
     ]
 
-    other = lay.move(
-        jnp.concatenate(
-            [lax.dynamic_slice_in_dim(scene[0], 512 * (1 - c), 512, 1), scene[0, :, 256:384]], 1
-        ),
-        swap,
-    )
-    *columns, strip, edge = call(
-        scene_kernel,
-        (idx, scene, other),
-        (0,),
-        [(256, 128)] * 4 + [(256, 128), (8, 128)],
-    )
-    columns = along_sp(columns)
-    edge = lay.move(edge, lambda g, zh, y, c, s: (g, zh, y, c, s + 1 - 2 * c))
-
-    unpack = lax.dynamic_slice_in_dim(jnp.asarray(con["unpack"]), 128 * (2 * s + c), ROWS, 1)
-    pack = jnp.asarray(con["pack"]).reshape(4, 512, N)
-    pack_rows = lax.dynamic_slice_in_dim(pack, 64 * (2 * s + c), 64, 1).reshape(2, 128, N)
+    scene, pieces[0] = lax.optimization_barrier((scene, pieces[0]))
+    other = lay.move(lax.dynamic_slice_in_dim(scene[0], 120 * (1 - c), 136, 0), swap)
+
     *field, pupil = call(
         pupil_kernel,
-        (idx, *pieces, con["m"]),
+        (idx, *pieces, con["m"], con["eighth"]),
         (0,),
         [(2, 128, 128)] * 4 + [(2, 128, 512)],
         [pltpu.VMEM((2, 128, 512), F32), bf16_buffer(4, 512, 512), fetch_sems(1)],
         (9,),
     )
     field = along_sp(field)
+
+    scene_part, strip, edge = call(
+        scene_kernel,
+        (idx, scene, other, con["pack"]),
+        (0,),
+        [(8, 2, 64, 128), (136, 128), (8, 128)],
+        [
+            pltpu.VMEM((N, 128), F32),
+            pltpu.VMEM((2, 512, 128), F32),
+            bf16_buffer(2, N, N),
+            fetch_sems(1),
+        ],
+        (3,),
+    )
+    edge = lay.move(
+        edge,
+        lambda g, zh, y, c, s: (
+            (g, zh, y, 1 - c, s - 1 + 2 * c) if 0 <= s - 1 + 2 * c < 4 else None
+        ),
+    )
     far, parts = call(
         functools.partial(optics_kernel, scale_psf),
-        (idx, *field, *columns, con["f"], con["tw_col"], con["pack"]),
+        (idx, *field, scene_part, con["f"], con["tw_col"]),
         (0,),
         [(2, 256, 512), (8, 4, 64, 128)],
         [
             pltpu.VMEM((2, 512, 128), F32),
-            pltpu.VMEM((N, 128), F32),
             bf16_buffer(4, 256, 256),
             pltpu.VMEM((256, 8), F32),
-            bf16_buffer(2, N, N),
-            fetch_sems(3),
+            fetch_sems(2),
         ],
-        (9, 10, 11),
-    )
-    half_window, spectrum = call(
+        (6, 7),
+    )
+    parts, edge = lax.optimization_barrier((to_eight(parts), edge))
+    fourier = [bf16_buffer(4, 256, 256), pltpu.VMEM((8, 256), F32)]
+    blurred, spectrum = call(
         blur_kernel,
-        (idx, to_eight(parts), con["f"], con["tw_row"]),
+        (idx, parts, con["f"], con["tw_row"]),
         (0,),
-        [(2, 288, 256), (2, 64, 128)][::-1],
+        [(8, ROWS, 128), (2, 288, 256)],
         [
             pltpu.VMEM((2, 64, N), F32),
-            bf16_buffer(4, 256, 256),
-            pltpu.VMEM((16, 256), F32),
+            pltpu.VMEM((N + 16, 128), F32),
+            *fourier,
             fetch_sems(2),
         ],
         (2, 3),
     )
-    window_parts = gathered(half_window)
+    blurred = to_eight(blurred)
     g_window, sums = call(
         functools.partial(net_kernel, pixel_count),
-        (idx, w1, b1, w2, *window_parts, unpack, strip, edge),
+        (idx, w1, b1, w2, blurred, con["window"], strip, edge),
         (0, 1, 2, 3),
         [(128, 128), (32, 24, 128)],
         [
-            pltpu.VMEM((N, 128), F32),
             pltpu.VMEM((9, ROWS, 128), F32),
             pltpu.VMEM((9, ROWS, 128), F32),
             pltpu.VMEM((32, ROWS, 128), F32),
             pltpu.VMEM((9, ROWS, 128), F32),
             pltpu.VMEM((32, 19, 8, 128), F32),
+            bf16_buffer(2, N, 128),
+            fetch_sems(1),
         ],
-    )
-    small = jnp.pad(jnp.sum(sums, 2).reshape(6, 128), ((0, 2), (0, 0)))
+        (5,),
+    )
+    small = jnp.pad(jnp.sum(sums, 2), ((0, 0), (0, 104)))
     g_parts = gathered(g_window)
     (otf_grad,) = call(
         otf_grad_kernel,
-        (idx, *g_parts, pack_rows, con["f"], con["tw_row"], spectrum),
+        (idx, *g_parts, con["near"], con["f"], con["tw_row"], spectrum),
         (0,),
         [(8, 2, 64, 128)],
         [
             pltpu.VMEM((N, 128), F32),
             pltpu.VMEM((2, 64, N), F32),
-            bf16_buffer(4, 256, 256),
-            pltpu.VMEM((16, 256), F32),
-            fetch_sems(2),
+            *fourier,
+            bf16_buffer(2, 128, 128),
+            fetch_sems(3),
         ],
-        (4, 5),
+        (9, 10, 11),
     )
     otf_grad = to_eight(otf_grad)
     field_grad = along_sp(
@@ -799,7 +820,7 @@
             psf_grad_kernel,
             (idx, otf_grad, far, con["f"], con["tw_col"], small),
             (0,),
-            [(2, 136, 128)] * 4,
+            [(2, 144, 128)] * 4,
             [
                 pltpu.VMEM((2, 512, 128), F32),
                 bf16_buffer(4, 256, 256),
@@ -811,9 +832,9 @@
     )
     keep, send = call(
         functools.partial(mask_grad_kernel, 2.0 * scale_psf),
-        (idx, ids, got, *field_grad, con["m"], pupil),
+        (idx, ids, got, *field_grad, con["m_back"], con["eighth"], pupil),
         (0, 1, 2),
-        [(136, 256)] * 2,
+        [(144, 256)] * 2,
         [
             pltpu.VMEM((2, 128, 512), F32),
             pltpu.VMEM((128, 512), F32),
@@ -828,8 +849,8 @@
         functools.partial(cut_kernel, lay.y),
         (idx, keep, lay.move(send, swap)),
         (0,),
-        [(piece + 8, 256)] * lay.y,
-        [pltpu.VMEM((136, 256), F32)],
+        [(piece + 16, 256)] * lay.y,
+        [pltpu.VMEM((144, 256), F32)],
     )
     total = blocks[0]
     for d in range(1, lay.y):
@@ -840,22 +861,25 @@
     part = total
     for d in range(1, lay.zh):
         total = total + lay.move(part, lambda g, zh, y, c, s, d=d: (g, zh + d, y, c, s))
-    small = total[piece:, :128].reshape(-1)
-    total = total[:piece]
-    ways = 4 * lay.y
+    part = total[:piece]
+    near_part = lay.move(
+        part, lambda g, zh, y, c, s: (g, zh, y, c, {0: 1, 3: 2}[s]) if s in (0, 3) else None
+    )
+    home = jnp.where(s == 1, jnp.stack([near_part, part]), jnp.stack([part, near_part]))
     near = lax.all_to_all(
-        jnp.broadcast_to(total, (ways, piece, 256)), ("y", "sp"), 0, 0, tiled=True
-    )
-    far = lay.move(near, lambda g, zh, y, c, s: (g, zh, y, 1 - c, s) if s == 1 + c else None)
-    (mask_grad,) = call(functools.partial(home_kernel, lay.y), (idx, near, far), (0,), [(N, 256)])
-    table = small[:768].reshape(32, 24)
-    return (
-        mask_grad,
-        table[:, :9],
-        table[:, 18],
-        table[:, 9:18].T,
-        table[0, 19] / pixel_count,
-    )
+        jnp.broadcast_to(home, (lay.y, 2, piece, 256)), "y", 0, 0, tiled=True
+    )
+    far = lay.move(
+        near, lambda g, zh, y, c, s: (g, zh, y, 1 - c, s) if s in (1, 2) else None
+    )
+    mask_grad, w1_grad, b1_grad, w2_grad, loss = call(
+        functools.partial(home_kernel, lay.y, pixel_count),
+        (idx, total[piece:], near, far),
+        (0,),
+        [(N, 256), (32, 9), (1, 32), (9, 32), (1, 1)],
+        [pltpu.VMEM((256, 512), F32)],
+    )
+    return mask_grad, w1_grad, b1_grad.reshape(32), w2_grad, loss.reshape(())
 
 
 def solution(mesh):

time: 194 us -> 187 us (0.964); the launches traced: 191 us -> 186 us
  blocking collectives: 33.5 us -> 8.06 us
  starting transfers between devices: 55.4 us -> 68.3 us
  waiting for transfers between devices: 44.5 us -> 54.3 us
  Pallas kernels: 35.4 us -> 37.4 us
    all_to_all x2 -> x1, blocking collectives: 33.5 us -> 8.06 us  [on_device(): lax.all_to_all(jnp.broadcast_to(home, (lay.y, 2, piece, 256)), 'y', 0, 0,...]
    all_to_all x1 -> x3, waiting for transfers between devices: 7.3 us -> 18.9 us  [to_eight(): return lax.all_to_all(blocks, ('core', 'sp'), 0, 0, tiled=True)]
    all_to_all x1 -> x3, starting transfers between devices: 4.44 us -> 15.3 us  [to_eight(): return lax.all_to_all(blocks, ('core', 'sp'), 0, 0, tiled=True)]
    unnamed x43 -> x48, local copies, waits for them, and re-layouts: 8.73 us -> 12 us
    ppermute x36 -> x32, starting transfers between devices: 51 us -> 53 us  [move(): return lax.ppermute(x, AXES, pairs)]
    pallas_call x11, Pallas kernels: 35.4 us -> 37.4 us  [call(): pl.pallas_call(kernel, out_shape=[jax.ShapeDtypeStruct(shape, F32) for sh...]
    dynamic_slice x3 -> x1, local copies, waits for them, and re-layouts: 3.26 us -> 1.24 us  [on_device(): lax.dynamic_slice_in_dim(scene[0], 120 * (1 - c), 136, 0)]
    ppermute x36 -> x32, waiting for transfers between devices: 37.2 us -> 35.4 us  [move(): return lax.ppermute(x, AXES, pairs)]
  transfers between devices with their start and end apart: 37 -> 35, of which waited for: 23 -> 20; matrix products, arithmetic and copies ran while one was open for 4% -> 1% of each run, Pallas kernels for 2% -> 3%
where the time goes in v3:
time: 187 us; the launch traced here: 186 us
  starting transfers between devices  68.3 us (37%)
  waiting for transfers between devices  54.3 us (29%)
  Pallas kernels  37.4 us (20%)
  local copies, waits for them, and re-layouts  13.2 us (7%)
  blocking collectives  8.06 us (4%)
  other arithmetic  2.64 us (1%)
  between operations  2.48 us (1%)
    ppermute x32, starting transfers between devices, move(): return lax.ppermute(x, AXES, pairs)  53 us
    pallas_call x11, Pallas kernels, call(): pl.pallas_call(kernel, out_shape=[jax.ShapeDtypeStruct(shape, F32) for sh...  37.4 us
    ppermute x32, waiting for transfers between devices, move(): return lax.ppermute(x, AXES, pairs)  35.4 us
    all_to_all x3, waiting for transfers between devices, to_eight(): return lax.all_to_all(blocks, ('core', 'sp'), 0, 0, tiled=True)  18.9 us
    all_to_all x3, starting transfers between devices, to_eight(): return lax.all_to_all(blocks, ('core', 'sp'), 0, 0, tiled=True)  15.3 us
    unnamed x48, local copies, waits for them, and re-layouts  12 us
    all_to_all x1, blocking collectives, on_device(): lax.all_to_all(jnp.broadcast_to(home, (lay.y, 2, piece, 256)), 'y', 0, 0,...  8.06 us
  transfers between devices with their start and end apart: 35, of which 20 were waited for; matrix products, arithmetic and copies ran while one was open for 1% of the time, Pallas kernels for 3%

profile of v3, /device:TPU:3, one launch (start us, length us, event | category | flops | bytes accessed | tf_op | source)
XLA Modules:
  0.0 186.5 jit_solution(4929447596014543161)
XLA Ops:
  20.4 4.9 %collective-permute-start.8 = (f32[2,128,128]{2,1,0:T(8,128)S(1)}, f32[2,128,128]{2,1,0:T(8,128)S(1)}, u32[]{:S(2)}, u32[]{:S(2)}) collective-permute-start(f32[2,128,128]{2,1,0:T(8,128)S(1)} %get-tuple-element.49), channel_id=1, source_target_pairs={{0,2},{1,3},{2,0},{3,1},{4,6},{5,7},{6,4},{7,5},{8,10},{9,11},{10,... | collective-permute-start | bytes 393224 | tf_op jit(solution)/shard_map/ppermute | solution.py:86
  25.5 2.8 %shard_map.202 = (f32[8,2,64,128]{3,2,1,0:T(8,128)S(1)}, f32[136,128]{1,0:T(8,128)S(1)}, f32[8,128]{1,0:T(8,128)S(1)}) custom-call(s32[4]{0:T(128)S(1)} %pad_add_fusion.idx, f32[1,256,1024]{2,1,0:T(8,128)S(1)} %copy-done.2, f32[136,1024]{1,0:T(8,128)S(1)} %collective-permute-done.10.other, bf16[2,1024,1024]{2,1,0:T(8,128)(2,1)S(1)} %copy-done.1), custom_call_target="tpu_custom_call" | custom-call | tf_op jit(solution)/shard_map/pallas_call | solution.py:180
  28.8 3.2 %collective-permute-done.9.b3 = f32[2,128,128]{2,1,0:T(8,128)S(1)} collective-permute-done((f32[2,128,128]{2,1,0:T(8,128)S(1)}, f32[2,128,128]{2,1,0:T(8,128)S(1)}, u32[]{:S(2)}, u32[]{:S(2)}) %collective-permute-start.9) | collective-permute-done | bytes 131104 | tf_op jit(solution)/shard_map/ppermute | solution.py:86
  32.0 3.9 %shard_map.203 = (f32[2,256,512]{2,1,0:T(8,128)S(1)}, f32[8,4,64,128]{3,2,1,0:T(8,128)}) custom-call(s32[4]{0:T(128)S(1)} %pad_add_fusion.idx, f32[2,128,128]{2,1,0:T(8,128)S(1)} %get-tuple-element.47.b0, f32[2,128,128]{2,1,0:T(8,128)S(1)} %collective-permute-done.7.b1, f32[2,128,128]{2,1,0:T(8,128)S(1)} %collective-permute-done.8.b2, ...), custom_call_target="tpu_custom_call" | custom-call | tf_op jit(solution)/shard_map/pallas_call | solution.py:180
  36.9 5.6 %all-to-all-start = ((f32[8,4,64,128]{3,2,1,0:T(8,128)}), f32[8,4,64,128]{3,2,1,0:T(8,128)S(1)}, u32[]{:S(2)}, u32[]{:S(2)}) async-start(f32[8,4,64,128]{3,2,1,0:T(8,128)} %get-tuple-element.53), calls=%async_computation | async-start | bytes 2097152 | tf_op jit(solution)/shard_map/all_to_all | solution.py:686
  42.5 3.3 %collective-permute-start.11 = (f32[8,128]{1,0:T(8,128)S(1)}, f32[8,128]{1,0:T(8,128)S(1)}, u32[]{:S(2)}, u32[]{:S(2)}) collective-permute-start(f32[8,128]{1,0:T(8,128)S(1)} %get-tuple-element.54), channel_id=1, source_target_pairs={{1,4},{2,5},{3,6},{4,1},{5,2},{6,3},{9,12},{10,13},{11,14},{12,9},... | collective-permute-start | bytes 12296 | tf_op jit(solution)/shard_map/ppermute | solution.py:86
  45.9 8.5 %collective-permute-done.11.refs_3_ = f32[8,128]{1,0:T(8,128)S(1)} collective-permute-done((f32[8,128]{1,0:T(8,128)S(1)}, f32[8,128]{1,0:T(8,128)S(1)}, u32[]{:S(2)}, u32[]{:S(2)}) %collective-permute-start.11) | collective-permute-done | bytes 4128 | tf_op jit(solution)/shard_map/ppermute | solution.py:86
  56.7 3.4 %shard_map.204 = (f32[8,144,128]{2,1,0:T(8,128)S(1)}, f32[2,288,256]{2,1,0:T(8,128)S(1)}) custom-call(s32[4]{0:T(128)S(1)} %pad_add_fusion.idx, f32[8,4,64,128]{3,2,1,0:T(8,128)S(1)} %all-to-all-done.blocks, bf16[4,256,256]{2,1,0:T(8,128)(2,1)S(1)} %copy-done, f32[8,256]{1,0:T(8,128)S(1)} %copy-done.19), custom_call_target="tpu_custom_call" | custom-call | tf_op jit(solution)/shard_map/pallas_call | solution.py:180
  61.8 4.8 %all-to-all-start.1 = ((f32[8,144,128]{2,1,0:T(8,128)}), f32[8,144,128]{2,1,0:T(8,128)S(1)}, u32[]{:S(2)}, u32[]{:S(2)}) async-start(f32[8,144,128]{2,1,0:T(8,128)} %copy-done.8), calls=%async_computation.1 | async-start | bytes 1179648 | tf_op jit(solution)/shard_map/all_to_all | solution.py:686
  66.6 9.2 %all-to-all-done.1.refs_0_ = f32[8,144,128]{2,1,0:T(8,128)S(1)} async-done(((f32[8,144,128]{2,1,0:T(8,128)}), f32[8,144,128]{2,1,0:T(8,128)S(1)}, u32[]{:S(2)}, u32[]{:S(2)}) %all-to-all-start.1) | async-done | bytes 589856 | tf_op jit(solution)/shard_map/all_to_all | solution.py:686
  76.9 13.6 %shard_map.205 = (f32[128,128]{1,0:T(8,128)S(1)}, f32[32,24,128]{2,1,0:T(8,128)S(1)}) custom-call(s32[4]{0:T(128)S(1)} %pad_add_fusion.idx, f32[32,9]{1,0:T(8,128)S(1)} %copy.22.w1, f32[32]{0:T(128)S(1)} %copy-done.21, f32[9,32]{1,0:T(8,128)S(1)} %copy-done.20, f32[8,144,128]{2,1,0:T(8,128)S(1)} %all-to-all-done.1.refs_0_, ...), custom_call_target="tpu_custom_call" | custom-call | tf_op jit(solution)/shard_map/pallas_call | solution.py:180
  90.6 2.7 %collective-permute-start.13 = (f32[128,128]{1,0:T(8,128)S(1)}, f32[128,128]{1,0:T(8,128)S(1)}, u32[]{:S(2)}, u32[]{:S(2)}) collective-permute-start(f32[128,128]{1,0:T(8,128)S(1)} %get-tuple-element.59.refs_0_), channel_id=1, source_target_pairs={{0,2},{1,3},{2,0},{3,1},{4,6},{5,7},{6,4},{7,5},{8,10},{9,11},{10,... | collective-permute-start | bytes 196616 | tf_op jit(solution)/shard_map/ppermute | solution.py:86
  101.4 3.4 %shard_map.206 = f32[8,2,64,128]{3,2,1,0:T(8,128)S(1)} custom-call(s32[4]{0:T(128)S(1)} %pad_add_fusion.idx, f32[128,128]{1,0:T(8,128)S(1)} %get-tuple-element.59.refs_0_, f32[128,128]{1,0:T(8,128)S(1)} %collective-permute-done.12.refs_1_, f32[128,128]{1,0:T(8,128)S(1)} %collective-permute-done.13.refs_2_, f32[128,128]{1,0:T(8,128)S(1)} %collective-permute-done.14.refs_3_, ...), custom_call_target="tpu_custom_call" | custom-call | tf_op jit(solution)/shard_map/pallas_call | solution.py:180
  105.6 4.9 %all-to-all-start.2 = ((f32[8,2,64,128]{3,2,1,0:T(8,128)}), f32[8,2,64,128]{3,2,1,0:T(8,128)S(1)}, u32[]{:S(2)}, u32[]{:S(2)}) async-start(f32[8,2,64,128]{3,2,1,0:T(8,128)} %copy-done.5), calls=%async_computation.2 | async-start | bytes 1048576 | tf_op jit(solution)/shard_map/all_to_all | solution.py:686
  111.7 7.4 %all-to-all-done.2.blocks = f32[8,2,64,128]{3,2,1,0:T(8,128)S(1)} async-done(((f32[8,2,64,128]{3,2,1,0:T(8,128)}), f32[8,2,64,128]{3,2,1,0:T(8,128)S(1)}, u32[]{:S(2)}, u32[]{:S(2)}) %all-to-all-start.2) | async-done | bytes 524320 | tf_op jit(solution)/shard_map/all_to_all | solution.py:686
  120.3 3.0 %shard_map.207 = (f32[2,144,128]{2,1,0:T(8,128)S(1)}, f32[2,144,128]{2,1,0:T(8,128)S(1)}, f32[2,144,128]{2,1,0:T(8,128)S(1)}, f32[2,144,128]{2,1,0:T(8,128)S(1)}) custom-call(s32[4]{0:T(128)S(1)} %pad_add_fusion.idx, f32[8,2,64,128]{3,2,1,0:T(8,128)S(1)} %all-to-all-done.2.blocks, f32[2,256,512]{2,1,0:T(8,128)S(1)} %copy-done.7, ...), custom_call_target="tpu_custom_call" | custom-call | tf_op jit(solution)/shard_map/pallas_call | solution.py:180
  123.5 2.7 %collective-permute-start.20 = (f32[2,144,128]{2,1,0:T(8,128)S(1)}, f32[2,144,128]{2,1,0:T(8,128)S(1)}, u32[]{:S(2)}, u32[]{:S(2)}) collective-permute-start(f32[2,144,128]{2,1,0:T(8,128)S(1)} %get-tuple-element.65), channel_id=1, source_target_pairs={{0,2},{1,3},{2,0},{3,1},{4,6},{5,7},{6,4},{7,5},{8,10},{9,11},{10,... | collective-permute-start | bytes 442376 | tf_op jit(solution)/shard_map/ppermute | solution.py:86
  130.5 3.7 %collective-permute-done.21.refs_3_ = f32[2,144,128]{2,1,0:T(8,128)S(1)} collective-permute-done((f32[2,144,128]{2,1,0:T(8,128)S(1)}, f32[2,144,128]{2,1,0:T(8,128)S(1)}, u32[]{:S(2)}, u32[]{:S(2)}) %collective-permute-start.21) | collective-permute-done | bytes 147488 | tf_op jit(solution)/shard_map/ppermute | solution.py:86
  145.6 2.6 %collective-permute-done.26 = f32[48,256]{1,0:T(8,128)S(1)} collective-permute-done((f32[48,256]{1,0:T(8,128)S(1)}, f32[48,256]{1,0:T(8,128)S(1)}, u32[]{:S(2)}, u32[]{:S(2)}) %collective-permute-start.26) | collective-permute-done | bytes 49184 | tf_op jit(solution)/shard_map/ppermute | solution.py:86
  148.3 2.9 %collective-permute-start.27 = (f32[48,256]{1,0:T(8,128)S(1)}, f32[48,256]{1,0:T(8,128)S(1)}, u32[]{:S(2)}, u32[]{:S(2)}) collective-permute-start(f32[48,256]{1,0:T(8,128)S(1)} %add.38), channel_id=1, source_target_pairs={{0,32},{1,33},{2,34},{3,35},{4,36},{5,37},{6,38},{7,39},{8,40},{9,... | collective-permute-start | bytes 147464 | tf_op jit(solution)/shard_map/ppermute | solution.py:86
  151.2 5.1 %collective-permute-start.28 = (f32[48,256]{1,0:T(8,128)S(1)}, f32[48,256]{1,0:T(8,128)S(1)}, u32[]{:S(2)}, u32[]{:S(2)}) collective-permute-start(f32[48,256]{1,0:T(8,128)S(1)} %add.38), channel_id=1, source_target_pairs={{0,64},{1,65},{2,66},{3,67},{4,68},{5,69},{6,70},{7,71},{8,72},{9,... | collective-permute-start | bytes 147464 | tf_op jit(solution)/shard_map/ppermute | solution.py:86
  162.3 3.4 %collective-permute-done.30 = f32[32,256]{1,0:T(8,128)S(1)} collective-permute-done((f32[32,256]{1,0:T(8,128)S(1)}, f32[32,256]{1,0:T(8,128)S(1)}, u32[]{:S(2)}, u32[]{:S(2)}) %collective-permute-start.30) | collective-permute-done | bytes 32800 | tf_op jit(solution)/shard_map/ppermute | solution.py:86
  165.7 8.1 %all_to_all.20.refs_0_ = f32[4,2,32,256]{3,2,1,0:T(8,128)S(1)} all-to-all(f32[4,2,32,256]{3,2,1,0:T(8,128)S(1)} %broadcast_in_dim.3), channel_id=1, replica_groups=mesh['grp'=2,'zh'=4,'y'=4,'core'=2,'sp'=4] {'y'}, dimensions={0} | all-to-all | bytes 524288 | tf_op jit(solution)/shard_map/all_to_all | solution.py:869
  173.8 9.2 %collective-permute-start.31 = (f32[4,2,32,256]{3,2,1,0:T(8,128)S(1)}, f32[4,2,32,256]{3,2,1,0:T(8,128)S(1)}, u32[]{:S(2)}, u32[]{:S(2)}) collective-permute-start(f32[4,2,32,256]{3,2,1,0:T(8,128)S(1)} %all_to_all.20.refs_0_), channel_id=1, source_target_pairs={{1,5},{2,6},{5,1},{6,2},{9,13},{10,14},{13,9},{14,10},{17,21},{18,... | collective-permute-start | bytes 786440 | tf_op jit(solution)/shard_map/ppermute | solution.py:86
  (119 shorter events, 61.9 us)
Async XLA Ops:
  5.6 19.9 %collective-permute-start.10 = (f32[136,1024]{1,0:T(8,128)S(1)}, f32[136,1024]{1,0:T(8,128)S(1)}, u32[]{:S(2)}, u32[]{:S(2)}) collective-permute-start(f32[136,1024]{1,0:T(8,128)S(1)} %dynamic-slice_bitcast_fusion), channel_id=1, source_target_pairs={{0,4},{1,5},{2,6},{3,7},{4,0},{5,1},{6,2},{7,3},{8,12},{9,13},{10,... | collective-permute-start | bytes 1671176 | tf_op jit(solution)/shard_map/ppermute | solution.py:86
  7.7 6.4 %collective-permute-start.3 = (f32[128,256]{1,0:T(8,128)S(1)}, f32[128,256]{1,0:T(8,128)S(1)}, u32[]{:S(2)}, u32[]{:S(2)}) collective-permute-start(f32[128,256]{1,0:T(8,128)S(1)} %get-tuple-element.43.refs_0_), channel_id=1, source_target_pairs={{1,5},{2,6},{9,13},{10,14},{17,21},{18,22},{25,29},{26,30},{33,37}... | collective-permute-start | bytes 393224 | tf_op jit(solution)/shard_map/ppermute | solution.py:86
  9.0 6.6 %collective-permute-start.4 = (f32[128,256]{1,0:T(8,128)S(1)}, f32[128,256]{1,0:T(8,128)S(1)}, u32[]{:S(2)}, u32[]{:S(2)}) collective-permute-start(f32[128,256]{1,0:T(8,128)S(1)} %get-tuple-element.44.refs_1_), channel_id=1, source_target_pairs={{1,5},{2,6},{9,13},{10,14},{17,21},{18,22},{25,29},{26,30},{33,37}... | collective-permute-start | bytes 393224 | tf_op jit(solution)/shard_map/ppermute | solution.py:86
  10.4 5.1 %collective-permute-start.5 = (f32[128,256]{1,0:T(8,128)S(1)}, f32[128,256]{1,0:T(8,128)S(1)}, u32[]{:S(2)}, u32[]{:S(2)}) collective-permute-start(f32[128,256]{1,0:T(8,128)S(1)} %collective-permute-done.1.refs_2_), channel_id=1, source_target_pairs={{0,4},{3,7},{8,12},{11,15},{16,20},{19,23},{24,28},{27,31},{32,36}... | collective-permute-start | bytes 393224 | tf_op jit(solution)/shard_map/ppermute | solution.py:86
  20.2 8.2 %collective-permute-start.7 = (f32[2,128,128]{2,1,0:T(8,128)S(1)}, f32[2,128,128]{2,1,0:T(8,128)S(1)}, u32[]{:S(2)}, u32[]{:S(2)}) collective-permute-start(f32[2,128,128]{2,1,0:T(8,128)S(1)} %get-tuple-element.48), channel_id=1, source_target_pairs={{0,1},{1,2},{2,3},{3,0},{4,5},{5,6},{6,7},{7,4},{8,9},{9,10},{10,1... | collective-permute-start | bytes 393224 | tf_op jit(solution)/shard_map/ppermute | solution.py:86
  20.4 8.4 %collective-permute-start.8 = (f32[2,128,128]{2,1,0:T(8,128)S(1)}, f32[2,128,128]{2,1,0:T(8,128)S(1)}, u32[]{:S(2)}, u32[]{:S(2)}) collective-permute-start(f32[2,128,128]{2,1,0:T(8,128)S(1)} %get-tuple-element.49), channel_id=1, source_target_pairs={{0,2},{1,3},{2,0},{3,1},{4,6},{5,7},{6,4},{7,5},{8,10},{9,11},{10,... | collective-permute-start | bytes 393224 | tf_op jit(solution)/shard_map/ppermute | solution.py:86
  25.3 6.7 %collective-permute-start.9 = (f32[2,128,128]{2,1,0:T(8,128)S(1)}, f32[2,128,128]{2,1,0:T(8,128)S(1)}, u32[]{:S(2)}, u32[]{:S(2)}) collective-permute-start(f32[2,128,128]{2,1,0:T(8,128)S(1)} %get-tuple-element.50), channel_id=1, source_target_pairs={{0,3},{1,0},{2,1},{3,2},{4,7},{5,4},{6,5},{7,6},{8,11},{9,8},{10,9... | collective-permute-start | bytes 393224 | tf_op jit(solution)/shard_map/ppermute | solution.py:86
  36.9 19.8 %all-to-all-start = ((f32[8,4,64,128]{3,2,1,0:T(8,128)}), f32[8,4,64,128]{3,2,1,0:T(8,128)S(1)}, u32[]{:S(2)}, u32[]{:S(2)}) async-start(f32[8,4,64,128]{3,2,1,0:T(8,128)} %get-tuple-element.53), calls=%async_computation | async-start | bytes 2097152 | tf_op jit(solution)/shard_map/all_to_all | solution.py:686
  42.5 11.8 %collective-permute-start.11 = (f32[8,128]{1,0:T(8,128)S(1)}, f32[8,128]{1,0:T(8,128)S(1)}, u32[]{:S(2)}, u32[]{:S(2)}) collective-permute-start(f32[8,128]{1,0:T(8,128)S(1)} %get-tuple-element.54), channel_id=1, source_target_pairs={{1,4},{2,5},{3,6},{4,1},{5,2},{6,3},{9,12},{10,13},{11,14},{12,9},... | collective-permute-start | bytes 12296 | tf_op jit(solution)/shard_map/ppermute | solution.py:86
  61.8 14.0 %all-to-all-start.1 = ((f32[8,144,128]{2,1,0:T(8,128)}), f32[8,144,128]{2,1,0:T(8,128)S(1)}, u32[]{:S(2)}, u32[]{:S(2)}) async-start(f32[8,144,128]{2,1,0:T(8,128)} %copy-done.8), calls=%async_computation.1 | async-start | bytes 1179648 | tf_op jit(solution)/shard_map/all_to_all | solution.py:686
  90.5 4.9 %collective-permute-start.12 = (f32[128,128]{1,0:T(8,128)S(1)}, f32[128,128]{1,0:T(8,128)S(1)}, u32[]{:S(2)}, u32[]{:S(2)}) collective-permute-start(f32[128,128]{1,0:T(8,128)S(1)} %get-tuple-element.59.refs_0_), channel_id=1, source_target_pairs={{0,1},{1,2},{2,3},{3,0},{4,5},{5,6},{6,7},{7,4},{8,9},{9,10},{10,1... | collective-permute-start | bytes 196616 | tf_op jit(solution)/shard_map/ppermute | solution.py:86
  90.6 4.8 %collective-permute-start.13 = (f32[128,128]{1,0:T(8,128)S(1)}, f32[128,128]{1,0:T(8,128)S(1)}, u32[]{:S(2)}, u32[]{:S(2)}) collective-permute-start(f32[128,128]{1,0:T(8,128)S(1)} %get-tuple-element.59.refs_0_), channel_id=1, source_target_pairs={{0,2},{1,3},{2,0},{3,1},{4,6},{5,7},{6,4},{7,5},{8,10},{9,11},{10,... | collective-permute-start | bytes 196616 | tf_op jit(solution)/shard_map/ppermute | solution.py:86
  93.6 4.8 %collective-permute-start.15 = (f32[128,128]{1,0:T(8,128)S(1)}, f32[128,128]{1,0:T(8,128)S(1)}, u32[]{:S(2)}, u32[]{:S(2)}) collective-permute-start(f32[128,128]{1,0:T(8,128)S(1)} %get-tuple-element.59.refs_0_), channel_id=1, source_target_pairs={{0,4},{1,5},{2,6},{3,7},{4,0},{5,1},{6,2},{7,3},{8,12},{9,13},{10,... | collective-permute-start | bytes 196616 | tf_op jit(solution)/shard_map/ppermute | solution.py:86
  105.6 13.5 %all-to-all-start.2 = ((f32[8,2,64,128]{3,2,1,0:T(8,128)}), f32[8,2,64,128]{3,2,1,0:T(8,128)S(1)}, u32[]{:S(2)}, u32[]{:S(2)}) async-start(f32[8,2,64,128]{3,2,1,0:T(8,128)} %copy-done.5), calls=%async_computation.2 | async-start | bytes 1048576 | tf_op jit(solution)/shard_map/all_to_all | solution.py:686
  123.4 5.8 %collective-permute-start.19 = (f32[2,144,128]{2,1,0:T(8,128)S(1)}, f32[2,144,128]{2,1,0:T(8,128)S(1)}, u32[]{:S(2)}, u32[]{:S(2)}) collective-permute-start(f32[2,144,128]{2,1,0:T(8,128)S(1)} %get-tuple-element.64), channel_id=1, source_target_pairs={{0,1},{1,2},{2,3},{3,0},{4,5},{5,6},{6,7},{7,4},{8,9},{9,10},{10,1... | collective-permute-start | bytes 442376 | tf_op jit(solution)/shard_map/ppermute | solution.py:86
  123.5 7.1 %collective-permute-start.20 = (f32[2,144,128]{2,1,0:T(8,128)S(1)}, f32[2,144,128]{2,1,0:T(8,128)S(1)}, u32[]{:S(2)}, u32[]{:S(2)}) collective-permute-start(f32[2,144,128]{2,1,0:T(8,128)S(1)} %get-tuple-element.65), channel_id=1, source_target_pairs={{0,2},{1,3},{2,0},{3,1},{4,6},{5,7},{6,4},{7,5},{8,10},{9,11},{10,... | collective-permute-start | bytes 442376 | tf_op jit(solution)/shard_map/ppermute | solution.py:86
  126.1 8.1 %collective-permute-start.21 = (f32[2,144,128]{2,1,0:T(8,128)S(1)}, f32[2,144,128]{2,1,0:T(8,128)S(1)}, u32[]{:S(2)}, u32[]{:S(2)}) collective-permute-start(f32[2,144,128]{2,1,0:T(8,128)S(1)} %get-tuple-element.66), channel_id=1, source_target_pairs={{0,3},{1,0},{2,1},{3,2},{4,7},{5,4},{6,5},{7,6},{8,11},{9,8},{10,9... | collective-permute-start | bytes 442376 | tf_op jit(solution)/shard_map/ppermute | solution.py:86
  139.3 5.0 %collective-permute-start.23 = (f32[48,256]{1,0:T(8,128)S(1)}, f32[48,256]{1,0:T(8,128)S(1)}, u32[]{:S(2)}, u32[]{:S(2)}) collective-permute-start(f32[48,256]{1,0:T(8,128)S(1)} %get-tuple-element.71), channel_id=1, source_target_pairs={{0,8},{1,9},{2,10},{3,11},{4,12},{5,13},{6,14},{7,15},{8,16},{9,17... | collective-permute-start | bytes 147464 | tf_op jit(solution)/shard_map/ppermute | solution.py:86
  139.4 4.9 %collective-permute-start.24 = (f32[48,256]{1,0:T(8,128)S(1)}, f32[48,256]{1,0:T(8,128)S(1)}, u32[]{:S(2)}, u32[]{:S(2)}) collective-permute-start(f32[48,256]{1,0:T(8,128)S(1)} %get-tuple-element.72), channel_id=1, source_target_pairs={{0,16},{1,17},{2,18},{3,19},{4,20},{5,21},{6,22},{7,23},{8,24},{9,... | collective-permute-start | bytes 147464 | tf_op jit(solution)/shard_map/ppermute | solution.py:86
  148.3 10.4 %collective-permute-start.27 = (f32[48,256]{1,0:T(8,128)S(1)}, f32[48,256]{1,0:T(8,128)S(1)}, u32[]{:S(2)}, u32[]{:S(2)}) collective-permute-start(f32[48,256]{1,0:T(8,128)S(1)} %add.38), channel_id=1, source_target_pairs={{0,32},{1,33},{2,34},{3,35},{4,36},{5,37},{6,38},{7,39},{8,40},{9,... | collective-permute-start | bytes 147464 | tf_op jit(solution)/shard_map/ppermute | solution.py:86
  151.2 7.6 %collective-permute-start.28 = (f32[48,256]{1,0:T(8,128)S(1)}, f32[48,256]{1,0:T(8,128)S(1)}, u32[]{:S(2)}, u32[]{:S(2)}) collective-permute-start(f32[48,256]{1,0:T(8,128)S(1)} %add.38), channel_id=1, source_target_pairs={{0,64},{1,65},{2,66},{3,67},{4,68},{5,69},{6,70},{7,71},{8,72},{9,... | collective-permute-start | bytes 147464 | tf_op jit(solution)/shard_map/ppermute | solution.py:86
  156.3 4.7 %collective-permute-start.29 = (f32[48,256]{1,0:T(8,128)S(1)}, f32[48,256]{1,0:T(8,128)S(1)}, u32[]{:S(2)}, u32[]{:S(2)}) collective-permute-start(f32[48,256]{1,0:T(8,128)S(1)} %add.38), channel_id=1, source_target_pairs={{0,96},{1,97},{2,98},{3,99},{4,100},{5,101},{6,102},{7,103},{8,104... | collective-permute-start | bytes 147464 | tf_op jit(solution)/shard_map/ppermute | solution.py:86
  161.0 4.7 %collective-permute-start.30 = (f32[32,256]{1,0:T(8,128)S(1)}, f32[32,256]{1,0:T(8,128)S(1)}, u32[]{:S(2)}, u32[]{:S(2)}) collective-permute-start(f32[32,256]{1,0:T(8,128)S(1)} %get-tuple-element.84), channel_id=1, source_target_pairs={{0,1},{3,2},{4,5},{7,6},{8,9},{11,10},{12,13},{15,14},{16,17},{19,... | collective-permute-start | bytes 98312 | tf_op jit(solution)/shard_map/ppermute | solution.py:86
  173.8 10.3 %collective-permute-start.31 = (f32[4,2,32,256]{3,2,1,0:T(8,128)S(1)}, f32[4,2,32,256]{3,2,1,0:T(8,128)S(1)}, u32[]{:S(2)}, u32[]{:S(2)}) collective-permute-start(f32[4,2,32,256]{3,2,1,0:T(8,128)S(1)} %all_to_all.20.refs_0_), channel_id=1, source_target_pairs={{1,5},{2,6},{5,1},{6,2},{9,13},{10,14},{13,9},{14,10},{17,21},{18,... | collective-permute-start | bytes 786440 | tf_op jit(solution)/shard_map/ppermute | solution.py:86
  (34 other events, 465.0 us)

commit v4 on v3

--- a/solution.py
+++ b/solution.py
@@ -47,15 +47,17 @@
     blocks = [np.r_[64 * q : 64 * q + 64, 512 + 64 * q : 576 + 64 * q] for q in range(8)]
     by_at = np.concatenate([blocks[2 * s + c] for c in range(2) for s in range(4)])
     near = packed[np.concatenate(blocks), 256:384].reshape(8, 128, 128).transpose(0, 2, 1)
+    window = np.stack(halves(unpack[256:384, by_at].T))
+    window = window.reshape(4, 2, 256, 128).transpose(0, 2, 1, 3).reshape(4, 256, 256)
+    near = np.stack(halves(near)).reshape(4, 2, 2, 128, 128)
+    near = near.transpose(0, 1, 3, 2, 4).reshape(4, 256, 256)
     cos_e, sin_e = trig([0, 1], half, 8)
     cos_t, sin_t = trig(quarter, fours, N)
     return {
         "m": np.stack(halves(cos_m) + halves(sin_m)),
         "m_back": np.stack(halves(cos_m.T) + halves(sin_m.T)),
-        "f": np.stack(halves(cos_f) + halves(sin_f)),
+        "f": np.concatenate([np.stack(halves(cos_f) + halves(sin_f)), window, near]),
         "pack": np.stack(halves(packed)),
-        "window": np.stack(halves(unpack[256:384, by_at].T)),
-        "near": np.stack(halves(near)),
         "eighth": np.stack([cos_e, sin_e], 1).astype(np.float32),
         "tw_col": np.concatenate([cos_t, sin_t], 1).astype(np.float32),
         "tw_row": np.concatenate([cos_t, sin_t], 1).T.astype(np.float32).copy(),
@@ -190,26 +192,6 @@
 relations = [(d, e) for e in range(2) for d in range(4)]
 
 
-class Fetch:
-    def __init__(self, sems, *pairs):
-        self.copies = [
-            pltpu.make_async_copy(src, dst, sems.at[at]) for at, (src, dst) in enumerate(pairs)
-        ]
-        for copy in self.copies:
-            copy.start()
-
-    def wait(self, at):
-        self.copies[at].wait()
-
-
-def bf16_buffer(*shape):
-    return pltpu.VMEM(shape, BF16)
-
-
-def fetch_sems(count):
-    return pltpu.SemaphoreType.DMA((count,))
-
-
 def ratio_of(wave):
     return 550.0 / (400.0 + 10.0 * jnp.full((8, 128), wave, jnp.int32).astype(F32))
 
@@ -228,8 +210,7 @@
     sent1[...] = grid[pl.ds(given, 128), 256:512]
 
 
-def scene_kernel(idx, scene, other, w_far, out, strip, edge, image, grid, w, sems):
-    fetch = Fetch(sems, (w_far, w))
+def scene_kernel(idx, scene, other, w, out, strip, edge, image, grid):
     owner = idx[2] == 1
     c = idx[1]
     rows = jnp.where(
@@ -240,7 +221,6 @@
     strip[...] = rows[:, 256:384]
     edge[...] = jnp.where(c == 0, rows[0:8, 256:384], rows[128:136, 256:384])
     image[...] = jnp.transpose(jnp.where(c == 0, rows[0:128], rows[8:136]))
-    fetch.wait(0)
     spectrum = by_left(w[0], w[1], image[...])
     grid[0] = spectrum[:512]
     grid[1] = spectrum[512:]
@@ -248,8 +228,7 @@
 
 
 def pupil_kernel(idx, *refs):
-    m_far, e, o0, o1, o2, o3, pupil, grid, m, sems = refs[8:]
-    fetch = Fetch(sems, (m_far, m))
+    m, e, o0, o1, o2, o3, pupil, grid = refs[8:]
     s = idx[0]
     c = idx[1]
     owner = idx[2] == 1
@@ -270,7 +249,6 @@
     pupil[0] = re
     pupil[1] = im
     re, im = times(re, im, e[c, 0:1, :], -e[c, 1:2, :])
-    fetch.wait(0)
     out_re, out_im = dft_right(re, im, mats_of(m), -1.0)
     grid[0] = out_re
     grid[1] = out_im
@@ -294,13 +272,11 @@
 
 
 def optics_kernel(scale, idx, b0, b1, b2, b3, scene, *refs):
-    f_far, tw_far, far, out, grid, f, tw, sems = refs
-    fetch = Fetch(sems, (tw_far, tw), (f_far, f))
+    f, tw, far, out, grid = refs
     for d, block in enumerate((b0, b1, b2, b3)):
         grid[:, pl.ds(aligned(from_of(idx, d)[0], 128), 128), :] = block[...]
     low = (grid[0, :256, :], grid[1, :256, :])
     high = (grid[0, 256:, :], grid[1, 256:, :])
-    fetch.wait(0)
     twists = [(tw[:, r : r + 1], tw[:, 4 + r : 5 + r]) for r in range(4)]
     res, ims = [], []
     for r in range(4):
@@ -310,7 +286,6 @@
             re, im = times(re, im, twists[r][0], -twists[r][1])
         res.append(re)
         ims.append(im)
-    fetch.wait(1)
     mats = mats_of(f)
     far_re, far_im = dft_left(
         jnp.concatenate(res, 1), jnp.concatenate(ims, 1), mats, -1.0
@@ -411,10 +386,7 @@
     )
 
 
-def blur_kernel(idx, blocks, f_far, tw_far, out, spectrum, grid, turned_grid, f, tw, sems):
-    fetch = Fetch(sems, (tw_far, tw), (f_far, f))
-    fetch.wait(0)
-    fetch.wait(1)
+def blur_kernel(idx, blocks, f, tw, out, spectrum, grid, turned_grid):
     mats = mats_of(f)
     re, im = row_transform(idx, blocks, 2, mats, tw, grid)
     spectrum[0] = re
@@ -449,21 +421,26 @@
 
 
 def net_kernel(pixel_count, idx, w1, b1, w2, *refs):
-    blocks, v_far, strip, edge, g_out, sums_out = refs[:6]
-    win_taps, g_taps, hidden, sums, acc, v, sems = refs[6:]
-    fetch = Fetch(sems, (v_far, v))
+    blocks, f, strip, edge, g_out, sums_out = refs[:6]
+    win_taps, g_taps, hidden, sums, acc = refs[6:]
     target = jnp.where(
         idx[1] == 0,
         jnp.concatenate([edge[...], strip[...]], 0),
         jnp.concatenate([strip[...], edge[...]], 0),
     )
-    spectra = jnp.concatenate([blocks[at] for at in range(8)], 1)
-    fetch.wait(0)
+    window = None
+    for at in range(4):
+        part = by_right(
+            jnp.concatenate([blocks[2 * at], blocks[2 * at + 1]], 1),
+            f[4 + at // 2, :, 128 * (at % 2) : 128 * (at % 2) + 128],
+            f[6 + at // 2, :, 128 * (at % 2) : 128 * (at % 2) + 128],
+        )
+        window = part if window is None else window + part
     rows = lax.broadcasted_iota(jnp.int32, (ROWS, 128), 0)
     lanes = lax.broadcasted_iota(jnp.int32, (ROWS, 128), 1)
     row_global = rows + (2 * idx[0] + idx[1]) * 128 - 8
     inside = (row_global >= 0) & (row_global < N)
-    window = jnp.where(inside, by_right(spectra, v[0], v[1]), 0.0)
+    window = jnp.where(inside, window, 0.0)
     for e in (-1, 0, 1):
         side = moved_lanes(window, e, lanes)
         for a in (-1, 0, 1):
@@ -547,16 +524,14 @@
 
 def otf_grad_kernel(idx, *refs):
     blocks = refs[:8]
-    w_far, f_far, tw_far, spectrum, out, window, grid, f, tw, w, sems = refs[8:]
-    fetch = Fetch(
-        sems, (f_far, f), (tw_far, tw), (w_far.at[:, 2 * idx[0] + idx[1]], w)
-    )
+    f, tw, spectrum, out, window, grid = refs[8:]
     for d, e in relations:
         s, c = from_of(idx, d, e)
         window[pl.ds(aligned(2 * s + c, 128), 128), :] = blocks[4 * e + d][...]
-    for at in range(3):
-        fetch.wait(at)
-    packed = jnp.transpose(by_right(window[...], w[0], w[1]))
+    rows = pl.ds(aligned(lax.rem(idx[0], 2), 128), 128)
+    cols = pl.ds(aligned(idx[1], 128), 128)
+    at = lax.div(idx[0], 2)
+    packed = jnp.transpose(by_right(window[...], f[8 + at, rows, cols], f[10 + at, rows, cols]))
     mats = mats_of(f)
     re, im = rows_out(idx, packed[:64], packed[64:], mats, tw)
     re, im = times(re, im, spectrum[0], -spectrum[1])
@@ -564,8 +539,7 @@
     eight_columns(out, grid)
 
 
-def psf_grad_kernel(idx, blocks, far, f_far, tw_far, small, o0, o1, o2, o3, grid, f, tw, sems):
-    fetch = Fetch(sems, (f_far, f), (tw_far, tw))
+def psf_grad_kernel(idx, blocks, far, f, tw, small, o0, o1, o2, o3, grid):
     for c in range(2):
         for s in range(4):
             grid[:, 128 * s + 64 * c : 128 * s + 64 * c + 64, :] = blocks[4 * c + s]
@@ -576,7 +550,6 @@
     low_re = jnp.where(zero_row, 0.5 * low_re, low_re)
     low_im = jnp.where(zero_row, 0.0, low_im)
     high = (grid[0, 256:, :], grid[1, 256:, :])
-    fetch.wait(1)
     twists = [(tw[:, r : r + 1], tw[:, 4 + r : 5 + r]) for r in range(4)]
     res, ims = [], []
     for r in range(4):
@@ -587,7 +560,6 @@
         re = re + nyquist if r % 2 == 0 else re - nyquist
         res.append(re)
         ims.append(im)
-    fetch.wait(0)
     mats = mats_of(f)
     g_psf = 2.0 * (
         by_left(mats[0], mats[1], jnp.concatenate(res, 1))
@@ -607,27 +579,25 @@
         grid[p, 256:, :] = second[p]
     for d, out in enumerate((o0, o1, o2, o3)):
         out[:, 0:128, :] = grid[:, pl.ds(aligned(spot_of(idx, d)[0], 128), 128), :]
-        out[0, 128:144, :] = small[0:16, :]
-        out[1, 128:144, :] = small[16:32, :]
+        out[0, 128:136, :] = small[...]
+        out[1, 128:136, :] = small[...]
 
 
 def mask_grad_kernel(scale, idx, ids, got, *refs):
-    b0, b1, b2, b3, m_far, e, pupil, keep, send, grid, whole, m, sems = refs
-    fetch = Fetch(sems, (m_far, m))
+    b0, b1, b2, b3, m, e, pupil, keep, send, grid, whole = refs
     small = None
     for d, block in enumerate((b0, b1, b2, b3)):
         grid[:, :, pl.ds(aligned(from_of(idx, d)[0], 128), 128)] = block[:, 0:128, :]
-        part = jnp.concatenate([block[0, 128:144, :], block[1, 128:144, :]], 1)
+        part = jnp.concatenate([block[0, 128:136, :], block[1, 128:136, :]], 1)
         small = part if small is None else small + part
-    fetch.wait(0)
     re, im = dft_right(grid[0], grid[1], mats_of(m), 1.0)
     re, im = times(re, im, e[idx[1], 0:1, :], e[idx[1], 1:2, :])
     factor = ratio_of(jnp.where(idx[2] == 1, ids[1], got[1]))[0:1, 0:1] * scale
     whole[...] = factor * (im * pupil[0] - re * pupil[1])
     keep[0:128, :] = whole[:, pl.ds(aligned(idx[1], 256), 256)]
     send[0:128, :] = whole[:, pl.ds(aligned(1 - idx[1], 256), 256)]
-    keep[128:144, :] = small
-    send[128:144, :] = small
+    keep[128:136, :] = small
+    send[128:136, :] = small
 
 
 def cut_kernel(ways, idx, keep, other, *refs):
@@ -638,7 +608,7 @@
     for d, out in enumerate(outs):
         to = lax.rem(idx[3] + d, ways)
         out[0:piece, :] = whole[pl.ds(aligned(to, piece), piece), :]
-        out[piece : piece + 16, :] = whole[128:144, :]
+        out[piece : piece + 8, :] = whole[128:136, :]
 
 
 def home_kernel(ways, pixel_count, idx, small, *refs):
@@ -655,12 +625,11 @@
     out[0:256, :] = jnp.zeros((256, 256), F32)
     out[768:1024, :] = jnp.zeros((256, 256), F32)
     out[256:768, :] = jnp.where(central, jnp.transpose(grid[...]), 0.0)
-    table = jnp.concatenate([small[:, :128], small[:, 128:]], 0)
-    flat = jnp.transpose(table)
-    w1_out[...] = table[:, 0:9]
+    flat = jnp.concatenate([small[:, 32 * g : 32 * g + 32] for g in range(3)], 0)
+    w1_out[...] = flat[0:9, :]
     w2_out[...] = flat[9:18, :]
     b1_out[...] = flat[18:19, :]
-    loss_out[...] = table[0:1, 19:20] / pixel_count
+    loss_out[...] = flat[19:20, 0:1] / pixel_count
 
 
 def on_device(lay, phase_mask, height_offsets, sample_ids, wave_ids, scene, w1, b1, w2):
@@ -729,8 +698,7 @@
         (idx, *pieces, con["m"], con["eighth"]),
         (0,),
         [(2, 128, 128)] * 4 + [(2, 128, 512)],
-        [pltpu.VMEM((2, 128, 512), F32), bf16_buffer(4, 512, 512), fetch_sems(1)],
-        (9,),
+        [pltpu.VMEM((2, 128, 512), F32)],
     )
     field = along_sp(field)
 
@@ -742,10 +710,7 @@
         [
             pltpu.VMEM((N, 128), F32),
             pltpu.VMEM((2, 512, 128), F32),
-            bf16_buffer(2, N, N),
-            fetch_sems(1),
         ],
-        (3,),
     )
     edge = lay.move(
         edge,
@@ -760,14 +725,9 @@
         [(2, 256, 512), (8, 4, 64, 128)],
         [
             pltpu.VMEM((2, 512, 128), F32),
-            bf16_buffer(4, 256, 256),
-            pltpu.VMEM((256, 8), F32),
-            fetch_sems(2),
         ],
-        (6, 7),
     )
     parts, edge = lax.optimization_barrier((to_eight(parts), edge))
-    fourier = [bf16_buffer(4, 256, 256), pltpu.VMEM((8, 256), F32)]
     blurred, spectrum = call(
         blur_kernel,
         (idx, parts, con["f"], con["tw_row"]),
@@ -776,15 +736,12 @@
         [
             pltpu.VMEM((2, 64, N), F32),
             pltpu.VMEM((N + 16, 128), F32),
-            *fourier,
-            fetch_sems(2),
         ],
-        (2, 3),
     )
     blurred = to_eight(blurred)
     g_window, sums = call(
         functools.partial(net_kernel, pixel_count),
-        (idx, w1, b1, w2, blurred, con["window"], strip, edge),
+        (idx, w1, b1, w2, blurred, con["f"], strip, edge),
         (0, 1, 2, 3),
         [(128, 128), (32, 24, 128)],
         [
@@ -793,26 +750,20 @@
             pltpu.VMEM((32, ROWS, 128), F32),
             pltpu.VMEM((9, ROWS, 128), F32),
             pltpu.VMEM((32, 19, 8, 128), F32),
-            bf16_buffer(2, N, 128),
-            fetch_sems(1),
         ],
-        (5,),
-    )
-    small = jnp.pad(jnp.sum(sums, 2), ((0, 0), (0, 104)))
+    )
+    small = jnp.sum(sums, 2).reshape(32, 3, 8).transpose(2, 1, 0).reshape(8, 96)
+    small = jnp.pad(small, ((0, 0), (0, 32)))
     g_parts = gathered(g_window)
     (otf_grad,) = call(
         otf_grad_kernel,
-        (idx, *g_parts, con["near"], con["f"], con["tw_row"], spectrum),
+        (idx, *g_parts, con["f"], con["tw_row"], spectrum),
         (0,),
         [(8, 2, 64, 128)],
         [
             pltpu.VMEM((N, 128), F32),
             pltpu.VMEM((2, 64, N), F32),
-            *fourier,
-            bf16_buffer(2, 128, 128),
-            fetch_sems(3),
         ],
-        (9, 10, 11),
     )
     otf_grad = to_eight(otf_grad)
     field_grad = along_sp(
@@ -820,28 +771,21 @@
             psf_grad_kernel,
             (idx, otf_grad, far, con["f"], con["tw_col"], small),
             (0,),
-            [(2, 144, 128)] * 4,
+            [(2, 136, 128)] * 4,
             [
                 pltpu.VMEM((2, 512, 128), F32),
-                bf16_buffer(4, 256, 256),
-                pltpu.VMEM((256, 8), F32),
-                fetch_sems(2),
             ],
-            (3, 4),
         )
     )
     keep, send = call(
         functools.partial(mask_grad_kernel, 2.0 * scale_psf),
         (idx, ids, got, *field_grad, con["m_back"], con["eighth"], pupil),
         (0, 1, 2),
-        [(144, 256)] * 2,
+        [(136, 256)] * 2,
         [
             pltpu.VMEM((2, 128, 512), F32),
             pltpu.VMEM((128, 512), F32),
-            bf16_buffer(4, 512, 512),
-            fetch_sems(1),
         ],
-        (7,),
     )
 
     piece = 128 // lay.y
@@ -849,8 +793,8 @@
         functools.partial(cut_kernel, lay.y),
         (idx, keep, lay.move(send, swap)),
         (0,),
-        [(piece + 16, 256)] * lay.y,
-        [pltpu.VMEM((144, 256), F32)],
+        [(piece + 8, 256)] * lay.y,
+        [pltpu.VMEM((136, 256), F32)],
     )
     total = blocks[0]
     for d in range(1, lay.y):
@@ -876,10 +820,10 @@
         functools.partial(home_kernel, lay.y, pixel_count),
         (idx, total[piece:], near, far),
         (0,),
-        [(N, 256), (32, 9), (1, 32), (9, 32), (1, 1)],
+        [(N, 256), (9, 32), (1, 32), (9, 32), (1, 1)],
         [pltpu.VMEM((256, 512), F32)],
     )
-    return mask_grad, w1_grad, b1_grad.reshape(32), w2_grad, loss.reshape(())
+    return mask_grad, w1_grad.T, b1_grad.reshape(32), w2_grad, loss.reshape(())
 
 
 def solution(mesh):

time: 187 us -> 182 us (0.973)
  local copies, waits for them, and re-layouts: 13.2 us -> 10.3 us
  Pallas kernels: 37.4 us -> 35.5 us
    unnamed x48 -> x43, local copies, waits for them, and re-layouts: 12 us -> 8.88 us
    pallas_call x11, Pallas kernels: 37.4 us -> 35.5 us  [call(): pl.pallas_call(kernel, out_shape=[jax.ShapeDtypeStruct(shape, F32) for sh...]
  transfers between devices with their start and end apart: 35 -> 35, of which waited for: 20 -> 20; matrix products, arithmetic and copies ran while one was open for 1% -> 1% of each run, Pallas kernels for 3% -> 2%
where the time goes in v4:
time: 182 us; the launch traced here: 181 us
  starting transfers between devices  68.4 us (38%)
  waiting for transfers between devices  53.9 us (30%)
  Pallas kernels  35.5 us (20%)
  local copies, waits for them, and re-layouts  10.3 us (6%)
  blocking collectives  7.96 us (4%)
  other arithmetic  2.64 us (1%)
  between operations  2.43 us (1%)
    ppermute x32, starting transfers between devices, move(): return lax.ppermute(x, AXES, pairs)  53 us
    pallas_call x11, Pallas kernels, call(): pl.pallas_call(kernel, out_shape=[jax.ShapeDtypeStruct(shape, F32) for sh...  35.5 us
    ppermute x32, waiting for transfers between devices, move(): return lax.ppermute(x, AXES, pairs)  35.1 us
    all_to_all x3, waiting for transfers between devices, to_eight(): return lax.all_to_all(blocks, ('core', 'sp'), 0, 0, tiled=True)  18.8 us
    all_to_all x3, starting transfers between devices, to_eight(): return lax.all_to_all(blocks, ('core', 'sp'), 0, 0, tiled=True)  15.3 us
    unnamed x43, local copies, waits for them, and re-layouts  8.88 us
    all_to_all x1, blocking collectives, on_device(): lax.all_to_all(jnp.broadcast_to(home, (lay.y, 2, piece, 256)), 'y', 0, 0,...  7.96 us
  transfers between devices with their start and end apart: 35, of which 20 were waited for; matrix products, arithmetic and copies ran while one was open for 1% of the time, Pallas kernels for 2%

profile of v4, /device:TPU:3, one launch (start us, length us, event | category | flops | bytes accessed | tf_op | source)
XLA Modules:
  0.0 181.1 jit_solution(18327766263431949377)
XLA Ops:
  20.1 4.9 %collective-permute-start.8 = (f32[2,128,128]{2,1,0:T(8,128)S(1)}, f32[2,128,128]{2,1,0:T(8,128)S(1)}, u32[]{:S(2)}, u32[]{:S(2)}) collective-permute-start(f32[2,128,128]{2,1,0:T(8,128)S(1)} %get-tuple-element.49), channel_id=1, source_target_pairs={{0,2},{1,3},{2,0},{3,1},{4,6},{5,7},{6,4},{7,5},{8,10},{9,11},{10,... | collective-permute-start | bytes 393224 | tf_op jit(solution)/shard_map/ppermute | solution.py:88
  28.5 3.2 %collective-permute-done.9.b3 = f32[2,128,128]{2,1,0:T(8,128)S(1)} collective-permute-done((f32[2,128,128]{2,1,0:T(8,128)S(1)}, f32[2,128,128]{2,1,0:T(8,128)S(1)}, u32[]{:S(2)}, u32[]{:S(2)}) %collective-permute-start.9) | collective-permute-done | bytes 131104 | tf_op jit(solution)/shard_map/ppermute | solution.py:88
  31.7 2.6 %shard_map.185 = (f32[2,256,512]{2,1,0:T(8,128)S(1)}, f32[8,4,64,128]{3,2,1,0:T(8,128)S(1)}) custom-call(s32[4]{0:T(128)S(1)} %pad_add_fusion.idx, f32[2,128,128]{2,1,0:T(8,128)S(1)} %get-tuple-element.47.b0, f32[2,128,128]{2,1,0:T(8,128)S(1)} %collective-permute-done.7.b1, f32[2,128,128]{2,1,0:T(8,128)S(1)} %collective-permute-done.8.b2, ...), custom_call_target="tpu_custom_call" | custom-call | tf_op jit(solution)/shard_map/pallas_call | solution.py:182
  36.4 5.6 %all-to-all-start = ((f32[8,4,64,128]{3,2,1,0:T(8,128)}), f32[8,4,64,128]{3,2,1,0:T(8,128)S(1)}, u32[]{:S(2)}, u32[]{:S(2)}) async-start(f32[8,4,64,128]{3,2,1,0:T(8,128)} %copy-done.5), calls=%async_computation | async-start | bytes 2097152 | tf_op jit(solution)/shard_map/all_to_all | solution.py:655
  42.0 3.3 %collective-permute-start.11 = (f32[8,128]{1,0:T(8,128)S(1)}, f32[8,128]{1,0:T(8,128)S(1)}, u32[]{:S(2)}, u32[]{:S(2)}) collective-permute-start(f32[8,128]{1,0:T(8,128)S(1)} %get-tuple-element.54), channel_id=1, source_target_pairs={{1,4},{2,5},{3,6},{4,1},{5,2},{6,3},{9,12},{10,13},{11,14},{12,9},... | collective-permute-start | bytes 12296 | tf_op jit(solution)/shard_map/ppermute | solution.py:88
  45.3 8.5 %collective-permute-done.11.refs_3_ = f32[8,128]{1,0:T(8,128)S(1)} collective-permute-done((f32[8,128]{1,0:T(8,128)S(1)}, f32[8,128]{1,0:T(8,128)S(1)}, u32[]{:S(2)}, u32[]{:S(2)}) %collective-permute-start.11) | collective-permute-done | bytes 4128 | tf_op jit(solution)/shard_map/ppermute | solution.py:88
  56.2 3.3 %shard_map.186 = (f32[8,144,128]{2,1,0:T(8,128)S(1)}, f32[2,288,256]{2,1,0:T(8,128)S(1)}) custom-call(s32[4]{0:T(128)S(1)} %pad_add_fusion.idx, f32[8,4,64,128]{3,2,1,0:T(8,128)S(1)} %all-to-all-done.blocks, bf16[12,256,256]{2,1,0:T(8,128)(2,1)S(1)} %copy-done, f32[8,256]{1,0:T(8,128)S(1)} %copy-done.17), custom_call_target="tpu_custom_call" | custom-call | tf_op jit(solution)/shard_map/pallas_call | solution.py:182
  61.1 4.8 %all-to-all-start.1 = ((f32[8,144,128]{2,1,0:T(8,128)}), f32[8,144,128]{2,1,0:T(8,128)S(1)}, u32[]{:S(2)}, u32[]{:S(2)}) async-start(f32[8,144,128]{2,1,0:T(8,128)} %copy-done.8), calls=%async_computation.1 | async-start | bytes 1179648 | tf_op jit(solution)/shard_map/all_to_all | solution.py:655
  66.0 9.2 %all-to-all-done.1.refs_0_ = f32[8,144,128]{2,1,0:T(8,128)S(1)} async-done(((f32[8,144,128]{2,1,0:T(8,128)}), f32[8,144,128]{2,1,0:T(8,128)S(1)}, u32[]{:S(2)}, u32[]{:S(2)}) %all-to-all-start.1) | async-done | bytes 589856 | tf_op jit(solution)/shard_map/all_to_all | solution.py:655
  75.2 13.5 %shard_map.187 = (f32[128,128]{1,0:T(8,128)S(1)}, f32[32,24,128]{2,1,0:T(8,128)S(1)}) custom-call(s32[4]{0:T(128)S(1)} %pad_add_fusion.idx, f32[32,9]{1,0:T(8,128)S(1)} %copy.23.w1, f32[32]{0:T(128)S(1)} %copy-done.19, f32[9,32]{1,0:T(8,128)S(1)} %copy-done.18, f32[8,144,128]{2,1,0:T(8,128)S(1)} %all-to-all-done.1.refs_0_, ...), custom_call_target="tpu_custom_call" | custom-call | tf_op jit(solution)/shard_map/pallas_call | solution.py:182
  89.4 2.7 %collective-permute-start.13 = (f32[128,128]{1,0:T(8,128)S(1)}, f32[128,128]{1,0:T(8,128)S(1)}, u32[]{:S(2)}, u32[]{:S(2)}) collective-permute-start(f32[128,128]{1,0:T(8,128)S(1)} %get-tuple-element.59.refs_0_), channel_id=1, source_target_pairs={{0,2},{1,3},{2,0},{3,1},{4,6},{5,7},{6,4},{7,5},{8,10},{9,11},{10,... | collective-permute-start | bytes 196616 | tf_op jit(solution)/shard_map/ppermute | solution.py:88
  99.3 4.0 %shard_map.188 = f32[8,2,64,128]{3,2,1,0:T(8,128)} custom-call(s32[4]{0:T(128)S(1)} %pad_add_fusion.idx, f32[128,128]{1,0:T(8,128)S(1)} %get-tuple-element.59.refs_0_, f32[128,128]{1,0:T(8,128)S(1)} %collective-permute-done.12.refs_1_, f32[128,128]{1,0:T(8,128)S(1)} %collective-permute-done.13.refs_2_, f32[128,128]{1,0:T(8,128)S(1)} %collective-permute-done.14.refs_3_, ...), custom_call_target="tpu_custom_call" | custom-call | tf_op jit(solution)/shard_map/pallas_call | solution.py:182
  103.3 4.9 %all-to-all-start.2 = ((f32[8,2,64,128]{3,2,1,0:T(8,128)}), f32[8,2,64,128]{3,2,1,0:T(8,128)S(1)}, u32[]{:S(2)}, u32[]{:S(2)}) async-start(f32[8,2,64,128]{3,2,1,0:T(8,128)} %shard_map.188), calls=%async_computation.2 | async-start | bytes 1048576 | tf_op jit(solution)/shard_map/all_to_all | solution.py:655
  109.6 7.2 %all-to-all-done.2.blocks = f32[8,2,64,128]{3,2,1,0:T(8,128)S(1)} async-done(((f32[8,2,64,128]{3,2,1,0:T(8,128)}), f32[8,2,64,128]{3,2,1,0:T(8,128)S(1)}, u32[]{:S(2)}, u32[]{:S(2)}) %all-to-all-start.2) | async-done | bytes 524320 | tf_op jit(solution)/shard_map/all_to_all | solution.py:655
  116.8 2.7 %shard_map.189 = (f32[2,136,128]{2,1,0:T(8,128)S(1)}, f32[2,136,128]{2,1,0:T(8,128)S(1)}, f32[2,136,128]{2,1,0:T(8,128)S(1)}, f32[2,136,128]{2,1,0:T(8,128)S(1)}) custom-call(s32[4]{0:T(128)S(1)} %pad_add_fusion.idx, f32[8,2,64,128]{3,2,1,0:T(8,128)S(1)} %all-to-all-done.2.blocks, f32[2,256,512]{2,1,0:T(8,128)S(1)} %copy-done.7, ...), custom_call_target="tpu_custom_call" | custom-call | tf_op jit(solution)/shard_map/pallas_call | solution.py:182
  119.6 2.7 %collective-permute-start.20 = (f32[2,136,128]{2,1,0:T(8,128)S(1)}, f32[2,136,128]{2,1,0:T(8,128)S(1)}, u32[]{:S(2)}, u32[]{:S(2)}) collective-permute-start(f32[2,136,128]{2,1,0:T(8,128)S(1)} %get-tuple-element.65), channel_id=1, source_target_pairs={{0,2},{1,3},{2,0},{3,1},{4,6},{5,7},{6,4},{7,5},{8,10},{9,11},{10,... | collective-permute-start | bytes 417800 | tf_op jit(solution)/shard_map/ppermute | solution.py:88
  126.5 3.5 %collective-permute-done.21.refs_3_ = f32[2,136,128]{2,1,0:T(8,128)S(1)} collective-permute-done((f32[2,136,128]{2,1,0:T(8,128)S(1)}, f32[2,136,128]{2,1,0:T(8,128)S(1)}, u32[]{:S(2)}, u32[]{:S(2)}) %collective-permute-start.21) | collective-permute-done | bytes 139296 | tf_op jit(solution)/shard_map/ppermute | solution.py:88
  135.0 2.5 %collective-permute-start.24 = (f32[40,256]{1,0:T(8,128)S(1)}, f32[40,256]{1,0:T(8,128)S(1)}, u32[]{:S(2)}, u32[]{:S(2)}) collective-permute-start(f32[40,256]{1,0:T(8,128)S(1)} %get-tuple-element.72), channel_id=1, source_target_pairs={{0,16},{1,17},{2,18},{3,19},{4,20},{5,21},{6,22},{7,23},{8,24},{9,... | collective-permute-start | bytes 122888 | tf_op jit(solution)/shard_map/ppermute | solution.py:88
  141.2 2.5 %collective-permute-done.26 = f32[40,256]{1,0:T(8,128)S(1)} collective-permute-done((f32[40,256]{1,0:T(8,128)S(1)}, f32[40,256]{1,0:T(8,128)S(1)}, u32[]{:S(2)}, u32[]{:S(2)}) %collective-permute-start.26) | collective-permute-done | bytes 40992 | tf_op jit(solution)/shard_map/ppermute | solution.py:88
  143.6 2.9 %collective-permute-start.27 = (f32[40,256]{1,0:T(8,128)S(1)}, f32[40,256]{1,0:T(8,128)S(1)}, u32[]{:S(2)}, u32[]{:S(2)}) collective-permute-start(f32[40,256]{1,0:T(8,128)S(1)} %add.38), channel_id=1, source_target_pairs={{0,32},{1,33},{2,34},{3,35},{4,36},{5,37},{6,38},{7,39},{8,40},{9,... | collective-permute-start | bytes 122888 | tf_op jit(solution)/shard_map/ppermute | solution.py:88
  146.5 5.1 %collective-permute-start.28 = (f32[40,256]{1,0:T(8,128)S(1)}, f32[40,256]{1,0:T(8,128)S(1)}, u32[]{:S(2)}, u32[]{:S(2)}) collective-permute-start(f32[40,256]{1,0:T(8,128)S(1)} %add.38), channel_id=1, source_target_pairs={{0,64},{1,65},{2,66},{3,67},{4,68},{5,69},{6,70},{7,71},{8,72},{9,... | collective-permute-start | bytes 122888 | tf_op jit(solution)/shard_map/ppermute | solution.py:88
  157.6 3.4 %collective-permute-done.30 = f32[32,256]{1,0:T(8,128)S(1)} collective-permute-done((f32[32,256]{1,0:T(8,128)S(1)}, f32[32,256]{1,0:T(8,128)S(1)}, u32[]{:S(2)}, u32[]{:S(2)}) %collective-permute-start.30) | collective-permute-done | bytes 32800 | tf_op jit(solution)/shard_map/ppermute | solution.py:88
  161.0 8.0 %all_to_all.20.refs_0_ = f32[4,2,32,256]{3,2,1,0:T(8,128)S(1)} all-to-all(f32[4,2,32,256]{3,2,1,0:T(8,128)S(1)} %broadcast_in_dim.3), channel_id=1, replica_groups=mesh['grp'=2,'zh'=4,'y'=4,'core'=2,'sp'=4] {'y'}, dimensions={0} | all-to-all | bytes 524288 | tf_op jit(solution)/shard_map/all_to_all | solution.py:813
  169.0 9.2 %collective-permute-start.31 = (f32[4,2,32,256]{3,2,1,0:T(8,128)S(1)}, f32[4,2,32,256]{3,2,1,0:T(8,128)S(1)}, u32[]{:S(2)}, u32[]{:S(2)}) collective-permute-start(f32[4,2,32,256]{3,2,1,0:T(8,128)S(1)} %all_to_all.20.refs_0_), channel_id=1, source_target_pairs={{1,5},{2,6},{5,1},{6,2},{9,13},{10,14},{13,9},{14,10},{17,21},{18,... | collective-permute-start | bytes 786440 | tf_op jit(solution)/shard_map/ppermute | solution.py:88
  (117 shorter events, 58.5 us)
Async XLA Ops:
  5.6 19.6 %collective-permute-start.10 = (f32[136,1024]{1,0:T(8,128)S(1)}, f32[136,1024]{1,0:T(8,128)S(1)}, u32[]{:S(2)}, u32[]{:S(2)}) collective-permute-start(f32[136,1024]{1,0:T(8,128)S(1)} %dynamic-slice_bitcast_fusion), channel_id=1, source_target_pairs={{0,4},{1,5},{2,6},{3,7},{4,0},{5,1},{6,2},{7,3},{8,12},{9,13},{10,... | collective-permute-start | bytes 1671176 | tf_op jit(solution)/shard_map/ppermute | solution.py:88
  7.7 6.4 %collective-permute-start.3 = (f32[128,256]{1,0:T(8,128)S(1)}, f32[128,256]{1,0:T(8,128)S(1)}, u32[]{:S(2)}, u32[]{:S(2)}) collective-permute-start(f32[128,256]{1,0:T(8,128)S(1)} %get-tuple-element.43.refs_0_), channel_id=1, source_target_pairs={{1,5},{2,6},{9,13},{10,14},{17,21},{18,22},{25,29},{26,30},{33,37}... | collective-permute-start | bytes 393224 | tf_op jit(solution)/shard_map/ppermute | solution.py:88
  9.0 6.6 %collective-permute-start.4 = (f32[128,256]{1,0:T(8,128)S(1)}, f32[128,256]{1,0:T(8,128)S(1)}, u32[]{:S(2)}, u32[]{:S(2)}) collective-permute-start(f32[128,256]{1,0:T(8,128)S(1)} %get-tuple-element.44.refs_1_), channel_id=1, source_target_pairs={{1,5},{2,6},{9,13},{10,14},{17,21},{18,22},{25,29},{26,30},{33,37}... | collective-permute-start | bytes 393224 | tf_op jit(solution)/shard_map/ppermute | solution.py:88
  10.4 5.1 %collective-permute-start.5 = (f32[128,256]{1,0:T(8,128)S(1)}, f32[128,256]{1,0:T(8,128)S(1)}, u32[]{:S(2)}, u32[]{:S(2)}) collective-permute-start(f32[128,256]{1,0:T(8,128)S(1)} %collective-permute-done.1.refs_2_), channel_id=1, source_target_pairs={{0,4},{3,7},{8,12},{11,15},{16,20},{19,23},{24,28},{27,31},{32,36}... | collective-permute-start | bytes 393224 | tf_op jit(solution)/shard_map/ppermute | solution.py:88
  11.1 4.4 %collective-permute-start.6 = (f32[128,256]{1,0:T(8,128)S(1)}, f32[128,256]{1,0:T(8,128)S(1)}, u32[]{:S(2)}, u32[]{:S(2)}) collective-permute-start(f32[128,256]{1,0:T(8,128)S(1)} %collective-permute-done.2.refs_3_), channel_id=1, source_target_pairs={{0,4},{3,7},{8,12},{11,15},{16,20},{19,23},{24,28},{27,31},{32,36}... | collective-permute-start | bytes 393224 | tf_op jit(solution)/shard_map/ppermute | solution.py:88
  19.9 7.7 %collective-permute-start.7 = (f32[2,128,128]{2,1,0:T(8,128)S(1)}, f32[2,128,128]{2,1,0:T(8,128)S(1)}, u32[]{:S(2)}, u32[]{:S(2)}) collective-permute-start(f32[2,128,128]{2,1,0:T(8,128)S(1)} %get-tuple-element.48), channel_id=1, source_target_pairs={{0,1},{1,2},{2,3},{3,0},{4,5},{5,6},{6,7},{7,4},{8,9},{9,10},{10,1... | collective-permute-start | bytes 393224 | tf_op jit(solution)/shard_map/ppermute | solution.py:88
  20.1 8.4 %collective-permute-start.8 = (f32[2,128,128]{2,1,0:T(8,128)S(1)}, f32[2,128,128]{2,1,0:T(8,128)S(1)}, u32[]{:S(2)}, u32[]{:S(2)}) collective-permute-start(f32[2,128,128]{2,1,0:T(8,128)S(1)} %get-tuple-element.49), channel_id=1, source_target_pairs={{0,2},{1,3},{2,0},{3,1},{4,6},{5,7},{6,4},{7,5},{8,10},{9,11},{10,... | collective-permute-start | bytes 393224 | tf_op jit(solution)/shard_map/ppermute | solution.py:88
  25.1 6.7 %collective-permute-start.9 = (f32[2,128,128]{2,1,0:T(8,128)S(1)}, f32[2,128,128]{2,1,0:T(8,128)S(1)}, u32[]{:S(2)}, u32[]{:S(2)}) collective-permute-start(f32[2,128,128]{2,1,0:T(8,128)S(1)} %get-tuple-element.50), channel_id=1, source_target_pairs={{0,3},{1,0},{2,1},{3,2},{4,7},{5,4},{6,5},{7,6},{8,11},{9,8},{10,9... | collective-permute-start | bytes 393224 | tf_op jit(solution)/shard_map/ppermute | solution.py:88
  36.4 19.8 %all-to-all-start = ((f32[8,4,64,128]{3,2,1,0:T(8,128)}), f32[8,4,64,128]{3,2,1,0:T(8,128)S(1)}, u32[]{:S(2)}, u32[]{:S(2)}) async-start(f32[8,4,64,128]{3,2,1,0:T(8,128)} %copy-done.5), calls=%async_computation | async-start | bytes 2097152 | tf_op jit(solution)/shard_map/all_to_all | solution.py:655
  42.0 11.8 %collective-permute-start.11 = (f32[8,128]{1,0:T(8,128)S(1)}, f32[8,128]{1,0:T(8,128)S(1)}, u32[]{:S(2)}, u32[]{:S(2)}) collective-permute-start(f32[8,128]{1,0:T(8,128)S(1)} %get-tuple-element.54), channel_id=1, source_target_pairs={{1,4},{2,5},{3,6},{4,1},{5,2},{6,3},{9,12},{10,13},{11,14},{12,9},... | collective-permute-start | bytes 12296 | tf_op jit(solution)/shard_map/ppermute | solution.py:88
  61.1 14.0 %all-to-all-start.1 = ((f32[8,144,128]{2,1,0:T(8,128)}), f32[8,144,128]{2,1,0:T(8,128)S(1)}, u32[]{:S(2)}, u32[]{:S(2)}) async-start(f32[8,144,128]{2,1,0:T(8,128)} %copy-done.8), calls=%async_computation.1 | async-start | bytes 1179648 | tf_op jit(solution)/shard_map/all_to_all | solution.py:655
  89.4 4.8 %collective-permute-start.12 = (f32[128,128]{1,0:T(8,128)S(1)}, f32[128,128]{1,0:T(8,128)S(1)}, u32[]{:S(2)}, u32[]{:S(2)}) collective-permute-start(f32[128,128]{1,0:T(8,128)S(1)} %get-tuple-element.59.refs_0_), channel_id=1, source_target_pairs={{0,1},{1,2},{2,3},{3,0},{4,5},{5,6},{6,7},{7,4},{8,9},{9,10},{10,1... | collective-permute-start | bytes 196616 | tf_op jit(solution)/shard_map/ppermute | solution.py:88
  89.4 4.8 %collective-permute-start.13 = (f32[128,128]{1,0:T(8,128)S(1)}, f32[128,128]{1,0:T(8,128)S(1)}, u32[]{:S(2)}, u32[]{:S(2)}) collective-permute-start(f32[128,128]{1,0:T(8,128)S(1)} %get-tuple-element.59.refs_0_), channel_id=1, source_target_pairs={{0,2},{1,3},{2,0},{3,1},{4,6},{5,7},{6,4},{7,5},{8,10},{9,11},{10,... | collective-permute-start | bytes 196616 | tf_op jit(solution)/shard_map/ppermute | solution.py:88
  92.5 4.8 %collective-permute-start.15 = (f32[128,128]{1,0:T(8,128)S(1)}, f32[128,128]{1,0:T(8,128)S(1)}, u32[]{:S(2)}, u32[]{:S(2)}) collective-permute-start(f32[128,128]{1,0:T(8,128)S(1)} %get-tuple-element.59.refs_0_), channel_id=1, source_target_pairs={{0,4},{1,5},{2,6},{3,7},{4,0},{5,1},{6,2},{7,3},{8,12},{9,13},{10,... | collective-permute-start | bytes 196616 | tf_op jit(solution)/shard_map/ppermute | solution.py:88
  103.3 13.5 %all-to-all-start.2 = ((f32[8,2,64,128]{3,2,1,0:T(8,128)}), f32[8,2,64,128]{3,2,1,0:T(8,128)S(1)}, u32[]{:S(2)}, u32[]{:S(2)}) async-start(f32[8,2,64,128]{3,2,1,0:T(8,128)} %shard_map.188), calls=%async_computation.2 | async-start | bytes 1048576 | tf_op jit(solution)/shard_map/all_to_all | solution.py:655
  119.5 5.8 %collective-permute-start.19 = (f32[2,136,128]{2,1,0:T(8,128)S(1)}, f32[2,136,128]{2,1,0:T(8,128)S(1)}, u32[]{:S(2)}, u32[]{:S(2)}) collective-permute-start(f32[2,136,128]{2,1,0:T(8,128)S(1)} %get-tuple-element.64), channel_id=1, source_target_pairs={{0,1},{1,2},{2,3},{3,0},{4,5},{5,6},{6,7},{7,4},{8,9},{9,10},{10,1... | collective-permute-start | bytes 417800 | tf_op jit(solution)/shard_map/ppermute | solution.py:88
  119.6 6.9 %collective-permute-start.20 = (f32[2,136,128]{2,1,0:T(8,128)S(1)}, f32[2,136,128]{2,1,0:T(8,128)S(1)}, u32[]{:S(2)}, u32[]{:S(2)}) collective-permute-start(f32[2,136,128]{2,1,0:T(8,128)S(1)} %get-tuple-element.65), channel_id=1, source_target_pairs={{0,2},{1,3},{2,0},{3,1},{4,6},{5,7},{6,4},{7,5},{8,10},{9,11},{10,... | collective-permute-start | bytes 417800 | tf_op jit(solution)/shard_map/ppermute | solution.py:88
  122.3 7.7 %collective-permute-start.21 = (f32[2,136,128]{2,1,0:T(8,128)S(1)}, f32[2,136,128]{2,1,0:T(8,128)S(1)}, u32[]{:S(2)}, u32[]{:S(2)}) collective-permute-start(f32[2,136,128]{2,1,0:T(8,128)S(1)} %get-tuple-element.66), channel_id=1, source_target_pairs={{0,3},{1,0},{2,1},{3,2},{4,7},{5,4},{6,5},{7,6},{8,11},{9,8},{10,9... | collective-permute-start | bytes 417800 | tf_op jit(solution)/shard_map/ppermute | solution.py:88
  135.0 4.7 %collective-permute-start.24 = (f32[40,256]{1,0:T(8,128)S(1)}, f32[40,256]{1,0:T(8,128)S(1)}, u32[]{:S(2)}, u32[]{:S(2)}) collective-permute-start(f32[40,256]{1,0:T(8,128)S(1)} %get-tuple-element.72), channel_id=1, source_target_pairs={{0,16},{1,17},{2,18},{3,19},{4,20},{5,21},{6,22},{7,23},{8,24},{9,... | collective-permute-start | bytes 122888 | tf_op jit(solution)/shard_map/ppermute | solution.py:88
  143.6 10.4 %collective-permute-start.27 = (f32[40,256]{1,0:T(8,128)S(1)}, f32[40,256]{1,0:T(8,128)S(1)}, u32[]{:S(2)}, u32[]{:S(2)}) collective-permute-start(f32[40,256]{1,0:T(8,128)S(1)} %add.38), channel_id=1, source_target_pairs={{0,32},{1,33},{2,34},{3,35},{4,36},{5,37},{6,38},{7,39},{8,40},{9,... | collective-permute-start | bytes 122888 | tf_op jit(solution)/shard_map/ppermute | solution.py:88
  146.5 7.5 %collective-permute-start.28 = (f32[40,256]{1,0:T(8,128)S(1)}, f32[40,256]{1,0:T(8,128)S(1)}, u32[]{:S(2)}, u32[]{:S(2)}) collective-permute-start(f32[40,256]{1,0:T(8,128)S(1)} %add.38), channel_id=1, source_target_pairs={{0,64},{1,65},{2,66},{3,67},{4,68},{5,69},{6,70},{7,71},{8,72},{9,... | collective-permute-start | bytes 122888 | tf_op jit(solution)/shard_map/ppermute | solution.py:88
  151.6 4.6 %collective-permute-start.29 = (f32[40,256]{1,0:T(8,128)S(1)}, f32[40,256]{1,0:T(8,128)S(1)}, u32[]{:S(2)}, u32[]{:S(2)}) collective-permute-start(f32[40,256]{1,0:T(8,128)S(1)} %add.38), channel_id=1, source_target_pairs={{0,96},{1,97},{2,98},{3,99},{4,100},{5,101},{6,102},{7,103},{8,104... | collective-permute-start | bytes 122888 | tf_op jit(solution)/shard_map/ppermute | solution.py:88
  156.3 4.7 %collective-permute-start.30 = (f32[32,256]{1,0:T(8,128)S(1)}, f32[32,256]{1,0:T(8,128)S(1)}, u32[]{:S(2)}, u32[]{:S(2)}) collective-permute-start(f32[32,256]{1,0:T(8,128)S(1)} %get-tuple-element.79), channel_id=1, source_target_pairs={{0,1},{3,2},{4,5},{7,6},{8,9},{11,10},{12,13},{15,14},{16,17},{19,... | collective-permute-start | bytes 98312 | tf_op jit(solution)/shard_map/ppermute | solution.py:88
  169.0 10.4 %collective-permute-start.31 = (f32[4,2,32,256]{3,2,1,0:T(8,128)S(1)}, f32[4,2,32,256]{3,2,1,0:T(8,128)S(1)}, u32[]{:S(2)}, u32[]{:S(2)}) collective-permute-start(f32[4,2,32,256]{3,2,1,0:T(8,128)S(1)} %all_to_all.20.refs_0_), channel_id=1, source_target_pairs={{1,5},{2,6},{5,1},{6,2},{9,13},{10,14},{13,9},{14,10},{17,21},{18,... | collective-permute-start | bytes 786440 | tf_op jit(solution)/shard_map/ppermute | solution.py:88
  (32 other events, 416.1 us)

commit v5 on v4

--- a/solution.py
+++ b/solution.py
@@ -213,11 +213,8 @@
 def scene_kernel(idx, scene, other, w, out, strip, edge, image, grid):
     owner = idx[2] == 1
     c = idx[1]
-    rows = jnp.where(
-        owner,
-        scene[0, pl.ds(aligned(15 * c, 8), 136), :],
-        other[...],
-    )
+    part = pl.ds(aligned(15 * c, 8), 136)
+    rows = jnp.where(owner, scene[0, part, :], other[0, part, :])
     strip[...] = rows[:, 256:384]
     edge[...] = jnp.where(c == 0, rows[0:8, 256:384], rows[128:136, 256:384])
     image[...] = jnp.transpose(jnp.where(c == 0, rows[0:128], rows[8:136]))
@@ -420,9 +417,31 @@
 ROWS = 144
 
 
+def row_pair(ref, row):
+    parts = [ref[:, at : at + 8, :] for at in (row, row + 8)]
+    return jnp.concatenate([part.reshape(part.shape[0] * 8, 128) for part in parts], 1)
+
+
+def dot_rows(a, b):
+    return lax.dot_general(a, b, (((1,), (1,)), ((), ())), preferred_element_type=F32)
+
+
+def by_rows(a, b):
+    a_high, a_low = split(a)
+    b_high, b_low = split(b)
+    return dot_rows(a_high, b_high) + (dot_rows(a_high, b_low) + dot_rows(a_low, b_high))
+
+
+def same_rows(x):
+    rows = lax.broadcasted_iota(jnp.int32, x.shape, 0)
+    cols = lax.broadcasted_iota(jnp.int32, x.shape, 1)
+    kept = jnp.where((rows & 7) == (cols & 7), x, 0.0)
+    return jnp.sum(kept.reshape(32, 8, x.shape[1]), 1)
+
+
 def net_kernel(pixel_count, idx, w1, b1, w2, *refs):
     blocks, f, strip, edge, g_out, sums_out = refs[:6]
-    win_taps, g_taps, hidden, sums, acc = refs[6:]
+    win_taps, g_taps, hidden, sums, g_pre = refs[6:]
     target = jnp.where(
         idx[1] == 0,
         jnp.concatenate([edge[...], strip[...]], 0),
@@ -472,36 +491,21 @@
     residual = jnp.where(inside, restored - target, 0.0)
     own = (rows >= 8) & (rows < 136)
     own_residual = jnp.where(own, residual, 0.0)
-    loss = jnp.sum(own_residual * own_residual, 0, keepdims=True)
+    loss = jnp.sum(own_residual * own_residual, keepdims=True)
     g_restored = (2.0 / pixel_count) * residual
     for e in (-1, 0, 1):
         side = moved_lanes(g_restored, -e, lanes)
         for a in (-1, 0, 1):
             g_taps[3 * (a + 1) + e + 1] = jnp.where(inside, moved_rows(side, -a), 0.0)
-    acc[...] = jnp.zeros_like(acc)
-
-    def folded(x):
-        total = x[:8]
-        for row in range(8, x.shape[0], 8):
-            total = total + x[row : row + 8]
-        return total
-
-    for start, step, mine in [(0, 8, False)] + [(8 + 32 * k, 32, True) for k in range(4)] + [
-        (136, 8, False)
-    ]:
-        part = pl.ds(start, step)
-
-        def backward(c, total, part=part, step=step, mine=mine):
-            hid = hidden[c, part, :]
+    for k in range(ROWS // step):
+        part = pl.ds(k * step, step)
+
+        def backward(c, total, part=part):
             gh = w2[0, c] * g_taps[0, part, :]
             for t in range(1, 9):
                 gh = gh + w2[t, c] * g_taps[t, part, :]
-            gp = jnp.where(hid > 0.0, gh, 0.0)
-            if mine:
-                for t in range(9):
-                    acc[c, t] += folded(gp * win_taps[t, part, :])
-                    acc[c, 9 + t] += folded(hid * g_taps[t, part, :])
-                acc[c, 18] += folded(gp)
+            gp = jnp.where(hidden[c, part, :] > 0.0, gh, 0.0)
+            g_pre[c, part, :] = gp
             return tuple(total[t] + w1[c, t] * gp for t in range(9))
 
         total = lax.fori_loop(
@@ -517,9 +521,19 @@
             side = part if side is None else side + part
         g_window = g_window + moved_lanes(side, -e, lanes)
     g_out[...] = g_window[8:136]
-    for c in range(32):
-        sums_out[c, 0:19, :] = jnp.sum(acc[c], 1)
-        sums_out[c, 19:24, :] = jnp.broadcast_to(loss, (5, 128))
+    first, second = None, None
+    for row in range(0, 128, 16):
+        with_taps = jnp.concatenate(
+            [row_pair(win_taps, row + 8), jnp.ones((8, 256), F32)], 0
+        )
+        one = by_rows(row_pair(g_pre, row + 8), with_taps)
+        two = by_rows(row_pair(hidden, row + 8), row_pair(g_taps, row + 8))
+        first = one if first is None else first + one
+        second = two if second is None else second + two
+    sums_out[...] = jnp.zeros_like(sums_out)
+    sums_out[:, 0:80] = same_rows(first)
+    sums_out[:, 80:88] = jnp.broadcast_to(loss * 0.125, (32, 8))
+    sums_out[:, 128:200] = same_rows(second)
 
 
 def otf_grad_kernel(idx, *refs):
@@ -625,11 +639,11 @@
     out[0:256, :] = jnp.zeros((256, 256), F32)
     out[768:1024, :] = jnp.zeros((256, 256), F32)
     out[256:768, :] = jnp.where(central, jnp.transpose(grid[...]), 0.0)
-    flat = jnp.concatenate([small[:, 32 * g : 32 * g + 32] for g in range(3)], 0)
+    flat = jnp.concatenate([small[:, 32 * g : 32 * g + 32] for g in range(4)], 0)
     w1_out[...] = flat[0:9, :]
-    w2_out[...] = flat[9:18, :]
-    b1_out[...] = flat[18:19, :]
-    loss_out[...] = flat[19:20, 0:1] / pixel_count
+    w2_out[...] = flat[16:25, :]
+    b1_out[...] = flat[9:10, :]
+    loss_out[...] = flat[10:11, 0:1] / pixel_count
 
 
 def on_device(lay, phase_mask, height_offsets, sample_ids, wave_ids, scene, w1, b1, w2):
@@ -690,8 +704,9 @@
         for block, inner in zip(pieces, (True, True, False, False))
     ]
 
-    scene, pieces[0] = lax.optimization_barrier((scene, pieces[0]))
-    other = lay.move(lax.dynamic_slice_in_dim(scene[0], 120 * (1 - c), 136, 0), swap)
+    other = lay.move(
+        scene, lambda g, zh, y, c, s: (g, zh, y, 1 - c, s) if c == g else None
+    )
 
     *field, pupil = call(
         pupil_kernel,
@@ -743,17 +758,16 @@
         functools.partial(net_kernel, pixel_count),
         (idx, w1, b1, w2, blurred, con["f"], strip, edge),
         (0, 1, 2, 3),
-        [(128, 128), (32, 24, 128)],
+        [(128, 128), (32, 256)],
         [
             pltpu.VMEM((9, ROWS, 128), F32),
             pltpu.VMEM((9, ROWS, 128), F32),
             pltpu.VMEM((32, ROWS, 128), F32),
             pltpu.VMEM((9, ROWS, 128), F32),
-            pltpu.VMEM((32, 19, 8, 128), F32),
+            pltpu.VMEM((32, ROWS, 128), F32),
         ],
     )
-    small = jnp.sum(sums, 2).reshape(32, 3, 8).transpose(2, 1, 0).reshape(8, 96)
-    small = jnp.pad(small, ((0, 0), (0, 32)))
+    small = jnp.sum(sums.reshape(32, 4, 8, 8), 3).transpose(2, 1, 0).reshape(8, 128)
     g_parts = gathered(g_window)
     (otf_grad,) = call(
         otf_grad_kernel,

time: 182 us -> 179 us (0.984)
  local copies, waits for them, and re-layouts: 10.3 us -> 8.27 us
    ppermute x32, waiting for transfers between devices: 35.1 us -> 33.2 us  [move(): return lax.ppermute(x, AXES, pairs)]
    ppermute x32, starting transfers between devices: 53 us -> 55 us  [move(): return lax.ppermute(x, AXES, pairs)]
    unnamed x43 -> x35, local copies, waits for them, and re-layouts: 8.88 us -> 8.06 us
  transfers between devices with their start and end apart: 35 -> 35, of which waited for: 20 -> 19; matrix products, arithmetic and copies ran while one was open for 1% -> 1% of each run, Pallas kernels for 2% -> 3%
where the time goes in v5:
time: 179 us; the launch traced here: 178 us
  starting transfers between devices  70.2 us (39%)
  waiting for transfers between devices  53 us (30%)
  Pallas kernels  34.3 us (19%)
  blocking collectives  8.59 us (5%)
  local copies, waits for them, and re-layouts  8.27 us (5%)
  between operations  2.32 us (1%)
    ppermute x32, starting transfers between devices, move(): return lax.ppermute(x, AXES, pairs)  55 us
    pallas_call x11, Pallas kernels, call(): pl.pallas_call(kernel, out_shape=[jax.ShapeDtypeStruct(shape, F32) for sh...  34.3 us
    ppermute x32, waiting for transfers between devices, move(): return lax.ppermute(x, AXES, pairs)  33.2 us
    all_to_all x3, waiting for transfers between devices, to_eight(): return lax.all_to_all(blocks, ('core', 'sp'), 0, 0, tiled=True)  19.9 us
    all_to_all x3, starting transfers between devices, to_eight(): return lax.all_to_all(blocks, ('core', 'sp'), 0, 0, tiled=True)  15.2 us
    all_to_all x1, blocking collectives, on_device(): lax.all_to_all(jnp.broadcast_to(home, (lay.y, 2, piece, 256)), 'y', 0, 0,...  8.59 us
    unnamed x35, local copies, waits for them, and re-layouts  8.06 us
  transfers between devices with their start and end apart: 35, of which 19 were waited for; matrix products, arithmetic and copies ran while one was open for 1% of the time, Pallas kernels for 3%

profile of v5, /device:TPU:3, one launch (start us, length us, event | category | flops | bytes accessed | tf_op | source)
XLA Modules:
  0.0 178.3 jit_solution(2842101978676672668)
XLA Ops:
  11.1 2.9 %collective-permute-done.3.refs_4_ = f32[128,256]{1,0:T(8,128)S(1)} collective-permute-done((f32[128,256]{1,0:T(8,128)S(1)}, f32[128,256]{1,0:T(8,128)S(1)}, u32[]{:S(2)}, u32[]{:S(2)}) %collective-permute-start.3) | collective-permute-done | bytes 131104 | tf_op jit(solution)/shard_map/ppermute | solution.py:88
  20.5 4.5 %collective-permute-start.8 = (f32[2,128,128]{2,1,0:T(8,128)S(1)}, f32[2,128,128]{2,1,0:T(8,128)S(1)}, u32[]{:S(2)}, u32[]{:S(2)}) collective-permute-start(f32[2,128,128]{2,1,0:T(8,128)S(1)} %get-tuple-element.46), channel_id=1, source_target_pairs={{0,2},{1,3},{2,0},{3,1},{4,6},{5,7},{6,4},{7,5},{8,10},{9,11},{10,... | collective-permute-start | bytes 393224 | tf_op jit(solution)/shard_map/ppermute | solution.py:88
  26.8 2.4 %shard_map.184 = (f32[8,2,64,128]{3,2,1,0:T(8,128)S(1)}, f32[136,128]{1,0:T(8,128)S(1)}, f32[8,128]{1,0:T(8,128)S(1)}) custom-call(s32[4]{0:T(128)S(1)} %pad_add_fusion.idx, f32[1,256,1024]{2,1,0:T(8,128)S(1)} %copy-done.4, f32[1,256,1024]{2,1,0:T(8,128)S(1)} %collective-permute-done.10.other, bf16[2,1024,1024]{2,1,0:T(8,128)(2,1)S(1)} %copy-done.1), custom_call_target="tpu_custom_call" | custom-call | tf_op jit(solution)/shard_map/pallas_call | solution.py:182
  31.7 2.6 %shard_map.185 = (f32[2,256,512]{2,1,0:T(8,128)S(1)}, f32[8,4,64,128]{3,2,1,0:T(8,128)S(1)}) custom-call(s32[4]{0:T(128)S(1)} %pad_add_fusion.idx, f32[2,128,128]{2,1,0:T(8,128)S(1)} %get-tuple-element.44.b0, f32[2,128,128]{2,1,0:T(8,128)S(1)} %collective-permute-done.7.b1, f32[2,128,128]{2,1,0:T(8,128)S(1)} %collective-permute-done.8.b2, ...), custom_call_target="tpu_custom_call" | custom-call | tf_op jit(solution)/shard_map/pallas_call | solution.py:182
  36.3 5.6 %all-to-all-start = ((f32[8,4,64,128]{3,2,1,0:T(8,128)}), f32[8,4,64,128]{3,2,1,0:T(8,128)S(1)}, u32[]{:S(2)}, u32[]{:S(2)}) async-start(f32[8,4,64,128]{3,2,1,0:T(8,128)} %copy-done.5), calls=%async_computation | async-start | bytes 2097152 | tf_op jit(solution)/shard_map/all_to_all | solution.py:669
  41.9 3.3 %collective-permute-start.11 = (f32[8,128]{1,0:T(8,128)S(1)}, f32[8,128]{1,0:T(8,128)S(1)}, u32[]{:S(2)}, u32[]{:S(2)}) collective-permute-start(f32[8,128]{1,0:T(8,128)S(1)} %get-tuple-element.50), channel_id=1, source_target_pairs={{1,4},{2,5},{3,6},{4,1},{5,2},{6,3},{9,12},{10,13},{11,14},{12,9},... | collective-permute-start | bytes 12296 | tf_op jit(solution)/shard_map/ppermute | solution.py:88
  45.3 8.5 %collective-permute-done.11.refs_3_ = f32[8,128]{1,0:T(8,128)S(1)} collective-permute-done((f32[8,128]{1,0:T(8,128)S(1)}, f32[8,128]{1,0:T(8,128)S(1)}, u32[]{:S(2)}, u32[]{:S(2)}) %collective-permute-start.11) | collective-permute-done | bytes 4128 | tf_op jit(solution)/shard_map/ppermute | solution.py:88
  56.1 4.1 %shard_map.186 = (f32[8,144,128]{2,1,0:T(8,128)}, f32[2,288,256]{2,1,0:T(8,128)S(1)}) custom-call(s32[4]{0:T(128)S(1)} %pad_add_fusion.idx, f32[8,4,64,128]{3,2,1,0:T(8,128)S(1)} %all-to-all-done.blocks, bf16[12,256,256]{2,1,0:T(8,128)(2,1)S(1)} %copy-done, f32[8,256]{1,0:T(8,128)S(1)} %copy-done.13), custom_call_target="tpu_custom_call" | custom-call | tf_op jit(solution)/shard_map/pallas_call | solution.py:182
  60.2 4.6 %all-to-all-start.1 = ((f32[8,144,128]{2,1,0:T(8,128)}), f32[8,144,128]{2,1,0:T(8,128)S(1)}, u32[]{:S(2)}, u32[]{:S(2)}) async-start(f32[8,144,128]{2,1,0:T(8,128)} %get-tuple-element.52), calls=%async_computation.1 | async-start | bytes 1179648 | tf_op jit(solution)/shard_map/all_to_all | solution.py:669
  65.0 9.2 %all-to-all-done.1.refs_0_ = f32[8,144,128]{2,1,0:T(8,128)S(1)} async-done(((f32[8,144,128]{2,1,0:T(8,128)}), f32[8,144,128]{2,1,0:T(8,128)S(1)}, u32[]{:S(2)}, u32[]{:S(2)}) %all-to-all-start.1) | async-done | bytes 589856 | tf_op jit(solution)/shard_map/all_to_all | solution.py:669
  74.1 11.5 %shard_map.187 = (f32[128,128]{1,0:T(8,128)S(1)}, f32[32,256]{1,0:T(8,128)S(1)}) custom-call(s32[4]{0:T(128)S(1)} %pad_add_fusion.idx, f32[32,9]{1,0:T(8,128)S(1)} %copy.23.w1, f32[32]{0:T(128)S(1)} %copy-done.15, f32[9,32]{1,0:T(8,128)S(1)} %copy-done.14, f32[8,144,128]{2,1,0:T(8,128)S(1)} %all-to-all-done.1.refs_0_, bf16[12,256,256]{2,1,0:T(8,128)(2,1)S(1)} %copy-done, ...), custom_call_target="tpu_custom_call" | custom-call | tf_op jit(solution)/shard_map/pallas_call | solution.py:182
  85.8 2.7 %collective-permute-start.13 = (f32[128,128]{1,0:T(8,128)S(1)}, f32[128,128]{1,0:T(8,128)S(1)}, u32[]{:S(2)}, u32[]{:S(2)}) collective-permute-start(f32[128,128]{1,0:T(8,128)S(1)} %get-tuple-element.55.refs_0_), channel_id=1, source_target_pairs={{0,2},{1,3},{2,0},{3,1},{4,6},{5,7},{6,4},{7,5},{8,10},{9,11},{10,... | collective-permute-start | bytes 196616 | tf_op jit(solution)/shard_map/ppermute | solution.py:88
  94.5 4.0 %shard_map.188 = f32[8,2,64,128]{3,2,1,0:T(8,128)} custom-call(s32[4]{0:T(128)S(1)} %pad_add_fusion.idx, f32[128,128]{1,0:T(8,128)S(1)} %get-tuple-element.55.refs_0_, f32[128,128]{1,0:T(8,128)S(1)} %collective-permute-done.12.refs_1_, f32[128,128]{1,0:T(8,128)S(1)} %collective-permute-done.13.refs_2_, f32[128,128]{1,0:T(8,128)S(1)} %collective-permute-done.14.refs_3_, ...), custom_call_target="tpu_custom_call" | custom-call | tf_op jit(solution)/shard_map/pallas_call | solution.py:182
  98.6 4.9 %all-to-all-start.2 = ((f32[8,2,64,128]{3,2,1,0:T(8,128)}), f32[8,2,64,128]{3,2,1,0:T(8,128)S(1)}, u32[]{:S(2)}, u32[]{:S(2)}) async-start(f32[8,2,64,128]{3,2,1,0:T(8,128)} %shard_map.188), calls=%async_computation.2 | async-start | bytes 1048576 | tf_op jit(solution)/shard_map/all_to_all | solution.py:669
  103.7 8.3 %all-to-all-done.2.blocks = f32[8,2,64,128]{3,2,1,0:T(8,128)S(1)} async-done(((f32[8,2,64,128]{3,2,1,0:T(8,128)}), f32[8,2,64,128]{3,2,1,0:T(8,128)S(1)}, u32[]{:S(2)}, u32[]{:S(2)}) %all-to-all-start.2) | async-done | bytes 524320 | tf_op jit(solution)/shard_map/all_to_all | solution.py:669
  113.4 2.7 %shard_map.189 = (f32[2,136,128]{2,1,0:T(8,128)S(1)}, f32[2,136,128]{2,1,0:T(8,128)S(1)}, f32[2,136,128]{2,1,0:T(8,128)S(1)}, f32[2,136,128]{2,1,0:T(8,128)S(1)}) custom-call(s32[4]{0:T(128)S(1)} %pad_add_fusion.idx, f32[8,2,64,128]{3,2,1,0:T(8,128)S(1)} %all-to-all-done.2.blocks, f32[2,256,512]{2,1,0:T(8,128)S(1)} %copy-done.7, ...), custom_call_target="tpu_custom_call" | custom-call | tf_op jit(solution)/shard_map/pallas_call | solution.py:182
  116.2 2.7 %collective-permute-start.20 = (f32[2,136,128]{2,1,0:T(8,128)S(1)}, f32[2,136,128]{2,1,0:T(8,128)S(1)}, u32[]{:S(2)}, u32[]{:S(2)}) collective-permute-start(f32[2,136,128]{2,1,0:T(8,128)S(1)} %get-tuple-element.61), channel_id=1, source_target_pairs={{0,2},{1,3},{2,0},{3,1},{4,6},{5,7},{6,4},{7,5},{8,10},{9,11},{10,... | collective-permute-start | bytes 417800 | tf_op jit(solution)/shard_map/ppermute | solution.py:88
  123.1 3.5 %collective-permute-done.21.refs_3_ = f32[2,136,128]{2,1,0:T(8,128)S(1)} collective-permute-done((f32[2,136,128]{2,1,0:T(8,128)S(1)}, f32[2,136,128]{2,1,0:T(8,128)S(1)}, u32[]{:S(2)}, u32[]{:S(2)}) %collective-permute-start.21) | collective-permute-done | bytes 139296 | tf_op jit(solution)/shard_map/ppermute | solution.py:88
  131.9 2.6 %collective-permute-start.24 = (f32[40,256]{1,0:T(8,128)S(1)}, f32[40,256]{1,0:T(8,128)S(1)}, u32[]{:S(2)}, u32[]{:S(2)}) collective-permute-start(f32[40,256]{1,0:T(8,128)S(1)} %get-tuple-element.68), channel_id=1, source_target_pairs={{0,16},{1,17},{2,18},{3,19},{4,20},{5,21},{6,22},{7,23},{8,24},{9,... | collective-permute-start | bytes 122888 | tf_op jit(solution)/shard_map/ppermute | solution.py:88
  140.7 2.9 %collective-permute-start.27 = (f32[40,256]{1,0:T(8,128)S(1)}, f32[40,256]{1,0:T(8,128)S(1)}, u32[]{:S(2)}, u32[]{:S(2)}) collective-permute-start(f32[40,256]{1,0:T(8,128)S(1)} %add.32), channel_id=1, source_target_pairs={{0,32},{1,33},{2,34},{3,35},{4,36},{5,37},{6,38},{7,39},{8,40},{9,... | collective-permute-start | bytes 122888 | tf_op jit(solution)/shard_map/ppermute | solution.py:88
  143.6 5.1 %collective-permute-start.28 = (f32[40,256]{1,0:T(8,128)S(1)}, f32[40,256]{1,0:T(8,128)S(1)}, u32[]{:S(2)}, u32[]{:S(2)}) collective-permute-start(f32[40,256]{1,0:T(8,128)S(1)} %add.32), channel_id=1, source_target_pairs={{0,64},{1,65},{2,66},{3,67},{4,68},{5,69},{6,70},{7,71},{8,72},{9,... | collective-permute-start | bytes 122888 | tf_op jit(solution)/shard_map/ppermute | solution.py:88
  154.0 3.4 %collective-permute-done.30 = f32[32,256]{1,0:T(8,128)S(1)} collective-permute-done((f32[32,256]{1,0:T(8,128)S(1)}, f32[32,256]{1,0:T(8,128)S(1)}, u32[]{:S(2)}, u32[]{:S(2)}) %collective-permute-start.30) | collective-permute-done | bytes 32800 | tf_op jit(solution)/shard_map/ppermute | solution.py:88
  157.4 8.6 %all_to_all.20.refs_0_ = f32[4,2,32,256]{3,2,1,0:T(8,128)S(1)} all-to-all(f32[4,2,32,256]{3,2,1,0:T(8,128)S(1)} %broadcast_in_dim.3), channel_id=1, replica_groups=mesh['grp'=2,'zh'=4,'y'=4,'core'=2,'sp'=4] {'y'}, dimensions={0} | all-to-all | bytes 524288 | tf_op jit(solution)/shard_map/all_to_all | solution.py:827
  166.0 9.4 %collective-permute-start.31 = (f32[4,2,32,256]{3,2,1,0:T(8,128)S(1)}, f32[4,2,32,256]{3,2,1,0:T(8,128)S(1)}, u32[]{:S(2)}, u32[]{:S(2)}) collective-permute-start(f32[4,2,32,256]{3,2,1,0:T(8,128)S(1)} %all_to_all.20.refs_0_), channel_id=1, source_target_pairs={{1,5},{2,6},{5,1},{6,2},{9,13},{10,14},{13,9},{14,10},{17,21},{18,... | collective-permute-start | bytes 786440 | tf_op jit(solution)/shard_map/ppermute | solution.py:88
  (107 shorter events, 55.9 us)
Async XLA Ops:
  0.6 24.9 %collective-permute-start.10 = (f32[1,256,1024]{2,1,0:T(8,128)}, f32[1,256,1024]{2,1,0:T(8,128)S(1)}, u32[]{:S(2)}, u32[]{:S(2)}) collective-permute-start(f32[1,256,1024]{2,1,0:T(8,128)} %scene.1), channel_id=1, source_target_pairs={{0,4},{1,5},{2,6},{3,7},{8,12},{9,13},{10,14},{11,15},{16,20},{17,... | collective-permute-start | bytes 3145736 | tf_op jit(solution)/shard_map/ppermute | solution.py:88
  7.0 7.0 %collective-permute-start.3 = (f32[128,256]{1,0:T(8,128)S(1)}, f32[128,256]{1,0:T(8,128)S(1)}, u32[]{:S(2)}, u32[]{:S(2)}) collective-permute-start(f32[128,256]{1,0:T(8,128)S(1)} %get-tuple-element.40.refs_0_), channel_id=1, source_target_pairs={{1,5},{2,6},{9,13},{10,14},{17,21},{18,22},{25,29},{26,30},{33,37}... | collective-permute-start | bytes 393224 | tf_op jit(solution)/shard_map/ppermute | solution.py:88
  8.3 7.2 %collective-permute-start.4 = (f32[128,256]{1,0:T(8,128)S(1)}, f32[128,256]{1,0:T(8,128)S(1)}, u32[]{:S(2)}, u32[]{:S(2)}) collective-permute-start(f32[128,256]{1,0:T(8,128)S(1)} %get-tuple-element.41.refs_1_), channel_id=1, source_target_pairs={{1,5},{2,6},{9,13},{10,14},{17,21},{18,22},{25,29},{26,30},{33,37}... | collective-permute-start | bytes 393224 | tf_op jit(solution)/shard_map/ppermute | solution.py:88
  9.8 5.7 %collective-permute-start.5 = (f32[128,256]{1,0:T(8,128)S(1)}, f32[128,256]{1,0:T(8,128)S(1)}, u32[]{:S(2)}, u32[]{:S(2)}) collective-permute-start(f32[128,256]{1,0:T(8,128)S(1)} %collective-permute-done.1.refs_2_), channel_id=1, source_target_pairs={{0,4},{3,7},{8,12},{11,15},{16,20},{19,23},{24,28},{27,31},{32,36}... | collective-permute-start | bytes 393224 | tf_op jit(solution)/shard_map/ppermute | solution.py:88
  10.4 5.0 %collective-permute-start.6 = (f32[128,256]{1,0:T(8,128)S(1)}, f32[128,256]{1,0:T(8,128)S(1)}, u32[]{:S(2)}, u32[]{:S(2)}) collective-permute-start(f32[128,256]{1,0:T(8,128)S(1)} %collective-permute-done.2.refs_3_), channel_id=1, source_target_pairs={{0,4},{3,7},{8,12},{11,15},{16,20},{19,23},{24,28},{27,31},{32,36}... | collective-permute-start | bytes 393224 | tf_op jit(solution)/shard_map/ppermute | solution.py:88
  19.8 9.4 %collective-permute-start.7 = (f32[2,128,128]{2,1,0:T(8,128)S(1)}, f32[2,128,128]{2,1,0:T(8,128)S(1)}, u32[]{:S(2)}, u32[]{:S(2)}) collective-permute-start(f32[2,128,128]{2,1,0:T(8,128)S(1)} %get-tuple-element.45), channel_id=1, source_target_pairs={{0,1},{1,2},{2,3},{3,0},{4,5},{5,6},{6,7},{7,4},{8,9},{9,10},{10,1... | collective-permute-start | bytes 393224 | tf_op jit(solution)/shard_map/ppermute | solution.py:88
  20.5 8.8 %collective-permute-start.8 = (f32[2,128,128]{2,1,0:T(8,128)S(1)}, f32[2,128,128]{2,1,0:T(8,128)S(1)}, u32[]{:S(2)}, u32[]{:S(2)}) collective-permute-start(f32[2,128,128]{2,1,0:T(8,128)S(1)} %get-tuple-element.46), channel_id=1, source_target_pairs={{0,2},{1,3},{2,0},{3,1},{4,6},{5,7},{6,4},{7,5},{8,10},{9,11},{10,... | collective-permute-start | bytes 393224 | tf_op jit(solution)/shard_map/ppermute | solution.py:88
  25.0 6.7 %collective-permute-start.9 = (f32[2,128,128]{2,1,0:T(8,128)S(1)}, f32[2,128,128]{2,1,0:T(8,128)S(1)}, u32[]{:S(2)}, u32[]{:S(2)}) collective-permute-start(f32[2,128,128]{2,1,0:T(8,128)S(1)} %get-tuple-element.47), channel_id=1, source_target_pairs={{0,3},{1,0},{2,1},{3,2},{4,7},{5,4},{6,5},{7,6},{8,11},{9,8},{10,9... | collective-permute-start | bytes 393224 | tf_op jit(solution)/shard_map/ppermute | solution.py:88
  36.3 19.8 %all-to-all-start = ((f32[8,4,64,128]{3,2,1,0:T(8,128)}), f32[8,4,64,128]{3,2,1,0:T(8,128)S(1)}, u32[]{:S(2)}, u32[]{:S(2)}) async-start(f32[8,4,64,128]{3,2,1,0:T(8,128)} %copy-done.5), calls=%async_computation | async-start | bytes 2097152 | tf_op jit(solution)/shard_map/all_to_all | solution.py:669
  41.9 11.8 %collective-permute-start.11 = (f32[8,128]{1,0:T(8,128)S(1)}, f32[8,128]{1,0:T(8,128)S(1)}, u32[]{:S(2)}, u32[]{:S(2)}) collective-permute-start(f32[8,128]{1,0:T(8,128)S(1)} %get-tuple-element.50), channel_id=1, source_target_pairs={{1,4},{2,5},{3,6},{4,1},{5,2},{6,3},{9,12},{10,13},{11,14},{12,9},... | collective-permute-start | bytes 12296 | tf_op jit(solution)/shard_map/ppermute | solution.py:88
  60.2 13.9 %all-to-all-start.1 = ((f32[8,144,128]{2,1,0:T(8,128)}), f32[8,144,128]{2,1,0:T(8,128)S(1)}, u32[]{:S(2)}, u32[]{:S(2)}) async-start(f32[8,144,128]{2,1,0:T(8,128)} %get-tuple-element.52), calls=%async_computation.1 | async-start | bytes 1179648 | tf_op jit(solution)/shard_map/all_to_all | solution.py:669
  85.7 4.8 %collective-permute-start.12 = (f32[128,128]{1,0:T(8,128)S(1)}, f32[128,128]{1,0:T(8,128)S(1)}, u32[]{:S(2)}, u32[]{:S(2)}) collective-permute-start(f32[128,128]{1,0:T(8,128)S(1)} %get-tuple-element.55.refs_0_), channel_id=1, source_target_pairs={{0,1},{1,2},{2,3},{3,0},{4,5},{5,6},{6,7},{7,4},{8,9},{9,10},{10,1... | collective-permute-start | bytes 196616 | tf_op jit(solution)/shard_map/ppermute | solution.py:88
  85.8 4.8 %collective-permute-start.13 = (f32[128,128]{1,0:T(8,128)S(1)}, f32[128,128]{1,0:T(8,128)S(1)}, u32[]{:S(2)}, u32[]{:S(2)}) collective-permute-start(f32[128,128]{1,0:T(8,128)S(1)} %get-tuple-element.55.refs_0_), channel_id=1, source_target_pairs={{0,2},{1,3},{2,0},{3,1},{4,6},{5,7},{6,4},{7,5},{8,10},{9,11},{10,... | collective-permute-start | bytes 196616 | tf_op jit(solution)/shard_map/ppermute | solution.py:88
  88.4 4.3 %collective-permute-start.14 = (f32[128,128]{1,0:T(8,128)S(1)}, f32[128,128]{1,0:T(8,128)S(1)}, u32[]{:S(2)}, u32[]{:S(2)}) collective-permute-start(f32[128,128]{1,0:T(8,128)S(1)} %get-tuple-element.55.refs_0_), channel_id=1, source_target_pairs={{0,3},{1,0},{2,1},{3,2},{4,7},{5,4},{6,5},{7,6},{8,11},{9,8},{10,9... | collective-permute-start | bytes 196616 | tf_op jit(solution)/shard_map/ppermute | solution.py:88
  88.8 4.8 %collective-permute-start.15 = (f32[128,128]{1,0:T(8,128)S(1)}, f32[128,128]{1,0:T(8,128)S(1)}, u32[]{:S(2)}, u32[]{:S(2)}) collective-permute-start(f32[128,128]{1,0:T(8,128)S(1)} %get-tuple-element.55.refs_0_), channel_id=1, source_target_pairs={{0,4},{1,5},{2,6},{3,7},{4,0},{5,1},{6,2},{7,3},{8,12},{9,13},{10,... | collective-permute-start | bytes 196616 | tf_op jit(solution)/shard_map/ppermute | solution.py:88
  98.6 13.5 %all-to-all-start.2 = ((f32[8,2,64,128]{3,2,1,0:T(8,128)}), f32[8,2,64,128]{3,2,1,0:T(8,128)S(1)}, u32[]{:S(2)}, u32[]{:S(2)}) async-start(f32[8,2,64,128]{3,2,1,0:T(8,128)} %shard_map.188), calls=%async_computation.2 | async-start | bytes 1048576 | tf_op jit(solution)/shard_map/all_to_all | solution.py:669
  116.1 5.8 %collective-permute-start.19 = (f32[2,136,128]{2,1,0:T(8,128)S(1)}, f32[2,136,128]{2,1,0:T(8,128)S(1)}, u32[]{:S(2)}, u32[]{:S(2)}) collective-permute-start(f32[2,136,128]{2,1,0:T(8,128)S(1)} %get-tuple-element.60), channel_id=1, source_target_pairs={{0,1},{1,2},{2,3},{3,0},{4,5},{5,6},{6,7},{7,4},{8,9},{9,10},{10,1... | collective-permute-start | bytes 417800 | tf_op jit(solution)/shard_map/ppermute | solution.py:88
  116.2 6.9 %collective-permute-start.20 = (f32[2,136,128]{2,1,0:T(8,128)S(1)}, f32[2,136,128]{2,1,0:T(8,128)S(1)}, u32[]{:S(2)}, u32[]{:S(2)}) collective-permute-start(f32[2,136,128]{2,1,0:T(8,128)S(1)} %get-tuple-element.61), channel_id=1, source_target_pairs={{0,2},{1,3},{2,0},{3,1},{4,6},{5,7},{6,4},{7,5},{8,10},{9,11},{10,... | collective-permute-start | bytes 417800 | tf_op jit(solution)/shard_map/ppermute | solution.py:88
  118.9 7.7 %collective-permute-start.21 = (f32[2,136,128]{2,1,0:T(8,128)S(1)}, f32[2,136,128]{2,1,0:T(8,128)S(1)}, u32[]{:S(2)}, u32[]{:S(2)}) collective-permute-start(f32[2,136,128]{2,1,0:T(8,128)S(1)} %get-tuple-element.62), channel_id=1, source_target_pairs={{0,3},{1,0},{2,1},{3,2},{4,7},{5,4},{6,5},{7,6},{8,11},{9,8},{10,9... | collective-permute-start | bytes 417800 | tf_op jit(solution)/shard_map/ppermute | solution.py:88
  131.9 4.5 %collective-permute-start.24 = (f32[40,256]{1,0:T(8,128)S(1)}, f32[40,256]{1,0:T(8,128)S(1)}, u32[]{:S(2)}, u32[]{:S(2)}) collective-permute-start(f32[40,256]{1,0:T(8,128)S(1)} %get-tuple-element.68), channel_id=1, source_target_pairs={{0,16},{1,17},{2,18},{3,19},{4,20},{5,21},{6,22},{7,23},{8,24},{9,... | collective-permute-start | bytes 122888 | tf_op jit(solution)/shard_map/ppermute | solution.py:88
  140.7 10.4 %collective-permute-start.27 = (f32[40,256]{1,0:T(8,128)S(1)}, f32[40,256]{1,0:T(8,128)S(1)}, u32[]{:S(2)}, u32[]{:S(2)}) collective-permute-start(f32[40,256]{1,0:T(8,128)S(1)} %add.32), channel_id=1, source_target_pairs={{0,32},{1,33},{2,34},{3,35},{4,36},{5,37},{6,38},{7,39},{8,40},{9,... | collective-permute-start | bytes 122888 | tf_op jit(solution)/shard_map/ppermute | solution.py:88
  143.6 7.5 %collective-permute-start.28 = (f32[40,256]{1,0:T(8,128)S(1)}, f32[40,256]{1,0:T(8,128)S(1)}, u32[]{:S(2)}, u32[]{:S(2)}) collective-permute-start(f32[40,256]{1,0:T(8,128)S(1)} %add.32), channel_id=1, source_target_pairs={{0,64},{1,65},{2,66},{3,67},{4,68},{5,69},{6,70},{7,71},{8,72},{9,... | collective-permute-start | bytes 122888 | tf_op jit(solution)/shard_map/ppermute | solution.py:88
  152.7 4.7 %collective-permute-start.30 = (f32[32,256]{1,0:T(8,128)S(1)}, f32[32,256]{1,0:T(8,128)S(1)}, u32[]{:S(2)}, u32[]{:S(2)}) collective-permute-start(f32[32,256]{1,0:T(8,128)S(1)} %get-tuple-element.75), channel_id=1, source_target_pairs={{0,1},{3,2},{4,5},{7,6},{8,9},{11,10},{12,13},{15,14},{16,17},{19,... | collective-permute-start | bytes 98312 | tf_op jit(solution)/shard_map/ppermute | solution.py:88
  166.0 10.5 %collective-permute-start.31 = (f32[4,2,32,256]{3,2,1,0:T(8,128)S(1)}, f32[4,2,32,256]{3,2,1,0:T(8,128)S(1)}, u32[]{:S(2)}, u32[]{:S(2)}) collective-permute-start(f32[4,2,32,256]{3,2,1,0:T(8,128)S(1)} %all_to_all.20.refs_0_), channel_id=1, source_target_pairs={{1,5},{2,6},{5,1},{6,2},{9,13},{10,14},{13,9},{14,10},{17,21},{18,... | collective-permute-start | bytes 786440 | tf_op jit(solution)/shard_map/ppermute | solution.py:88
  (28 other events, 310.6 us)

commit v6 on v5

--- a/solution.py
+++ b/solution.py
@@ -464,7 +464,7 @@
         side = moved_lanes(window, e, lanes)
         for a in (-1, 0, 1):
             win_taps[3 * (a + 1) + e + 1] = moved_rows(side, a)
-    step = 24
+    step = 48
     for k in range(ROWS // step):
         part = pl.ds(k * step, step)
 
@@ -477,7 +477,7 @@
             return tuple(total[t] + w2[t, c] * hid for t in range(9))
 
         total = lax.fori_loop(
-            0, 32, forward, tuple(jnp.zeros((step, 128), F32) for _ in range(9)), unroll=4
+            0, 32, forward, tuple(jnp.zeros((step, 128), F32) for _ in range(9)), unroll=32
         )
         for t in range(9):
             sums[t, part, :] = total[t]
@@ -509,7 +509,7 @@
             return tuple(total[t] + w1[c, t] * gp for t in range(9))
 
         total = lax.fori_loop(
-            0, 32, backward, tuple(jnp.zeros((step, 128), F32) for _ in range(9)), unroll=4
+            0, 32, backward, tuple(jnp.zeros((step, 128), F32) for _ in range(9)), unroll=32
         )
         for t in range(9):
             sums[t, part, :] = total[t]
@@ -704,9 +704,6 @@
         for block, inner in zip(pieces, (True, True, False, False))
     ]
 
-    other = lay.move(
-        scene, lambda g, zh, y, c, s: (g, zh, y, 1 - c, s) if c == g else None
-    )
 
     *field, pupil = call(
         pupil_kernel,
@@ -714,6 +711,10 @@
         (0,),
         [(2, 128, 128)] * 4 + [(2, 128, 512)],
         [pltpu.VMEM((2, 128, 512), F32)],
+    )
+    scene, pupil = lax.optimization_barrier((scene, pupil))
+    other = lay.move(
+        scene, lambda g, zh, y, c, s: (g, zh, y, 1 - c, s) if c == g else None
     )
     field = along_sp(field)
 

time: 179 us -> 178 us (level)
  Pallas kernels: 34.3 us -> 31.5 us
  local copies, waits for them, and re-layouts: 8.27 us -> 10.4 us
    pallas_call x11, Pallas kernels: 34.3 us -> 31.5 us  [call(): pl.pallas_call(kernel, out_shape=[jax.ShapeDtypeStruct(shape, F32) for sh...]
    unnamed x35 -> x41, local copies, waits for them, and re-layouts: 8.06 us -> 10.2 us
  transfers between devices with their start and end apart: 35 -> 35, of which waited for: 19 -> 19; matrix products, arithmetic and copies ran while one was open for 1% -> 0% of each run, Pallas kernels for 3% -> 1%
where the time goes in v6:
time: 178 us; the launch traced here: 177 us
  starting transfers between devices  70.8 us (40%)
  waiting for transfers between devices  51.9 us (29%)
  Pallas kernels  31.5 us (18%)
  local copies, waits for them, and re-layouts  10.4 us (6%)
  blocking collectives  8.6 us (5%)
  between operations  2.33 us (1%)
    ppermute x32, starting transfers between devices, move(): return lax.ppermute(x, AXES, pairs)  54.5 us
    ppermute x32, waiting for transfers between devices, move(): return lax.ppermute(x, AXES, pairs)  32.1 us
    pallas_call x11, Pallas kernels, call(): pl.pallas_call(kernel, out_shape=[jax.ShapeDtypeStruct(shape, F32) for sh...  31.5 us
    all_to_all x3, waiting for transfers between devices, to_eight(): return lax.all_to_all(blocks, ('core', 'sp'), 0, 0, tiled=True)  19.9 us
    all_to_all x3, starting transfers between devices, to_eight(): return lax.all_to_all(blocks, ('core', 'sp'), 0, 0, tiled=True)  16.4 us
    unnamed x41, local copies, waits for them, and re-layouts  10.2 us
    all_to_all x1, blocking collectives, on_device(): lax.all_to_all(jnp.broadcast_to(home, (lay.y, 2, piece, 256)), 'y', 0, 0,...  8.6 us
  transfers between devices with their start and end apart: 35, of which 19 were waited for; matrix products, arithmetic and copies ran while one was open for 0% of the time, Pallas kernels for 1%

profile of v6, /device:TPU:3, one launch (start us, length us, event | category | flops | bytes accessed | tf_op | source)
XLA Modules:
  0.0 177.3 jit_solution(9074774874895974759)
XLA Ops:
  9.8 2.8 %collective-permute-done.3.refs_4_ = f32[128,256]{1,0:T(8,128)S(1)} collective-permute-done((f32[128,256]{1,0:T(8,128)S(1)}, f32[128,256]{1,0:T(8,128)S(1)}, u32[]{:S(2)}, u32[]{:S(2)}) %collective-permute-start.3) | collective-permute-done | bytes 131104 | tf_op jit(solution)/shard_map/ppermute | solution.py:88
  20.8 4.9 %collective-permute-start.8 = (f32[2,128,128]{2,1,0:T(8,128)S(1)}, f32[2,128,128]{2,1,0:T(8,128)S(1)}, u32[]{:S(2)}, u32[]{:S(2)}) collective-permute-start(f32[2,128,128]{2,1,0:T(8,128)S(1)} %get-tuple-element.48), channel_id=1, source_target_pairs={{0,2},{1,3},{2,0},{3,1},{4,6},{5,7},{6,4},{7,5},{8,10},{9,11},{10,... | collective-permute-start | bytes 393224 | tf_op jit(solution)/shard_map/ppermute | solution.py:88
  27.1 2.4 %shard_map.184 = (f32[8,2,64,128]{3,2,1,0:T(8,128)S(1)}, f32[136,128]{1,0:T(8,128)S(1)}, f32[8,128]{1,0:T(8,128)S(1)}) custom-call(s32[4]{0:T(128)S(1)} %pad_add_fusion.idx, f32[1,256,1024]{2,1,0:T(8,128)S(1)} %copy-done.4, f32[1,256,1024]{2,1,0:T(8,128)S(1)} %collective-permute-done.10.other, bf16[2,1024,1024]{2,1,0:T(8,128)(2,1)S(1)} %copy-done.1), custom_call_target="tpu_custom_call" | custom-call | tf_op jit(solution)/shard_map/pallas_call | solution.py:182
  31.4 2.6 %shard_map.185 = (f32[2,256,512]{2,1,0:T(8,128)S(1)}, f32[8,4,64,128]{3,2,1,0:T(8,128)S(1)}) custom-call(s32[4]{0:T(128)S(1)} %pad_add_fusion.idx, f32[2,128,128]{2,1,0:T(8,128)S(1)} %get-tuple-element.46.b0, f32[2,128,128]{2,1,0:T(8,128)S(1)} %collective-permute-done.7.b1, f32[2,128,128]{2,1,0:T(8,128)S(1)} %collective-permute-done.8.b2, ...), custom_call_target="tpu_custom_call" | custom-call | tf_op jit(solution)/shard_map/pallas_call | solution.py:182
  36.0 6.7 %all-to-all-start = ((f32[8,4,64,128]{3,2,1,0:T(8,128)}), f32[8,4,64,128]{3,2,1,0:T(8,128)S(1)}, u32[]{:S(2)}, u32[]{:S(2)}) async-start(f32[8,4,64,128]{3,2,1,0:T(8,128)} %copy-done.5), calls=%async_computation | async-start | bytes 2097152 | tf_op jit(solution)/shard_map/all_to_all | solution.py:669
  42.7 3.3 %collective-permute-start.11 = (f32[8,128]{1,0:T(8,128)S(1)}, f32[8,128]{1,0:T(8,128)S(1)}, u32[]{:S(2)}, u32[]{:S(2)}) collective-permute-start(f32[8,128]{1,0:T(8,128)S(1)} %get-tuple-element.54), channel_id=1, source_target_pairs={{1,4},{2,5},{3,6},{4,1},{5,2},{6,3},{9,12},{10,13},{11,14},{12,9},... | collective-permute-start | bytes 12296 | tf_op jit(solution)/shard_map/ppermute | solution.py:88
  46.0 8.5 %collective-permute-done.11.refs_3_ = f32[8,128]{1,0:T(8,128)S(1)} collective-permute-done((f32[8,128]{1,0:T(8,128)S(1)}, f32[8,128]{1,0:T(8,128)S(1)}, u32[]{:S(2)}, u32[]{:S(2)}) %collective-permute-start.11) | collective-permute-done | bytes 4128 | tf_op jit(solution)/shard_map/ppermute | solution.py:88
  56.8 3.3 %shard_map.186 = (f32[8,144,128]{2,1,0:T(8,128)S(1)}, f32[2,288,256]{2,1,0:T(8,128)S(1)}) custom-call(s32[4]{0:T(128)S(1)} %pad_add_fusion.idx, f32[8,4,64,128]{3,2,1,0:T(8,128)S(1)} %all-to-all-done.blocks, bf16[12,256,256]{2,1,0:T(8,128)(2,1)S(1)} %copy-done, f32[8,256]{1,0:T(8,128)S(1)} %copy-done.16), custom_call_target="tpu_custom_call" | custom-call | tf_op jit(solution)/shard_map/pallas_call | solution.py:182
  61.8 4.8 %all-to-all-start.1 = ((f32[8,144,128]{2,1,0:T(8,128)}), f32[8,144,128]{2,1,0:T(8,128)S(1)}, u32[]{:S(2)}, u32[]{:S(2)}) async-start(f32[8,144,128]{2,1,0:T(8,128)} %copy-done.8), calls=%async_computation.1 | async-start | bytes 1179648 | tf_op jit(solution)/shard_map/all_to_all | solution.py:669
  66.7 9.2 %all-to-all-done.1.refs_0_ = f32[8,144,128]{2,1,0:T(8,128)S(1)} async-done(((f32[8,144,128]{2,1,0:T(8,128)}), f32[8,144,128]{2,1,0:T(8,128)S(1)}, u32[]{:S(2)}, u32[]{:S(2)}) %all-to-all-start.1) | async-done | bytes 589856 | tf_op jit(solution)/shard_map/all_to_all | solution.py:669
  75.9 9.4 %shard_map.187 = (f32[128,128]{1,0:T(8,128)S(1)}, f32[32,256]{1,0:T(8,128)S(1)}) custom-call(s32[4]{0:T(128)S(1)} %pad_add_fusion.idx, f32[32,9]{1,0:T(8,128)S(1)} %copy.23.w1, f32[32]{0:T(128)S(1)} %copy-done.18, f32[9,32]{1,0:T(8,128)S(1)} %copy-done.17, f32[8,144,128]{2,1,0:T(8,128)S(1)} %all-to-all-done.1.refs_0_, bf16[12,256,256]{2,1,0:T(8,128)(2,1)S(1)} %copy-done, ...), custom_call_target="tpu_custom_call" | custom-call | tf_op jit(solution)/shard_map/pallas_call | solution.py:182
  85.4 2.7 %collective-permute-start.13 = (f32[128,128]{1,0:T(8,128)S(1)}, f32[128,128]{1,0:T(8,128)S(1)}, u32[]{:S(2)}, u32[]{:S(2)}) collective-permute-start(f32[128,128]{1,0:T(8,128)S(1)} %get-tuple-element.59.refs_0_), channel_id=1, source_target_pairs={{0,2},{1,3},{2,0},{3,1},{4,6},{5,7},{6,4},{7,5},{8,10},{9,11},{10,... | collective-permute-start | bytes 196616 | tf_op jit(solution)/shard_map/ppermute | solution.py:88
  95.2 4.1 %shard_map.188 = f32[8,2,64,128]{3,2,1,0:T(8,128)} custom-call(s32[4]{0:T(128)S(1)} %pad_add_fusion.idx, f32[128,128]{1,0:T(8,128)S(1)} %get-tuple-element.59.refs_0_, f32[128,128]{1,0:T(8,128)S(1)} %collective-permute-done.12.refs_1_, f32[128,128]{1,0:T(8,128)S(1)} %collective-permute-done.13.refs_2_, f32[128,128]{1,0:T(8,128)S(1)} %collective-permute-done.14.refs_3_, ...), custom_call_target="tpu_custom_call" | custom-call | tf_op jit(solution)/shard_map/pallas_call | solution.py:182
  99.3 4.9 %all-to-all-start.2 = ((f32[8,2,64,128]{3,2,1,0:T(8,128)}), f32[8,2,64,128]{3,2,1,0:T(8,128)S(1)}, u32[]{:S(2)}, u32[]{:S(2)}) async-start(f32[8,2,64,128]{3,2,1,0:T(8,128)} %shard_map.188), calls=%async_computation.2 | async-start | bytes 1048576 | tf_op jit(solution)/shard_map/all_to_all | solution.py:669
  104.4 8.3 %all-to-all-done.2.blocks = f32[8,2,64,128]{3,2,1,0:T(8,128)S(1)} async-done(((f32[8,2,64,128]{3,2,1,0:T(8,128)}), f32[8,2,64,128]{3,2,1,0:T(8,128)S(1)}, u32[]{:S(2)}, u32[]{:S(2)}) %all-to-all-start.2) | async-done | bytes 524320 | tf_op jit(solution)/shard_map/all_to_all | solution.py:669
  112.8 2.7 %shard_map.189 = (f32[2,136,128]{2,1,0:T(8,128)S(1)}, f32[2,136,128]{2,1,0:T(8,128)S(1)}, f32[2,136,128]{2,1,0:T(8,128)S(1)}, f32[2,136,128]{2,1,0:T(8,128)S(1)}) custom-call(s32[4]{0:T(128)S(1)} %pad_add_fusion.idx, f32[8,2,64,128]{3,2,1,0:T(8,128)S(1)} %all-to-all-done.2.blocks, f32[2,256,512]{2,1,0:T(8,128)S(1)} %copy-done.7, ...), custom_call_target="tpu_custom_call" | custom-call | tf_op jit(solution)/shard_map/pallas_call | solution.py:182
  115.6 2.7 %collective-permute-start.20 = (f32[2,136,128]{2,1,0:T(8,128)S(1)}, f32[2,136,128]{2,1,0:T(8,128)S(1)}, u32[]{:S(2)}, u32[]{:S(2)}) collective-permute-start(f32[2,136,128]{2,1,0:T(8,128)S(1)} %get-tuple-element.65), channel_id=1, source_target_pairs={{0,2},{1,3},{2,0},{3,1},{4,6},{5,7},{6,4},{7,5},{8,10},{9,11},{10,... | collective-permute-start | bytes 417800 | tf_op jit(solution)/shard_map/ppermute | solution.py:88
  122.1 3.6 %collective-permute-done.21.refs_3_ = f32[2,136,128]{2,1,0:T(8,128)S(1)} collective-permute-done((f32[2,136,128]{2,1,0:T(8,128)S(1)}, f32[2,136,128]{2,1,0:T(8,128)S(1)}, u32[]{:S(2)}, u32[]{:S(2)}) %collective-permute-start.21) | collective-permute-done | bytes 139296 | tf_op jit(solution)/shard_map/ppermute | solution.py:88
  130.8 2.5 %collective-permute-start.24 = (f32[40,256]{1,0:T(8,128)S(1)}, f32[40,256]{1,0:T(8,128)S(1)}, u32[]{:S(2)}, u32[]{:S(2)}) collective-permute-start(f32[40,256]{1,0:T(8,128)S(1)} %get-tuple-element.72), channel_id=1, source_target_pairs={{0,16},{1,17},{2,18},{3,19},{4,20},{5,21},{6,22},{7,23},{8,24},{9,... | collective-permute-start | bytes 122888 | tf_op jit(solution)/shard_map/ppermute | solution.py:88
  139.4 2.9 %collective-permute-start.27 = (f32[40,256]{1,0:T(8,128)S(1)}, f32[40,256]{1,0:T(8,128)S(1)}, u32[]{:S(2)}, u32[]{:S(2)}) collective-permute-start(f32[40,256]{1,0:T(8,128)S(1)} %add.32), channel_id=1, source_target_pairs={{0,32},{1,33},{2,34},{3,35},{4,36},{5,37},{6,38},{7,39},{8,40},{9,... | collective-permute-start | bytes 122888 | tf_op jit(solution)/shard_map/ppermute | solution.py:88
  142.3 5.1 %collective-permute-start.28 = (f32[40,256]{1,0:T(8,128)S(1)}, f32[40,256]{1,0:T(8,128)S(1)}, u32[]{:S(2)}, u32[]{:S(2)}) collective-permute-start(f32[40,256]{1,0:T(8,128)S(1)} %add.32), channel_id=1, source_target_pairs={{0,64},{1,65},{2,66},{3,67},{4,68},{5,69},{6,70},{7,71},{8,72},{9,... | collective-permute-start | bytes 122888 | tf_op jit(solution)/shard_map/ppermute | solution.py:88
  152.9 3.4 %collective-permute-done.30 = f32[32,256]{1,0:T(8,128)S(1)} collective-permute-done((f32[32,256]{1,0:T(8,128)S(1)}, f32[32,256]{1,0:T(8,128)S(1)}, u32[]{:S(2)}, u32[]{:S(2)}) %collective-permute-start.30) | collective-permute-done | bytes 32800 | tf_op jit(solution)/shard_map/ppermute | solution.py:88
  156.3 8.6 %all_to_all.20.refs_0_ = f32[4,2,32,256]{3,2,1,0:T(8,128)S(1)} all-to-all(f32[4,2,32,256]{3,2,1,0:T(8,128)S(1)} %broadcast_in_dim.3), channel_id=1, replica_groups=mesh['grp'=2,'zh'=4,'y'=4,'core'=2,'sp'=4] {'y'}, dimensions={0} | all-to-all | bytes 524288 | tf_op jit(solution)/shard_map/all_to_all | solution.py:828
  164.9 9.5 %collective-permute-start.31 = (f32[4,2,32,256]{3,2,1,0:T(8,128)S(1)}, f32[4,2,32,256]{3,2,1,0:T(8,128)S(1)}, u32[]{:S(2)}, u32[]{:S(2)}) collective-permute-start(f32[4,2,32,256]{3,2,1,0:T(8,128)S(1)} %all_to_all.20.refs_0_), channel_id=1, source_target_pairs={{1,5},{2,6},{5,1},{6,2},{9,13},{10,14},{13,9},{14,10},{17,21},{18,... | collective-permute-start | bytes 786440 | tf_op jit(solution)/shard_map/ppermute | solution.py:88
  (113 shorter events, 56.0 us)
Async XLA Ops:
  5.7 6.9 %collective-permute-start.3 = (f32[128,256]{1,0:T(8,128)S(1)}, f32[128,256]{1,0:T(8,128)S(1)}, u32[]{:S(2)}, u32[]{:S(2)}) collective-permute-start(f32[128,256]{1,0:T(8,128)S(1)} %get-tuple-element.42.refs_0_), channel_id=1, source_target_pairs={{1,5},{2,6},{9,13},{10,14},{17,21},{18,22},{25,29},{26,30},{33,37}... | collective-permute-start | bytes 393224 | tf_op jit(solution)/shard_map/ppermute | solution.py:88
  7.0 7.1 %collective-permute-start.4 = (f32[128,256]{1,0:T(8,128)S(1)}, f32[128,256]{1,0:T(8,128)S(1)}, u32[]{:S(2)}, u32[]{:S(2)}) collective-permute-start(f32[128,256]{1,0:T(8,128)S(1)} %get-tuple-element.43.refs_1_), channel_id=1, source_target_pairs={{1,5},{2,6},{9,13},{10,14},{17,21},{18,22},{25,29},{26,30},{33,37}... | collective-permute-start | bytes 393224 | tf_op jit(solution)/shard_map/ppermute | solution.py:88
  8.5 5.6 %collective-permute-start.5 = (f32[128,256]{1,0:T(8,128)S(1)}, f32[128,256]{1,0:T(8,128)S(1)}, u32[]{:S(2)}, u32[]{:S(2)}) collective-permute-start(f32[128,256]{1,0:T(8,128)S(1)} %collective-permute-done.1.refs_2_), channel_id=1, source_target_pairs={{0,4},{3,7},{8,12},{11,15},{16,20},{19,23},{24,28},{27,31},{32,36}... | collective-permute-start | bytes 393224 | tf_op jit(solution)/shard_map/ppermute | solution.py:88
  9.1 5.0 %collective-permute-start.6 = (f32[128,256]{1,0:T(8,128)S(1)}, f32[128,256]{1,0:T(8,128)S(1)}, u32[]{:S(2)}, u32[]{:S(2)}) collective-permute-start(f32[128,256]{1,0:T(8,128)S(1)} %collective-permute-done.2.refs_3_), channel_id=1, source_target_pairs={{0,4},{3,7},{8,12},{11,15},{16,20},{19,23},{24,28},{27,31},{32,36}... | collective-permute-start | bytes 393224 | tf_op jit(solution)/shard_map/ppermute | solution.py:88
  19.3 6.6 %collective-permute-start.10 = (f32[1,256,1024]{2,1,0:T(8,128)}, f32[1,256,1024]{2,1,0:T(8,128)S(1)}, u32[]{:S(2)}, u32[]{:S(2)}) collective-permute-start(f32[1,256,1024]{2,1,0:T(8,128)} %scene), channel_id=1, source_target_pairs={{0,4},{1,5},{2,6},{3,7},{8,12},{9,13},{10,14},{11,15},{16,20},{17,... | collective-permute-start | bytes 3145736 | tf_op jit(solution)/shard_map/ppermute | solution.py:88
  20.6 9.0 %collective-permute-start.7 = (f32[2,128,128]{2,1,0:T(8,128)S(1)}, f32[2,128,128]{2,1,0:T(8,128)S(1)}, u32[]{:S(2)}, u32[]{:S(2)}) collective-permute-start(f32[2,128,128]{2,1,0:T(8,128)S(1)} %get-tuple-element.47), channel_id=1, source_target_pairs={{0,1},{1,2},{2,3},{3,0},{4,5},{5,6},{6,7},{7,4},{8,9},{9,10},{10,1... | collective-permute-start | bytes 393224 | tf_op jit(solution)/shard_map/ppermute | solution.py:88
  20.8 8.8 %collective-permute-start.8 = (f32[2,128,128]{2,1,0:T(8,128)S(1)}, f32[2,128,128]{2,1,0:T(8,128)S(1)}, u32[]{:S(2)}, u32[]{:S(2)}) collective-permute-start(f32[2,128,128]{2,1,0:T(8,128)S(1)} %get-tuple-element.48), channel_id=1, source_target_pairs={{0,2},{1,3},{2,0},{3,1},{4,6},{5,7},{6,4},{7,5},{8,10},{9,11},{10,... | collective-permute-start | bytes 393224 | tf_op jit(solution)/shard_map/ppermute | solution.py:88
  25.7 5.6 %collective-permute-start.9 = (f32[2,128,128]{2,1,0:T(8,128)S(1)}, f32[2,128,128]{2,1,0:T(8,128)S(1)}, u32[]{:S(2)}, u32[]{:S(2)}) collective-permute-start(f32[2,128,128]{2,1,0:T(8,128)S(1)} %get-tuple-element.49), channel_id=1, source_target_pairs={{0,3},{1,0},{2,1},{3,2},{4,7},{5,4},{6,5},{7,6},{8,11},{9,8},{10,9... | collective-permute-start | bytes 393224 | tf_op jit(solution)/shard_map/ppermute | solution.py:88
  36.0 20.9 %all-to-all-start = ((f32[8,4,64,128]{3,2,1,0:T(8,128)}), f32[8,4,64,128]{3,2,1,0:T(8,128)S(1)}, u32[]{:S(2)}, u32[]{:S(2)}) async-start(f32[8,4,64,128]{3,2,1,0:T(8,128)} %copy-done.5), calls=%async_computation | async-start | bytes 2097152 | tf_op jit(solution)/shard_map/all_to_all | solution.py:669
  42.7 11.8 %collective-permute-start.11 = (f32[8,128]{1,0:T(8,128)S(1)}, f32[8,128]{1,0:T(8,128)S(1)}, u32[]{:S(2)}, u32[]{:S(2)}) collective-permute-start(f32[8,128]{1,0:T(8,128)S(1)} %get-tuple-element.54), channel_id=1, source_target_pairs={{1,4},{2,5},{3,6},{4,1},{5,2},{6,3},{9,12},{10,13},{11,14},{12,9},... | collective-permute-start | bytes 12296 | tf_op jit(solution)/shard_map/ppermute | solution.py:88
  61.8 14.0 %all-to-all-start.1 = ((f32[8,144,128]{2,1,0:T(8,128)}), f32[8,144,128]{2,1,0:T(8,128)S(1)}, u32[]{:S(2)}, u32[]{:S(2)}) async-start(f32[8,144,128]{2,1,0:T(8,128)} %copy-done.8), calls=%async_computation.1 | async-start | bytes 1179648 | tf_op jit(solution)/shard_map/all_to_all | solution.py:669
  85.3 4.8 %collective-permute-start.12 = (f32[128,128]{1,0:T(8,128)S(1)}, f32[128,128]{1,0:T(8,128)S(1)}, u32[]{:S(2)}, u32[]{:S(2)}) collective-permute-start(f32[128,128]{1,0:T(8,128)S(1)} %get-tuple-element.59.refs_0_), channel_id=1, source_target_pairs={{0,1},{1,2},{2,3},{3,0},{4,5},{5,6},{6,7},{7,4},{8,9},{9,10},{10,1... | collective-permute-start | bytes 196616 | tf_op jit(solution)/shard_map/ppermute | solution.py:88
  85.4 4.8 %collective-permute-start.13 = (f32[128,128]{1,0:T(8,128)S(1)}, f32[128,128]{1,0:T(8,128)S(1)}, u32[]{:S(2)}, u32[]{:S(2)}) collective-permute-start(f32[128,128]{1,0:T(8,128)S(1)} %get-tuple-element.59.refs_0_), channel_id=1, source_target_pairs={{0,2},{1,3},{2,0},{3,1},{4,6},{5,7},{6,4},{7,5},{8,10},{9,11},{10,... | collective-permute-start | bytes 196616 | tf_op jit(solution)/shard_map/ppermute | solution.py:88
  88.0 4.3 %collective-permute-start.14 = (f32[128,128]{1,0:T(8,128)S(1)}, f32[128,128]{1,0:T(8,128)S(1)}, u32[]{:S(2)}, u32[]{:S(2)}) collective-permute-start(f32[128,128]{1,0:T(8,128)S(1)} %get-tuple-element.59.refs_0_), channel_id=1, source_target_pairs={{0,3},{1,0},{2,1},{3,2},{4,7},{5,4},{6,5},{7,6},{8,11},{9,8},{10,9... | collective-permute-start | bytes 196616 | tf_op jit(solution)/shard_map/ppermute | solution.py:88
  88.4 4.8 %collective-permute-start.15 = (f32[128,128]{1,0:T(8,128)S(1)}, f32[128,128]{1,0:T(8,128)S(1)}, u32[]{:S(2)}, u32[]{:S(2)}) collective-permute-start(f32[128,128]{1,0:T(8,128)S(1)} %get-tuple-element.59.refs_0_), channel_id=1, source_target_pairs={{0,4},{1,5},{2,6},{3,7},{4,0},{5,1},{6,2},{7,3},{8,12},{9,13},{10,... | collective-permute-start | bytes 196616 | tf_op jit(solution)/shard_map/ppermute | solution.py:88
  99.3 13.5 %all-to-all-start.2 = ((f32[8,2,64,128]{3,2,1,0:T(8,128)}), f32[8,2,64,128]{3,2,1,0:T(8,128)S(1)}, u32[]{:S(2)}, u32[]{:S(2)}) async-start(f32[8,2,64,128]{3,2,1,0:T(8,128)} %shard_map.188), calls=%async_computation.2 | async-start | bytes 1048576 | tf_op jit(solution)/shard_map/all_to_all | solution.py:669
  115.5 5.8 %collective-permute-start.19 = (f32[2,136,128]{2,1,0:T(8,128)S(1)}, f32[2,136,128]{2,1,0:T(8,128)S(1)}, u32[]{:S(2)}, u32[]{:S(2)}) collective-permute-start(f32[2,136,128]{2,1,0:T(8,128)S(1)} %get-tuple-element.64), channel_id=1, source_target_pairs={{0,1},{1,2},{2,3},{3,0},{4,5},{5,6},{6,7},{7,4},{8,9},{9,10},{10,1... | collective-permute-start | bytes 417800 | tf_op jit(solution)/shard_map/ppermute | solution.py:88
  115.6 6.5 %collective-permute-start.20 = (f32[2,136,128]{2,1,0:T(8,128)S(1)}, f32[2,136,128]{2,1,0:T(8,128)S(1)}, u32[]{:S(2)}, u32[]{:S(2)}) collective-permute-start(f32[2,136,128]{2,1,0:T(8,128)S(1)} %get-tuple-element.65), channel_id=1, source_target_pairs={{0,2},{1,3},{2,0},{3,1},{4,6},{5,7},{6,4},{7,5},{8,10},{9,11},{10,... | collective-permute-start | bytes 417800 | tf_op jit(solution)/shard_map/ppermute | solution.py:88
  118.3 7.5 %collective-permute-start.21 = (f32[2,136,128]{2,1,0:T(8,128)S(1)}, f32[2,136,128]{2,1,0:T(8,128)S(1)}, u32[]{:S(2)}, u32[]{:S(2)}) collective-permute-start(f32[2,136,128]{2,1,0:T(8,128)S(1)} %get-tuple-element.66), channel_id=1, source_target_pairs={{0,3},{1,0},{2,1},{3,2},{4,7},{5,4},{6,5},{7,6},{8,11},{9,8},{10,9... | collective-permute-start | bytes 417800 | tf_op jit(solution)/shard_map/ppermute | solution.py:88
  130.8 4.6 %collective-permute-start.24 = (f32[40,256]{1,0:T(8,128)S(1)}, f32[40,256]{1,0:T(8,128)S(1)}, u32[]{:S(2)}, u32[]{:S(2)}) collective-permute-start(f32[40,256]{1,0:T(8,128)S(1)} %get-tuple-element.72), channel_id=1, source_target_pairs={{0,16},{1,17},{2,18},{3,19},{4,20},{5,21},{6,22},{7,23},{8,24},{9,... | collective-permute-start | bytes 122888 | tf_op jit(solution)/shard_map/ppermute | solution.py:88
  139.4 10.4 %collective-permute-start.27 = (f32[40,256]{1,0:T(8,128)S(1)}, f32[40,256]{1,0:T(8,128)S(1)}, u32[]{:S(2)}, u32[]{:S(2)}) collective-permute-start(f32[40,256]{1,0:T(8,128)S(1)} %add.32), channel_id=1, source_target_pairs={{0,32},{1,33},{2,34},{3,35},{4,36},{5,37},{6,38},{7,39},{8,40},{9,... | collective-permute-start | bytes 122888 | tf_op jit(solution)/shard_map/ppermute | solution.py:88
  142.3 7.5 %collective-permute-start.28 = (f32[40,256]{1,0:T(8,128)S(1)}, f32[40,256]{1,0:T(8,128)S(1)}, u32[]{:S(2)}, u32[]{:S(2)}) collective-permute-start(f32[40,256]{1,0:T(8,128)S(1)} %add.32), channel_id=1, source_target_pairs={{0,64},{1,65},{2,66},{3,67},{4,68},{5,69},{6,70},{7,71},{8,72},{9,... | collective-permute-start | bytes 122888 | tf_op jit(solution)/shard_map/ppermute | solution.py:88
  151.6 4.7 %collective-permute-start.30 = (f32[32,256]{1,0:T(8,128)S(1)}, f32[32,256]{1,0:T(8,128)S(1)}, u32[]{:S(2)}, u32[]{:S(2)}) collective-permute-start(f32[32,256]{1,0:T(8,128)S(1)} %get-tuple-element.79), channel_id=1, source_target_pairs={{0,1},{3,2},{4,5},{7,6},{8,9},{11,10},{12,13},{15,14},{16,17},{19,... | collective-permute-start | bytes 98312 | tf_op jit(solution)/shard_map/ppermute | solution.py:88
  164.9 10.7 %collective-permute-start.31 = (f32[4,2,32,256]{3,2,1,0:T(8,128)S(1)}, f32[4,2,32,256]{3,2,1,0:T(8,128)S(1)}, u32[]{:S(2)}, u32[]{:S(2)}) collective-permute-start(f32[4,2,32,256]{3,2,1,0:T(8,128)S(1)} %all_to_all.20.refs_0_), channel_id=1, source_target_pairs={{1,5},{2,6},{5,1},{6,2},{9,13},{10,14},{13,9},{14,10},{17,21},{18,... | collective-permute-start | bytes 786440 | tf_op jit(solution)/shard_map/ppermute | solution.py:88
  (31 other events, 365.2 us)

commit v7 on v6

--- a/solution.py
+++ b/solution.py
@@ -51,14 +51,12 @@
     window = window.reshape(4, 2, 256, 128).transpose(0, 2, 1, 3).reshape(4, 256, 256)
     near = np.stack(halves(near)).reshape(4, 2, 2, 128, 128)
     near = near.transpose(0, 1, 3, 2, 4).reshape(4, 256, 256)
-    cos_e, sin_e = trig([0, 1], half, 8)
     cos_t, sin_t = trig(quarter, fours, N)
     return {
         "m": np.stack(halves(cos_m) + halves(sin_m)),
         "m_back": np.stack(halves(cos_m.T) + halves(sin_m.T)),
         "f": np.concatenate([np.stack(halves(cos_f) + halves(sin_f)), window, near]),
         "pack": np.stack(halves(packed)),
-        "eighth": np.stack([cos_e, sin_e], 1).astype(np.float32),
         "tw_col": np.concatenate([cos_t, sin_t], 1).astype(np.float32),
         "tw_row": np.concatenate([cos_t, sin_t], 1).T.astype(np.float32).copy(),
     }
@@ -160,6 +158,18 @@
     cos = jnp.where((q == 1) | (q == 2), -c0, c0)
     sin = jnp.where(q >= 2, -s0, s0)
     return cos, sin
+
+
+def eighth_turns(c):
+    step = (lax.broadcasted_iota(jnp.int32, (8, 512), 1) & 7) * c
+    side = 0.5**0.5
+    cos = jnp.where(step == 0, 1.0, jnp.where(step == 4, -1.0, 0.0))
+    cos = jnp.where((step == 1) | (step == 7), side, cos)
+    cos = jnp.where((step == 3) | (step == 5), -side, cos)
+    sin = jnp.where(step == 2, 1.0, jnp.where(step == 6, -1.0, 0.0))
+    sin = jnp.where((step == 1) | (step == 3), side, sin)
+    sin = jnp.where((step == 5) | (step == 7), -side, sin)
+    return cos[0:1, :], sin[0:1, :]
 
 
 def spot_of(idx, d, e=0):
@@ -200,14 +210,12 @@
     return ref[0], ref[1], ref[2], ref[3]
 
 
-def phase_kernel(idx, phases, own0, own1, sent0, sent1, grid):
+def phase_kernel(idx, phases, own, sent, grid):
     grid[...] = jnp.transpose(phases[...])
     kept = aligned(jnp.where(idx[0] == 1, 1, 0), 128)
     given = aligned(jnp.where(idx[0] == 1, 0, 1), 128)
-    own0[...] = grid[pl.ds(kept, 128), 0:256]
-    own1[...] = grid[pl.ds(kept, 128), 256:512]
-    sent0[...] = grid[pl.ds(given, 128), 0:256]
-    sent1[...] = grid[pl.ds(given, 128), 256:512]
+    own[...] = grid[pl.ds(kept, 128), :]
+    sent[...] = grid[pl.ds(given, 128), :]
 
 
 def scene_kernel(idx, scene, other, w, out, strip, edge, image, grid):
@@ -225,15 +233,12 @@
 
 
 def pupil_kernel(idx, *refs):
-    m, e, o0, o1, o2, o3, pupil, grid = refs[8:]
+    m, o0, o1, o2, o3, pupil, grid = refs[4:]
     s = idx[0]
     c = idx[1]
     owner = idx[2] == 1
     central = (s == 1) | (s == 2)
-    own = jnp.concatenate([refs[0][...], refs[1][...]], 1)
-    got = jnp.concatenate([refs[2][...], refs[3][...]], 1)
-    own_far = jnp.concatenate([refs[4][...], refs[5][...]], 1)
-    got_far = jnp.concatenate([refs[6][...], refs[7][...]], 1)
+    own, got, own_far, got_far = [ref[...] for ref in refs[:4]]
     phase = jnp.where(central, jnp.where(owner, own, own_far), jnp.where(owner, got, got_far))
     rows = lax.broadcasted_iota(jnp.int32, (128, 512), 0) + s * 128
     cols = lax.broadcasted_iota(jnp.int32, (128, 512), 1)
@@ -245,7 +250,8 @@
     im = jnp.where(inside, sin, 0.0)
     pupil[0] = re
     pupil[1] = im
-    re, im = times(re, im, e[c, 0:1, :], -e[c, 1:2, :])
+    turn_cos, turn_sin = eighth_turns(c)
+    re, im = times(re, im, turn_cos, -turn_sin)
     out_re, out_im = dft_right(re, im, mats_of(m), -1.0)
     grid[0] = out_re
     grid[1] = out_im
@@ -598,14 +604,15 @@
 
 
 def mask_grad_kernel(scale, idx, ids, got, *refs):
-    b0, b1, b2, b3, m, e, pupil, keep, send, grid, whole = refs
+    b0, b1, b2, b3, m, pupil, keep, send, grid, whole = refs
     small = None
     for d, block in enumerate((b0, b1, b2, b3)):
         grid[:, :, pl.ds(aligned(from_of(idx, d)[0], 128), 128)] = block[:, 0:128, :]
         part = jnp.concatenate([block[0, 128:136, :], block[1, 128:136, :]], 1)
         small = part if small is None else small + part
     re, im = dft_right(grid[0], grid[1], mats_of(m), 1.0)
-    re, im = times(re, im, e[idx[1], 0:1, :], e[idx[1], 1:2, :])
+    turn_cos, turn_sin = eighth_turns(idx[1])
+    re, im = times(re, im, turn_cos, turn_sin)
     factor = ratio_of(jnp.where(idx[2] == 1, ids[1], got[1]))[0:1, 0:1] * scale
     whole[...] = factor * (im * pupil[0] - re * pupil[1])
     keep[0:128, :] = whole[:, pl.ds(aligned(idx[1], 256), 256)]
@@ -682,17 +689,17 @@
         phase_kernel,
         (idx, phases),
         (0,),
-        [(128, 256)] * 4,
+        [(128, 512)] * 2,
         [pltpu.VMEM((256, 512), F32)],
     )
-    pieces = list(mine[:2]) + [
+    pieces = list(mine[:1]) + [
         lay.move(
             block,
             lambda g, zh, y, c, s: (
                 (g, zh, y, c, {1: 0, 2: 3}[s]) if s in (1, 2) and c == g else None
             ),
         )
-        for block in mine[2:]
+        for block in mine[1:]
     ]
     pieces += [
         lay.move(
@@ -701,13 +708,13 @@
                 (g, zh, y, 1 - c, s) if c == g and (s in (1, 2)) == inner else None
             ),
         )
-        for block, inner in zip(pieces, (True, True, False, False))
+        for block, inner in zip(pieces, (True, False))
     ]
 
 
     *field, pupil = call(
         pupil_kernel,
-        (idx, *pieces, con["m"], con["eighth"]),
+        (idx, *pieces, con["m"]),
         (0,),
         [(2, 128, 128)] * 4 + [(2, 128, 512)],
         [pltpu.VMEM((2, 128, 512), F32)],
@@ -794,7 +801,7 @@
     )
     keep, send = call(
         functools.partial(mask_grad_kernel, 2.0 * scale_psf),
-        (idx, ids, got, *field_grad, con["m_back"], con["eighth"], pupil),
+        (idx, ids, got, *field_grad, con["m_back"], pupil),
         (0, 1, 2),
         [(136, 256)] * 2,
         [

time: 178 us -> 177 us (level)
    unnamed x41 -> x37, local copies, waits for them, and re-layouts: 10.2 us -> 9.46 us
    ppermute x32 -> x29, waiting for transfers between devices: 32.1 us -> 32.3 us  [move(): return lax.ppermute(x, AXES, pairs)]
    ppermute x32 -> x29, starting transfers between devices: 54.5 us -> 54.5 us  [move(): return lax.ppermute(x, AXES, pairs)]
  transfers between devices with their start and end apart: 35 -> 32, of which waited for: 19 -> 18; matrix products, arithmetic and copies ran while one was open for 0% -> 0% of each run, Pallas kernels for 1% -> 1%
where the time goes in v7:
time: 177 us
  starting transfers between devices  70.8 us (40%)
  waiting for transfers between devices  52.2 us (29%)
  Pallas kernels  31.5 us (18%)
  local copies, waits for them, and re-layouts  9.67 us (5%)
  blocking collectives  8.6 us (5%)
  between operations  2.3 us (1%)
    ppermute x29, starting transfers between devices, move(): return lax.ppermute(x, AXES, pairs)  54.5 us
    ppermute x29, waiting for transfers between devices, move(): return lax.ppermute(x, AXES, pairs)  32.3 us
    pallas_call x11, Pallas kernels, call(): pl.pallas_call(kernel, out_shape=[jax.ShapeDtypeStruct(shape, F32) for sh...  31.5 us
    all_to_all x3, waiting for transfers between devices, to_eight(): return lax.all_to_all(blocks, ('core', 'sp'), 0, 0, tiled=True)  19.9 us
    all_to_all x3, starting transfers between devices, to_eight(): return lax.all_to_all(blocks, ('core', 'sp'), 0, 0, tiled=True)  16.3 us
    unnamed x37, local copies, waits for them, and re-layouts  9.46 us
    all_to_all x1, blocking collectives, on_device(): lax.all_to_all(jnp.broadcast_to(home, (lay.y, 2, piece, 256)), 'y', 0, 0,...  8.6 us
  transfers between devices with their start and end apart: 32, of which 18 were waited for; matrix products, arithmetic and copies ran while one was open for 0% of the time, Pallas kernels for 1%

profile of v7, /device:TPU:3, one launch (start us, length us, event | category | flops | bytes accessed | tf_op | source)
XLA Modules:
  0.0 176.7 jit_solution(2589288103446863443)
XLA Ops:
  7.2 4.5 %collective-permute-done.2.refs_2_ = f32[128,512]{1,0:T(8,128)S(1)} collective-permute-done((f32[128,512]{1,0:T(8,128)S(1)}, f32[128,512]{1,0:T(8,128)S(1)}, u32[]{:S(2)}, u32[]{:S(2)}) %collective-permute-start.2) | collective-permute-done | bytes 262176 | tf_op jit(solution)/shard_map/ppermute | solution.py:86
  17.6 7.6 %collective-permute-start.5 = (f32[2,128,128]{2,1,0:T(8,128)S(1)}, f32[2,128,128]{2,1,0:T(8,128)S(1)}, u32[]{:S(2)}, u32[]{:S(2)}) collective-permute-start(f32[2,128,128]{2,1,0:T(8,128)S(1)} %get-tuple-element.44), channel_id=1, source_target_pairs={{0,2},{1,3},{2,0},{3,1},{4,6},{5,7},{6,4},{7,5},{8,10},{9,11},{10,... | collective-permute-start | bytes 393224 | tf_op jit(solution)/shard_map/ppermute | solution.py:86
  26.6 2.4 %shard_map.175 = (f32[8,2,64,128]{3,2,1,0:T(8,128)S(1)}, f32[136,128]{1,0:T(8,128)S(1)}, f32[8,128]{1,0:T(8,128)S(1)}) custom-call(s32[4]{0:T(128)S(1)} %pad_add_fusion.idx, f32[1,256,1024]{2,1,0:T(8,128)S(1)} %copy-done.4, f32[1,256,1024]{2,1,0:T(8,128)S(1)} %collective-permute-done.7.other, bf16[2,1024,1024]{2,1,0:T(8,128)(2,1)S(1)} %copy-done.1), custom_call_target="tpu_custom_call" | custom-call | tf_op jit(solution)/shard_map/pallas_call | solution.py:192
  30.9 2.6 %shard_map.176 = (f32[2,256,512]{2,1,0:T(8,128)S(1)}, f32[8,4,64,128]{3,2,1,0:T(8,128)S(1)}) custom-call(s32[4]{0:T(128)S(1)} %pad_add_fusion.idx, f32[2,128,128]{2,1,0:T(8,128)S(1)} %get-tuple-element.42.b0, f32[2,128,128]{2,1,0:T(8,128)S(1)} %collective-permute-done.4.b1, f32[2,128,128]{2,1,0:T(8,128)S(1)} %collective-permute-done.5.b2, ...), custom_call_target="tpu_custom_call" | custom-call | tf_op jit(solution)/shard_map/pallas_call | solution.py:192
  35.5 6.7 %all-to-all-start = ((f32[8,4,64,128]{3,2,1,0:T(8,128)}), f32[8,4,64,128]{3,2,1,0:T(8,128)S(1)}, u32[]{:S(2)}, u32[]{:S(2)}) async-start(f32[8,4,64,128]{3,2,1,0:T(8,128)} %copy-done.5), calls=%async_computation | async-start | bytes 2097152 | tf_op jit(solution)/shard_map/all_to_all | solution.py:676
  42.2 3.3 %collective-permute-start.8 = (f32[8,128]{1,0:T(8,128)S(1)}, f32[8,128]{1,0:T(8,128)S(1)}, u32[]{:S(2)}, u32[]{:S(2)}) collective-permute-start(f32[8,128]{1,0:T(8,128)S(1)} %get-tuple-element.50), channel_id=1, source_target_pairs={{1,4},{2,5},{3,6},{4,1},{5,2},{6,3},{9,12},{10,13},{11,14},{12,9},... | collective-permute-start | bytes 12296 | tf_op jit(solution)/shard_map/ppermute | solution.py:86
  45.5 8.5 %collective-permute-done.8.refs_3_ = f32[8,128]{1,0:T(8,128)S(1)} collective-permute-done((f32[8,128]{1,0:T(8,128)S(1)}, f32[8,128]{1,0:T(8,128)S(1)}, u32[]{:S(2)}, u32[]{:S(2)}) %collective-permute-start.8) | collective-permute-done | bytes 4128 | tf_op jit(solution)/shard_map/ppermute | solution.py:86
  56.3 3.4 %shard_map.177 = (f32[8,144,128]{2,1,0:T(8,128)S(1)}, f32[2,288,256]{2,1,0:T(8,128)S(1)}) custom-call(s32[4]{0:T(128)S(1)} %pad_add_fusion.idx, f32[8,4,64,128]{3,2,1,0:T(8,128)S(1)} %all-to-all-done.blocks, bf16[12,256,256]{2,1,0:T(8,128)(2,1)S(1)} %copy-done, f32[8,256]{1,0:T(8,128)S(1)} %copy-done.14), custom_call_target="tpu_custom_call" | custom-call | tf_op jit(solution)/shard_map/pallas_call | solution.py:192
  61.3 4.8 %all-to-all-start.1 = ((f32[8,144,128]{2,1,0:T(8,128)}), f32[8,144,128]{2,1,0:T(8,128)S(1)}, u32[]{:S(2)}, u32[]{:S(2)}) async-start(f32[8,144,128]{2,1,0:T(8,128)} %copy-done.8), calls=%async_computation.1 | async-start | bytes 1179648 | tf_op jit(solution)/shard_map/all_to_all | solution.py:676
  66.2 9.2 %all-to-all-done.1.refs_0_ = f32[8,144,128]{2,1,0:T(8,128)S(1)} async-done(((f32[8,144,128]{2,1,0:T(8,128)}), f32[8,144,128]{2,1,0:T(8,128)S(1)}, u32[]{:S(2)}, u32[]{:S(2)}) %all-to-all-start.1) | async-done | bytes 589856 | tf_op jit(solution)/shard_map/all_to_all | solution.py:676
  75.4 9.4 %shard_map.178 = (f32[128,128]{1,0:T(8,128)S(1)}, f32[32,256]{1,0:T(8,128)S(1)}) custom-call(s32[4]{0:T(128)S(1)} %pad_add_fusion.idx, f32[32,9]{1,0:T(8,128)S(1)} %copy.22.w1, f32[32]{0:T(128)S(1)} %copy-done.16, f32[9,32]{1,0:T(8,128)S(1)} %copy-done.15, f32[8,144,128]{2,1,0:T(8,128)S(1)} %all-to-all-done.1.refs_0_, bf16[12,256,256]{2,1,0:T(8,128)(2,1)S(1)} %copy-done, ...), custom_call_target="tpu_custom_call" | custom-call | tf_op jit(solution)/shard_map/pallas_call | solution.py:192
  84.9 2.7 %collective-permute-start.10 = (f32[128,128]{1,0:T(8,128)S(1)}, f32[128,128]{1,0:T(8,128)S(1)}, u32[]{:S(2)}, u32[]{:S(2)}) collective-permute-start(f32[128,128]{1,0:T(8,128)S(1)} %get-tuple-element.55.refs_0_), channel_id=1, source_target_pairs={{0,2},{1,3},{2,0},{3,1},{4,6},{5,7},{6,4},{7,5},{8,10},{9,11},{10,... | collective-permute-start | bytes 196616 | tf_op jit(solution)/shard_map/ppermute | solution.py:86
  94.7 4.1 %shard_map.179 = f32[8,2,64,128]{3,2,1,0:T(8,128)} custom-call(s32[4]{0:T(128)S(1)} %pad_add_fusion.idx, f32[128,128]{1,0:T(8,128)S(1)} %get-tuple-element.55.refs_0_, f32[128,128]{1,0:T(8,128)S(1)} %collective-permute-done.9.refs_1_, f32[128,128]{1,0:T(8,128)S(1)} %collective-permute-done.10.refs_2_, f32[128,128]{1,0:T(8,128)S(1)} %collective-permute-done.11.refs_3_, ...), custom_call_target="tpu_custom_call" | custom-call | tf_op jit(solution)/shard_map/pallas_call | solution.py:192
  98.8 4.9 %all-to-all-start.2 = ((f32[8,2,64,128]{3,2,1,0:T(8,128)}), f32[8,2,64,128]{3,2,1,0:T(8,128)S(1)}, u32[]{:S(2)}, u32[]{:S(2)}) async-start(f32[8,2,64,128]{3,2,1,0:T(8,128)} %shard_map.179), calls=%async_computation.2 | async-start | bytes 1048576 | tf_op jit(solution)/shard_map/all_to_all | solution.py:676
  103.9 8.3 %all-to-all-done.2.blocks = f32[8,2,64,128]{3,2,1,0:T(8,128)S(1)} async-done(((f32[8,2,64,128]{3,2,1,0:T(8,128)}), f32[8,2,64,128]{3,2,1,0:T(8,128)S(1)}, u32[]{:S(2)}, u32[]{:S(2)}) %all-to-all-start.2) | async-done | bytes 524320 | tf_op jit(solution)/shard_map/all_to_all | solution.py:676
  112.3 2.7 %shard_map.180 = (f32[2,136,128]{2,1,0:T(8,128)S(1)}, f32[2,136,128]{2,1,0:T(8,128)S(1)}, f32[2,136,128]{2,1,0:T(8,128)S(1)}, f32[2,136,128]{2,1,0:T(8,128)S(1)}) custom-call(s32[4]{0:T(128)S(1)} %pad_add_fusion.idx, f32[8,2,64,128]{3,2,1,0:T(8,128)S(1)} %all-to-all-done.2.blocks, f32[2,256,512]{2,1,0:T(8,128)S(1)} %copy-done.7, ...), custom_call_target="tpu_custom_call" | custom-call | tf_op jit(solution)/shard_map/pallas_call | solution.py:192
  115.1 2.7 %collective-permute-start.17 = (f32[2,136,128]{2,1,0:T(8,128)S(1)}, f32[2,136,128]{2,1,0:T(8,128)S(1)}, u32[]{:S(2)}, u32[]{:S(2)}) collective-permute-start(f32[2,136,128]{2,1,0:T(8,128)S(1)} %get-tuple-element.61), channel_id=1, source_target_pairs={{0,2},{1,3},{2,0},{3,1},{4,6},{5,7},{6,4},{7,5},{8,10},{9,11},{10,... | collective-permute-start | bytes 417800 | tf_op jit(solution)/shard_map/ppermute | solution.py:86
  121.6 3.6 %collective-permute-done.18.refs_3_ = f32[2,136,128]{2,1,0:T(8,128)S(1)} collective-permute-done((f32[2,136,128]{2,1,0:T(8,128)S(1)}, f32[2,136,128]{2,1,0:T(8,128)S(1)}, u32[]{:S(2)}, u32[]{:S(2)}) %collective-permute-start.18) | collective-permute-done | bytes 139296 | tf_op jit(solution)/shard_map/ppermute | solution.py:86
  130.3 2.5 %collective-permute-start.21 = (f32[40,256]{1,0:T(8,128)S(1)}, f32[40,256]{1,0:T(8,128)S(1)}, u32[]{:S(2)}, u32[]{:S(2)}) collective-permute-start(f32[40,256]{1,0:T(8,128)S(1)} %get-tuple-element.68), channel_id=1, source_target_pairs={{0,16},{1,17},{2,18},{3,19},{4,20},{5,21},{6,22},{7,23},{8,24},{9,... | collective-permute-start | bytes 122888 | tf_op jit(solution)/shard_map/ppermute | solution.py:86
  138.9 2.9 %collective-permute-start.24 = (f32[40,256]{1,0:T(8,128)S(1)}, f32[40,256]{1,0:T(8,128)S(1)}, u32[]{:S(2)}, u32[]{:S(2)}) collective-permute-start(f32[40,256]{1,0:T(8,128)S(1)} %add.32), channel_id=1, source_target_pairs={{0,32},{1,33},{2,34},{3,35},{4,36},{5,37},{6,38},{7,39},{8,40},{9,... | collective-permute-start | bytes 122888 | tf_op jit(solution)/shard_map/ppermute | solution.py:86
  141.8 5.1 %collective-permute-start.25 = (f32[40,256]{1,0:T(8,128)S(1)}, f32[40,256]{1,0:T(8,128)S(1)}, u32[]{:S(2)}, u32[]{:S(2)}) collective-permute-start(f32[40,256]{1,0:T(8,128)S(1)} %add.32), channel_id=1, source_target_pairs={{0,64},{1,65},{2,66},{3,67},{4,68},{5,69},{6,70},{7,71},{8,72},{9,... | collective-permute-start | bytes 122888 | tf_op jit(solution)/shard_map/ppermute | solution.py:86
  152.4 3.4 %collective-permute-done.27 = f32[32,256]{1,0:T(8,128)S(1)} collective-permute-done((f32[32,256]{1,0:T(8,128)S(1)}, f32[32,256]{1,0:T(8,128)S(1)}, u32[]{:S(2)}, u32[]{:S(2)}) %collective-permute-start.27) | collective-permute-done | bytes 32800 | tf_op jit(solution)/shard_map/ppermute | solution.py:86
  155.8 8.6 %all_to_all.20.refs_0_ = f32[4,2,32,256]{3,2,1,0:T(8,128)S(1)} all-to-all(f32[4,2,32,256]{3,2,1,0:T(8,128)S(1)} %broadcast_in_dim.3), channel_id=1, replica_groups=mesh['grp'=2,'zh'=4,'y'=4,'core'=2,'sp'=4] {'y'}, dimensions={0} | all-to-all | bytes 524288 | tf_op jit(solution)/shard_map/all_to_all | solution.py:835
  164.3 9.5 %collective-permute-start.28 = (f32[4,2,32,256]{3,2,1,0:T(8,128)S(1)}, f32[4,2,32,256]{3,2,1,0:T(8,128)S(1)}, u32[]{:S(2)}, u32[]{:S(2)}) collective-permute-start(f32[4,2,32,256]{3,2,1,0:T(8,128)S(1)} %all_to_all.20.refs_0_), channel_id=1, source_target_pairs={{1,5},{2,6},{5,1},{6,2},{9,13},{10,14},{13,9},{14,10},{17,21},{18,... | collective-permute-start | bytes 786440 | tf_op jit(solution)/shard_map/ppermute | solution.py:86
  (103 shorter events, 51.2 us)
Async XLA Ops:
  5.0 6.6 %collective-permute-start.2 = (f32[128,512]{1,0:T(8,128)S(1)}, f32[128,512]{1,0:T(8,128)S(1)}, u32[]{:S(2)}, u32[]{:S(2)}) collective-permute-start(f32[128,512]{1,0:T(8,128)S(1)} %get-tuple-element.40.refs_0_), channel_id=1, source_target_pairs={{1,5},{2,6},{9,13},{10,14},{17,21},{18,22},{25,29},{26,30},{33,37}... | collective-permute-start | bytes 786440 | tf_op jit(solution)/shard_map/ppermute | solution.py:86
  6.5 5.2 %collective-permute-start.3 = (f32[128,512]{1,0:T(8,128)S(1)}, f32[128,512]{1,0:T(8,128)S(1)}, u32[]{:S(2)}, u32[]{:S(2)}) collective-permute-start(f32[128,512]{1,0:T(8,128)S(1)} %collective-permute-done.1.refs_1_), channel_id=1, source_target_pairs={{0,4},{3,7},{8,12},{11,15},{16,20},{19,23},{24,28},{27,31},{32,36}... | collective-permute-start | bytes 786440 | tf_op jit(solution)/shard_map/ppermute | solution.py:86
  16.2 9.2 %collective-permute-start.7 = (f32[1,256,1024]{2,1,0:T(8,128)}, f32[1,256,1024]{2,1,0:T(8,128)S(1)}, u32[]{:S(2)}, u32[]{:S(2)}) collective-permute-start(f32[1,256,1024]{2,1,0:T(8,128)} %scene), channel_id=1, source_target_pairs={{0,4},{1,5},{2,6},{3,7},{8,12},{9,13},{10,14},{11,15},{16,20},{17,... | collective-permute-start | bytes 3145736 | tf_op jit(solution)/shard_map/ppermute | solution.py:86
  17.4 11.6 %collective-permute-start.4 = (f32[2,128,128]{2,1,0:T(8,128)S(1)}, f32[2,128,128]{2,1,0:T(8,128)S(1)}, u32[]{:S(2)}, u32[]{:S(2)}) collective-permute-start(f32[2,128,128]{2,1,0:T(8,128)S(1)} %get-tuple-element.43), channel_id=1, source_target_pairs={{0,1},{1,2},{2,3},{3,0},{4,5},{5,6},{6,7},{7,4},{8,9},{9,10},{10,1... | collective-permute-start | bytes 393224 | tf_op jit(solution)/shard_map/ppermute | solution.py:86
  17.6 11.4 %collective-permute-start.5 = (f32[2,128,128]{2,1,0:T(8,128)S(1)}, f32[2,128,128]{2,1,0:T(8,128)S(1)}, u32[]{:S(2)}, u32[]{:S(2)}) collective-permute-start(f32[2,128,128]{2,1,0:T(8,128)S(1)} %get-tuple-element.44), channel_id=1, source_target_pairs={{0,2},{1,3},{2,0},{3,1},{4,6},{5,7},{6,4},{7,5},{8,10},{9,11},{10,... | collective-permute-start | bytes 393224 | tf_op jit(solution)/shard_map/ppermute | solution.py:86
  25.2 5.6 %collective-permute-start.6 = (f32[2,128,128]{2,1,0:T(8,128)S(1)}, f32[2,128,128]{2,1,0:T(8,128)S(1)}, u32[]{:S(2)}, u32[]{:S(2)}) collective-permute-start(f32[2,128,128]{2,1,0:T(8,128)S(1)} %get-tuple-element.45), channel_id=1, source_target_pairs={{0,3},{1,0},{2,1},{3,2},{4,7},{5,4},{6,5},{7,6},{8,11},{9,8},{10,9... | collective-permute-start | bytes 393224 | tf_op jit(solution)/shard_map/ppermute | solution.py:86
  35.5 20.9 %all-to-all-start = ((f32[8,4,64,128]{3,2,1,0:T(8,128)}), f32[8,4,64,128]{3,2,1,0:T(8,128)S(1)}, u32[]{:S(2)}, u32[]{:S(2)}) async-start(f32[8,4,64,128]{3,2,1,0:T(8,128)} %copy-done.5), calls=%async_computation | async-start | bytes 2097152 | tf_op jit(solution)/shard_map/all_to_all | solution.py:676
  42.2 11.8 %collective-permute-start.8 = (f32[8,128]{1,0:T(8,128)S(1)}, f32[8,128]{1,0:T(8,128)S(1)}, u32[]{:S(2)}, u32[]{:S(2)}) collective-permute-start(f32[8,128]{1,0:T(8,128)S(1)} %get-tuple-element.50), channel_id=1, source_target_pairs={{1,4},{2,5},{3,6},{4,1},{5,2},{6,3},{9,12},{10,13},{11,14},{12,9},... | collective-permute-start | bytes 12296 | tf_op jit(solution)/shard_map/ppermute | solution.py:86
  61.3 14.0 %all-to-all-start.1 = ((f32[8,144,128]{2,1,0:T(8,128)}), f32[8,144,128]{2,1,0:T(8,128)S(1)}, u32[]{:S(2)}, u32[]{:S(2)}) async-start(f32[8,144,128]{2,1,0:T(8,128)} %copy-done.8), calls=%async_computation.1 | async-start | bytes 1179648 | tf_op jit(solution)/shard_map/all_to_all | solution.py:676
  84.8 4.8 %collective-permute-start.9 = (f32[128,128]{1,0:T(8,128)S(1)}, f32[128,128]{1,0:T(8,128)S(1)}, u32[]{:S(2)}, u32[]{:S(2)}) collective-permute-start(f32[128,128]{1,0:T(8,128)S(1)} %get-tuple-element.55.refs_0_), channel_id=1, source_target_pairs={{0,1},{1,2},{2,3},{3,0},{4,5},{5,6},{6,7},{7,4},{8,9},{9,10},{10,1... | collective-permute-start | bytes 196616 | tf_op jit(solution)/shard_map/ppermute | solution.py:86
  84.9 4.8 %collective-permute-start.10 = (f32[128,128]{1,0:T(8,128)S(1)}, f32[128,128]{1,0:T(8,128)S(1)}, u32[]{:S(2)}, u32[]{:S(2)}) collective-permute-start(f32[128,128]{1,0:T(8,128)S(1)} %get-tuple-element.55.refs_0_), channel_id=1, source_target_pairs={{0,2},{1,3},{2,0},{3,1},{4,6},{5,7},{6,4},{7,5},{8,10},{9,11},{10,... | collective-permute-start | bytes 196616 | tf_op jit(solution)/shard_map/ppermute | solution.py:86
  87.5 4.3 %collective-permute-start.11 = (f32[128,128]{1,0:T(8,128)S(1)}, f32[128,128]{1,0:T(8,128)S(1)}, u32[]{:S(2)}, u32[]{:S(2)}) collective-permute-start(f32[128,128]{1,0:T(8,128)S(1)} %get-tuple-element.55.refs_0_), channel_id=1, source_target_pairs={{0,3},{1,0},{2,1},{3,2},{4,7},{5,4},{6,5},{7,6},{8,11},{9,8},{10,9... | collective-permute-start | bytes 196616 | tf_op jit(solution)/shard_map/ppermute | solution.py:86
  87.9 4.8 %collective-permute-start.12 = (f32[128,128]{1,0:T(8,128)S(1)}, f32[128,128]{1,0:T(8,128)S(1)}, u32[]{:S(2)}, u32[]{:S(2)}) collective-permute-start(f32[128,128]{1,0:T(8,128)S(1)} %get-tuple-element.55.refs_0_), channel_id=1, source_target_pairs={{0,4},{1,5},{2,6},{3,7},{4,0},{5,1},{6,2},{7,3},{8,12},{9,13},{10,... | collective-permute-start | bytes 196616 | tf_op jit(solution)/shard_map/ppermute | solution.py:86
  98.8 13.5 %all-to-all-start.2 = ((f32[8,2,64,128]{3,2,1,0:T(8,128)}), f32[8,2,64,128]{3,2,1,0:T(8,128)S(1)}, u32[]{:S(2)}, u32[]{:S(2)}) async-start(f32[8,2,64,128]{3,2,1,0:T(8,128)} %shard_map.179), calls=%async_computation.2 | async-start | bytes 1048576 | tf_op jit(solution)/shard_map/all_to_all | solution.py:676
  115.0 5.8 %collective-permute-start.16 = (f32[2,136,128]{2,1,0:T(8,128)S(1)}, f32[2,136,128]{2,1,0:T(8,128)S(1)}, u32[]{:S(2)}, u32[]{:S(2)}) collective-permute-start(f32[2,136,128]{2,1,0:T(8,128)S(1)} %get-tuple-element.60), channel_id=1, source_target_pairs={{0,1},{1,2},{2,3},{3,0},{4,5},{5,6},{6,7},{7,4},{8,9},{9,10},{10,1... | collective-permute-start | bytes 417800 | tf_op jit(solution)/shard_map/ppermute | solution.py:86
  115.1 6.5 %collective-permute-start.17 = (f32[2,136,128]{2,1,0:T(8,128)S(1)}, f32[2,136,128]{2,1,0:T(8,128)S(1)}, u32[]{:S(2)}, u32[]{:S(2)}) collective-permute-start(f32[2,136,128]{2,1,0:T(8,128)S(1)} %get-tuple-element.61), channel_id=1, source_target_pairs={{0,2},{1,3},{2,0},{3,1},{4,6},{5,7},{6,4},{7,5},{8,10},{9,11},{10,... | collective-permute-start | bytes 417800 | tf_op jit(solution)/shard_map/ppermute | solution.py:86
  117.7 7.5 %collective-permute-start.18 = (f32[2,136,128]{2,1,0:T(8,128)S(1)}, f32[2,136,128]{2,1,0:T(8,128)S(1)}, u32[]{:S(2)}, u32[]{:S(2)}) collective-permute-start(f32[2,136,128]{2,1,0:T(8,128)S(1)} %get-tuple-element.62), channel_id=1, source_target_pairs={{0,3},{1,0},{2,1},{3,2},{4,7},{5,4},{6,5},{7,6},{8,11},{9,8},{10,9... | collective-permute-start | bytes 417800 | tf_op jit(solution)/shard_map/ppermute | solution.py:86
  130.2 4.2 %collective-permute-start.20 = (f32[40,256]{1,0:T(8,128)S(1)}, f32[40,256]{1,0:T(8,128)S(1)}, u32[]{:S(2)}, u32[]{:S(2)}) collective-permute-start(f32[40,256]{1,0:T(8,128)S(1)} %get-tuple-element.67), channel_id=1, source_target_pairs={{0,8},{1,9},{2,10},{3,11},{4,12},{5,13},{6,14},{7,15},{8,16},{9,17... | collective-permute-start | bytes 122888 | tf_op jit(solution)/shard_map/ppermute | solution.py:86
  130.3 4.6 %collective-permute-start.21 = (f32[40,256]{1,0:T(8,128)S(1)}, f32[40,256]{1,0:T(8,128)S(1)}, u32[]{:S(2)}, u32[]{:S(2)}) collective-permute-start(f32[40,256]{1,0:T(8,128)S(1)} %get-tuple-element.68), channel_id=1, source_target_pairs={{0,16},{1,17},{2,18},{3,19},{4,20},{5,21},{6,22},{7,23},{8,24},{9,... | collective-permute-start | bytes 122888 | tf_op jit(solution)/shard_map/ppermute | solution.py:86
  138.9 10.4 %collective-permute-start.24 = (f32[40,256]{1,0:T(8,128)S(1)}, f32[40,256]{1,0:T(8,128)S(1)}, u32[]{:S(2)}, u32[]{:S(2)}) collective-permute-start(f32[40,256]{1,0:T(8,128)S(1)} %add.32), channel_id=1, source_target_pairs={{0,32},{1,33},{2,34},{3,35},{4,36},{5,37},{6,38},{7,39},{8,40},{9,... | collective-permute-start | bytes 122888 | tf_op jit(solution)/shard_map/ppermute | solution.py:86
  141.8 7.5 %collective-permute-start.25 = (f32[40,256]{1,0:T(8,128)S(1)}, f32[40,256]{1,0:T(8,128)S(1)}, u32[]{:S(2)}, u32[]{:S(2)}) collective-permute-start(f32[40,256]{1,0:T(8,128)S(1)} %add.32), channel_id=1, source_target_pairs={{0,64},{1,65},{2,66},{3,67},{4,68},{5,69},{6,70},{7,71},{8,72},{9,... | collective-permute-start | bytes 122888 | tf_op jit(solution)/shard_map/ppermute | solution.py:86
  146.9 4.1 %collective-permute-start.26 = (f32[40,256]{1,0:T(8,128)S(1)}, f32[40,256]{1,0:T(8,128)S(1)}, u32[]{:S(2)}, u32[]{:S(2)}) collective-permute-start(f32[40,256]{1,0:T(8,128)S(1)} %add.32), channel_id=1, source_target_pairs={{0,96},{1,97},{2,98},{3,99},{4,100},{5,101},{6,102},{7,103},{8,104... | collective-permute-start | bytes 122888 | tf_op jit(solution)/shard_map/ppermute | solution.py:86
  151.1 4.7 %collective-permute-start.27 = (f32[32,256]{1,0:T(8,128)S(1)}, f32[32,256]{1,0:T(8,128)S(1)}, u32[]{:S(2)}, u32[]{:S(2)}) collective-permute-start(f32[32,256]{1,0:T(8,128)S(1)} %get-tuple-element.75), channel_id=1, source_target_pairs={{0,1},{3,2},{4,5},{7,6},{8,9},{11,10},{12,13},{15,14},{16,17},{19,... | collective-permute-start | bytes 98312 | tf_op jit(solution)/shard_map/ppermute | solution.py:86
  164.3 10.6 %collective-permute-start.28 = (f32[4,2,32,256]{3,2,1,0:T(8,128)S(1)}, f32[4,2,32,256]{3,2,1,0:T(8,128)S(1)}, u32[]{:S(2)}, u32[]{:S(2)}) collective-permute-start(f32[4,2,32,256]{3,2,1,0:T(8,128)S(1)} %all_to_all.20.refs_0_), channel_id=1, source_target_pairs={{1,5},{2,6},{5,1},{6,2},{9,13},{10,14},{13,9},{14,10},{17,21},{18,... | collective-permute-start | bytes 786440 | tf_op jit(solution)/shard_map/ppermute | solution.py:86
  (26 other events, 301.2 us)
